TPU v7x, 32 devices: a whole 2x2x4 slice. The times are simulated.
32 devices in a mesh: dp: 2 (over x), row: 4 (over y, core), col: 4 (over z).
Axes of the slice: x: 2, y: 2, z: 4, core: 2. Of those that a mesh axis runs over, the one named last changes fastest.
Arguments:
- tokens: bfloat16 [8192, 1024], P(('dp', 'col'), 'row'), may hold values from -8 to 8
- w_qkv: bfloat16 [3, 1024, 1024], P(None, 'row', 'col'), may hold values from -0.1875 to 0.1875
- bias_qv: bfloat16 [2, 1024], P(None, 'col'), may hold values from -3 to 3
- w_out: bfloat16 [1024, 1024], P('col', 'row'), may hold values from -2 to 2
- bias_out: bfloat16 [1024], P('row'), may hold values from -3 to 3
- gain_one: bfloat16 [1024], P('row'), may hold values from 0.25 to 1.75
- shift_one: bfloat16 [1024], P('row'), may hold values from -3 to 3
- w_in: bfloat16 [1024, 4096], P('row', 'col'), may hold values from -0.1875 to 0.1875
- bias_in: bfloat16 [4096], P('col'), may hold values from -3 to 3
- w_back: bfloat16 [4096, 1024], P('col', 'row'), may hold values from -0.09375 to 0.09375
- bias_back: bfloat16 [1024], P('row'), may hold values from -3 to 3
- gain_two: bfloat16 [1024], P('row'), may hold values from 0.25 to 1.75
- shift_two: bfloat16 [1024], P('row'), may hold values from -3 to 3
- cotangent: bfloat16 [8192, 1024], P(('dp', 'col'), 'row'), may hold values from -8 to 8
Outputs:
- output: bfloat16 [8192, 1024], P(('dp', 'col'), 'row')
- grad_tokens: float32 [8192, 1024], P(('dp', 'col'), 'row')
- grad_w_qkv: float32 [3, 1024, 1024], P(None, 'row', 'col')
- grad_bias_qv: float32 [2, 1024], P(None, 'col')
- grad_w_out: float32 [1024, 1024], P('col', 'row')
- grad_bias_out: float32 [1024], P('row')
- grad_gain_one: float32 [1024], P('row')
- grad_shift_one: float32 [1024], P('row')
- grad_w_in: float32 [1024, 4096], P('row', 'col')
- grad_bias_in: float32 [4096], P('col')
- grad_w_back: float32 [4096, 1024], P('col', 'row')
- grad_bias_back: float32 [1024], P('row')
- grad_gain_two: float32 [1024], P('row')
- grad_shift_two: float32 [1024], P('row')
All inputs are finite; a program needn't handle non-finite values.
Results may differ from a plain program's by a relative error of at most 0.012.
The roundings to bfloat16 on the way count: a program that leaves them out, or rounds other values in their place, can miss the bound.
Values may be sent and summed in bfloat16 or wider, within the bound.
No kernel may reach another device: no remote copies, remote signals or barrier semaphores. Data moves between devices by JAX's collectives and lax.ppermute only.
A program may use at most 128 MiB of HBM per device.

v0:
```python
import jax
import jax.numpy as jnp
from jax import lax
from jax.sharding import PartitionSpec as P

HEAD_DIM = 64
SEQ_LEN = 512
norm_eps = 1e-12

f32 = jnp.float32
bf16 = jnp.bfloat16

REL = (0, 2, 1, 3)


def swap(values, axis, bit):
    size = lax.axis_size(axis)
    return lax.ppermute(values, axis, [(i, i ^ bit) for i in range(size)])


def dot(left, right, left_dim, right_dim):
    return lax.dot_general(
        left, right, (((left_dim,), (right_dim,)), ((), ())), preferred_element_type=f32
    )


def after(values, earlier):
    return lax.optimization_barrier((values, earlier))[0]


def trade(values, axis):
    return lax.all_to_all(values, axis, 0, 0, tiled=True)


def to_rel(values, dim):
    r = lax.axis_index("row")
    size = values.shape[dim] // 4
    parts = [lax.dynamic_slice_in_dim(values, (r ^ j) * size, size, dim) for j in REL]
    return jnp.concatenate(parts, dim)


def from_rel(values, dim):
    r = lax.axis_index("row")
    size = values.shape[dim] // 4
    parts = []
    for a in range(4):
        j = r ^ a
        place = ((j & 1) << 1) | (j >> 1)
        parts.append(lax.dynamic_slice_in_dim(values, place * size, size, dim))
    return jnp.concatenate(parts, dim)


def row_reduce(own, across, beside, diagonal, dim):
    size = own.shape[dim]
    got = swap(jnp.concatenate([beside, diagonal], dim).astype(bf16), "row", 1)
    far = across + lax.slice_in_dim(got, size, 2 * size, axis=dim).astype(f32)
    far = swap(far.astype(bf16), "row", 2)
    return own + lax.slice_in_dim(got, 0, size, axis=dim).astype(f32) + far.astype(f32)


def line_step(up, down, step):
    size = lax.axis_size("col")
    return (
        lax.ppermute(up, "col", [(i, i - 1) for i in range(1, size - step + 1)]),
        lax.ppermute(down, "col", [(i, i + 1) for i in range(step - 1, size - 1)]),
    )


def line_blocks(steps):
    size, here = lax.axis_size("col"), lax.axis_index("col")
    return [
        jnp.where(here + k < size, steps[k][0], steps[size - k][1]) for k in range(1, size)
    ]


def in_col_order(blocks):
    size, here = lax.axis_size("col"), lax.axis_index("col")
    out = jnp.zeros((size,) + blocks[0].shape, blocks[0].dtype)
    for step, b in enumerate(blocks):
        place = (here + step) % size
        out = lax.dynamic_update_slice_in_dim(out, b[None], place, 0)
    return out


def spread(block, axis):
    return trade(jnp.broadcast_to(block[None], (lax.axis_size(axis),) + block.shape), axis)


def normalize(resid):
    row_mean = jnp.mean(resid, 1, keepdims=True)
    centered = resid - row_mean
    variance = jnp.mean(centered * centered, 1, keepdims=True)
    inv_std = lax.rsqrt(variance + norm_eps)
    return centered * inv_std, inv_std


def norm_backward(incoming, normed, inv_std, gain):
    scaled = incoming * gain
    return inv_std * (
        scaled
        - jnp.mean(scaled, 1, keepdims=True)
        - normed * jnp.mean(scaled * normed, 1, keepdims=True)
    )


def dp_sum(values, first_bit):
    size = lax.axis_size("dp")
    bit = first_bit
    while bit < size:
        low = values.astype(bf16)
        values = low.astype(f32) + swap(low, "dp", bit).astype(f32)
        bit *= 2
    return values


def per_device(
    tokens,
    w_qkv,
    bias_qv,
    w_out,
    bias_out,
    gain_one,
    shift_one,
    w_in,
    bias_in,
    w_back,
    bias_back,
    gain_two,
    shift_two,
    cotangent,
):
    rows, cols = lax.axis_size("row"), lax.axis_size("col")
    r, n = lax.axis_index("row"), lax.axis_index("dp") & 1
    dp_size = lax.axis_size("dp")
    group, width_local = tokens.shape
    block = group // rows
    width = width_local * rows
    heads_tile = w_qkv.shape[2]
    head_piece = heads_tile // rows
    heads_width = cols * head_piece
    hid_tile = w_in.shape[1]
    hid_piece = hid_tile // rows
    half = hid_piece // 2
    hid_half = cols * half
    seq_count = group // SEQ_LEN
    head_count = heads_width // HEAD_DIM
    score_scale = HEAD_DIM ** (-0.5)
    seq_shape = (seq_count, SEQ_LEN, head_count, HEAD_DIM)

    heads_rows = 3 * head_piece
    wq = jnp.transpose(w_qkv, (2, 0, 1)).reshape(rows, head_piece, 3, width_local)
    wq = jnp.transpose(wq, (0, 2, 1, 3)).reshape(rows, heads_rows, width_local)
    wo = w_out.reshape(rows, head_piece, width_local)
    first = trade(jnp.concatenate([wq, wo], 1), "row")
    first = jnp.transpose(first, (1, 0, 2)).reshape(-1, width)
    first = jnp.concatenate([to_rel(first[:heads_rows], 1), first[heads_rows:]], 0)
    hid_bias = lax.dynamic_slice(bias_in, (r * hid_piece,), (hid_piece,))
    head_bias = lax.dynamic_slice(bias_qv, (0, r * head_piece), (2, head_piece)).reshape(-1)
    bias_row = jnp.concatenate([hid_bias, head_bias])
    bias_rows = jnp.pad(bias_row[None], ((0, 31), (0, width - bias_row.shape[0])))

    wi = jnp.transpose(w_in).reshape(rows, hid_piece, width_local)
    wi = lax.dynamic_slice_in_dim(wi, n * half, half, 1)
    wb = w_back.reshape(rows, hid_piece, width_local)
    wb = lax.dynamic_slice_in_dim(wb, n * half, half, 1)
    vectors = jnp.stack([bias_out, gain_one, shift_one, bias_back, gain_two, shift_two])
    vectors = jnp.pad(vectors, ((0, 10), (0, 0)))
    vectors = jnp.broadcast_to(vectors[None], (rows,) + vectors.shape)
    mixed = trade(after(jnp.concatenate([wi, wb, vectors], 1), first), "row")
    mixed = jnp.transpose(mixed, (1, 0, 2)).reshape(-1, width)
    wi, wb = mixed[:half], mixed[half : 2 * half]
    vectors = mixed[2 * half :].astype(f32)
    bias_out_f, gain_one_f, shift_one_f, bias_back_f, gain_two_f, shift_two_f = [
        vectors[i] for i in range(6)
    ]

    def both_halves(mine):
        other = swap(mine, "dp", 1)
        return jnp.concatenate([jnp.where(n == 0, mine, other), jnp.where(n == 0, other, mine)], 0)

    begin = jnp.concatenate([first, bias_rows], 0)
    line_half = begin.shape[0] // 2
    mine = lax.dynamic_slice_in_dim(begin, n * line_half, line_half, 0)
    steps = [(mine, mine)]
    steps.append(line_step(mine, mine, 1))
    steps[1], wi = lax.optimization_barrier((steps[1], wi))
    steps.append(line_step(*steps[1], 2))
    steps.append(line_step(*steps[2], 3))
    wi = spread(wi, "col").reshape(hid_half, width)
    steps[3], wi = lax.optimization_barrier((steps[3], wi))
    ours = line_blocks(steps)
    middle = swap(ours[1], "dp", 1)
    ends = swap(jnp.stack([ours[0], ours[2]]), "dp", 1)
    line = [begin]
    for our, their in zip(ours, [ends[0], middle, ends[1]]):
        both = [jnp.where(n == 0, our, their), jnp.where(n == 0, their, our)]
        line.append(jnp.concatenate(both, 0))
    wq_all = in_col_order([b[:heads_rows].reshape(3, head_piece, width) for b in line])
    wq_all = jnp.transpose(wq_all, (1, 0, 2, 3)).reshape(3 * heads_width, width)
    bias_at = heads_rows + head_piece
    wo_all = in_col_order([b[heads_rows:bias_at] for b in line]).reshape(heads_width, width)
    col_bias = in_col_order([b[bias_at, : bias_row.shape[0]] for b in line]).astype(f32)
    bias_q = col_bias[:, hid_piece : hid_piece + head_piece].reshape(-1)
    bias_v = col_bias[:, hid_piece + head_piece :].reshape(-1)
    bias_in_f = jnp.transpose(col_bias[:, :hid_piece].reshape(cols, 2, half), (1, 0, 2)).reshape(-1)

    across = swap(tokens, "row", 2)
    beside = swap(tokens, "row", 1)
    diagonal = swap(across, "row", 1)
    tokens_all = jnp.concatenate([tokens, across, beside, diagonal], 1)

    wb = spread(after(wb, steps[3]), "col").reshape(hid_half, width)
    wi_all = both_halves(wi)
    cot = after(cotangent, wb).reshape(rows, block, width_local)
    cot = jnp.transpose(trade(cot, "row"), (1, 0, 2)).reshape(block, width).astype(f32)

    joined = dot(tokens_all, wq_all, 1, 1)
    queries = (joined[:, :heads_width] + bias_q).astype(bf16).reshape(seq_shape)
    key_rows = joined[:, heads_width : 2 * heads_width].astype(bf16).reshape(seq_shape)
    value_rows = (joined[:, 2 * heads_width :] + bias_v).astype(bf16).reshape(seq_shape)
    scores = (
        jnp.einsum("sqhd,skhd->shqk", queries, key_rows, preferred_element_type=f32) * score_scale
    )
    row_peak = jnp.max(scores, -1, keepdims=True)
    expo_scores = jnp.exp(scores - row_peak)
    row_total = jnp.sum(expo_scores, -1, keepdims=True)
    attn_weights = expo_scores / row_total
    log_total = row_peak + jnp.log(row_total)
    context = jnp.einsum(
        "shqk,skhd->sqhd", attn_weights.astype(bf16), value_rows, preferred_element_type=f32
    )
    context, wb, wi_all = lax.optimization_barrier((context, wb, wi_all))
    wb_all = both_halves(wb)
    context = to_rel(context.reshape(group, heads_width).astype(bf16), 0)

    send = dot(context[2 * block :], wo_all, 1, 0).astype(bf16)
    keep = dot(context[: 2 * block], wo_all, 1, 0)
    attended = row_reduce(keep[:block], keep[block:], send[:block], send[block:], 0) + bias_out_f
    tokens_own = lax.dynamic_slice_in_dim(tokens_all, r * block, block, 0)
    tokens_own = from_rel(tokens_own, 1).astype(f32)
    normed_one, inv_one = normalize(tokens_own + attended)
    hidden_one = normed_one * gain_one_f + shift_one_f

    def chips(values):
        over = swap(values, "row", 2)
        near = jnp.concatenate([values, swap(values, "row", 1)], 0)
        return near, jnp.concatenate([over, swap(over, "row", 1)], 0)

    def reduce_chips(near, far):
        return row_reduce(near[:block], far[:block], near[block:], far[block:], 0)

    hidden = chips(hidden_one.astype(bf16))
    pre_act, cdf, activated, mlp = [], [], [], []
    for h in hidden:
        pre = dot(h, wi_all, 1, 1) + bias_in_f
        pre_act.append(pre)
        cdf.append(0.5 * (1.0 + lax.erf(pre * 0.7071067811865476)))
        activated.append((pre * cdf[-1]).astype(bf16))
        mlp.append(dot(activated[-1], wb_all, 1, 0))
    mlp_out = reduce_chips(*mlp) + bias_back_f
    normed_two, inv_two = normalize(hidden_one + mlp_out)
    output = (normed_two * gain_two_f + shift_two_f).astype(bf16)

    d_two = norm_backward(cot, normed_two, inv_two, gain_two_f)
    d_mlp_low = d_two.astype(bf16)
    d_mlp = chips(d_mlp_low)
    d_pre, d_hid = [], []
    for k in range(2):
        d_activated = dot(d_mlp[k], wb_all, 1, 1)
        pdf = jnp.exp(-0.5 * pre_act[k] * pre_act[k]) * 0.3989422804014327
        d_pre.append((d_activated * (cdf[k] + pre_act[k] * pdf)).astype(bf16))
        d_hid.append(dot(d_pre[k], wi_all, 1, 0))
    d_hidden = d_two + reduce_chips(*d_hid)
    def hidden_grad(left, right):
        return sum(dot(a, b, 0, 0) for a, b in zip(left, right)).astype(bf16)

    grad_wb = hidden_grad(activated, d_mlp)
    grad_wi = hidden_grad(d_pre, hidden)
    hid_grads_gate = None
    if dp_size == 2:
        grad_wb = trade(grad_wb.reshape(2 * cols, half, width), ("dp", "col"))
        hid_grads_gate = grad_wb
        grad_wb = jnp.sum(grad_wb.astype(f32), 0).astype(bf16)
        grad_wi = lax.psum_scatter(grad_wi, ("dp", "col"), scatter_dimension=0, tiled=True)
        hid_grads = both_halves(jnp.stack([grad_wb, grad_wi])[None])
    else:
        hid_grads = jnp.stack([grad_wb, grad_wi]).reshape(2, 2, cols, half, width)
        hid_grads = jnp.transpose(hid_grads, (2, 1, 0, 3, 4)).reshape(-1, width)
        hid_grads = lax.psum_scatter(hid_grads, "col", scatter_dimension=0, tiled=True)
        hid_grads = lax.psum(hid_grads.astype(f32), "dp").astype(bf16).reshape(2, 2, half, width)
    hid_grads = jnp.transpose(hid_grads, (1, 0, 2, 3)).reshape(2 * hid_piece, width)
    hid_grads = jnp.concatenate([hid_grads, output], 0).reshape(-1, rows, width_local)
    hid_grads = jnp.transpose(hid_grads, (1, 0, 2))
    pieces = [lax.dynamic_slice_in_dim(hid_grads, r ^ j, 1, 0) for j in range(rows)]
    pieces = jnp.concatenate(
        [pieces[0]] + [swap(pieces[j], "row", j) for j in range(1, rows)], 0
    )
    hid_grads = jnp.concatenate(
        [lax.dynamic_slice_in_dim(pieces, r ^ a, 1, 0) for a in range(rows)], 0
    )
    output = hid_grads[:, 2 * hid_piece :].reshape(group, width_local)
    grad_w_back = hid_grads[:, :hid_piece].reshape(hid_tile, width_local).astype(f32)
    grad_w_in = hid_grads[:, hid_piece : 2 * hid_piece].reshape(hid_tile, width_local)
    grad_w_in = jnp.transpose(grad_w_in).astype(f32)

    d_one = norm_backward(d_hidden, normed_one, inv_one, gain_one_f)
    d_att = d_one.astype(bf16)
    over = swap(d_att, "row", 2)
    d_att_all = jnp.concatenate([d_att, over, swap(d_att, "row", 1), swap(over, "row", 1)], 0)
    d_att_all, _ = lax.optimization_barrier((d_att_all, hid_grads_gate))

    def by_owner(values):
        each = values.shape[1]
        got = jnp.transpose(values, (2, 0, 1, 3)).reshape(-1, each, width_local)
        raw = trade(got, ("row", "col"))
        got = jnp.sum(raw.reshape(rows, cols, each, width_local).astype(f32), 1)
        return dp_sum(got, 1), raw

    grad_wo = dot(context, d_att_all, 0, 0).astype(bf16).reshape(cols, head_piece, rows, width_local)
    grad_w_out = by_owner(grad_wo)[0].reshape(heads_tile, width_local)

    d_context = from_rel(dot(d_att_all, wo_all, 1, 1).astype(bf16), 0).reshape(seq_shape)
    scores_again = (
        jnp.einsum("sqhd,skhd->shqk", queries, key_rows, preferred_element_type=f32) * score_scale
    )
    weights_again = jnp.exp(scores_again - log_total)
    d_value = jnp.einsum(
        "shqk,sqhd->skhd", weights_again.astype(bf16), d_context, preferred_element_type=f32
    )
    d_weights = jnp.einsum("sqhd,skhd->shqk", d_context, value_rows, preferred_element_type=f32)
    row_inner = jnp.sum(d_weights * weights_again, -1, keepdims=True)
    d_scores = (weights_again * (d_weights - row_inner)).astype(bf16)
    d_query = (
        jnp.einsum("shqk,skhd->sqhd", d_scores, key_rows, preferred_element_type=f32) * score_scale
    )
    d_key = (
        jnp.einsum("shqk,sqhd->skhd", d_scores, queries, preferred_element_type=f32) * score_scale
    )
    d_joined = jnp.concatenate(
        [
            d_query.reshape(group, heads_width),
            d_key.reshape(group, heads_width),
            d_value.reshape(group, heads_width),
        ],
        1,
    ).astype(bf16)
    grad_wq = dot(d_joined, tokens_all, 0, 0).astype(bf16)
    grad_wq = from_rel(grad_wq, 1).reshape(3, cols, head_piece, width)
    grad_wq = jnp.transpose(grad_wq, (1, 0, 2, 3)).reshape(cols, heads_rows, rows, width_local)
    head_sums = jnp.sum(d_joined.reshape(group, 3, cols, head_piece), 0, dtype=f32)
    head_sums = jnp.concatenate([head_sums[0], head_sums[2]], 1).astype(bf16)
    head_sums = jnp.pad(head_sums, ((0, 0), (0, width_local - 2 * head_piece)))
    head_sums = jnp.broadcast_to(head_sums[:, None, None], (cols, 16, rows, width_local))
    grad_wq, arrived = by_owner(jnp.concatenate([grad_wq, head_sums], 1))
    head_sums = grad_wq[:, heads_rows, : 2 * head_piece].reshape(rows, 2, head_piece)
    grad_bias_qv = jnp.transpose(head_sums, (1, 0, 2)).reshape(2, heads_tile)
    grad_wq = grad_wq[:, :heads_rows].reshape(rows, 3, head_piece, width_local)
    grad_w_qkv = jnp.transpose(grad_wq, (1, 3, 0, 2)).reshape(3, width_local, heads_tile)

    split = 2 * width_local
    d_one_rel = to_rel(d_one, 1)
    own_rows = (jnp.arange(rows) == r)[:, None, None]

    def with_own(values, own):
        values = values.reshape(rows, block, split)
        return (values + jnp.where(own_rows, own[None], 0.0)).reshape(group, split)

    keep = with_own(dot(d_joined, wq_all[:, :split], 1, 0), d_one_rel[:, :split])
    send = with_own(dot(d_joined, wq_all[:, split:], 1, 0), d_one_rel[:, split:]).astype(bf16)
    grad_tokens = row_reduce(
        keep[:, :width_local],
        keep[:, width_local:],
        send[:, :width_local],
        send[:, width_local:],
        1,
    )

    vector_grads = jnp.stack(
        [
            jnp.sum(d_att, 0, dtype=f32),
            jnp.sum(d_hidden * normed_one, 0),
            jnp.sum(d_hidden, 0),
            jnp.sum(d_mlp_low, 0, dtype=f32),
            jnp.sum(cot * normed_two, 0),
            jnp.sum(cot, 0),
        ]
    )
    vector_grads = jnp.transpose(vector_grads.reshape(6, rows, width_local), (1, 0, 2))
    hid_sums = sum(jnp.sum(d, 0, dtype=f32) for d in d_pre).reshape(2, cols, half)
    hid_sums = jnp.transpose(hid_sums, (1, 0, 2)).reshape(1, cols, 1, hid_piece)
    small = jnp.concatenate(
        [
            jnp.broadcast_to(vector_grads[:, None], (rows, cols, 6, width_local)),
            jnp.broadcast_to(hid_sums, (rows, cols, 2, width_local)),
        ],
        2,
    )
    small = jnp.broadcast_to(small[None], (dp_size,) + small.shape)
    small = after(small, arrived)
    small = trade(small.reshape(-1, 8, width_local), ("dp", "row", "col"))
    small = small.reshape(dp_size, rows, cols, 8, width_local)
    vector_grads = jnp.sum(small[:, :, :, :6], (0, 1, 2))
    grad_bias_in = jnp.sum(small[:, :, :, 6], (0, 2)).reshape(hid_tile)

    return (
        output,
        grad_tokens,
        grad_w_qkv,
        grad_bias_qv,
        grad_w_out,
        vector_grads[0],
        vector_grads[1],
        vector_grads[2],
        grad_w_in,
        grad_bias_in,
        grad_w_back,
        vector_grads[3],
        vector_grads[4],
        vector_grads[5],
    )


def solution(mesh):
    in_specs = (
        P(("dp", "col"), "row"),
        P(None, "row", "col"),
        P(None, "col"),
        P("col", "row"),
        P("row"),
        P("row"),
        P("row"),
        P("row", "col"),
        P("col"),
        P("col", "row"),
        P("row"),
        P("row"),
        P("row"),
        P(("dp", "col"), "row"),
    )
    out_specs = (
        P(("dp", "col"), "row"),
        P(("dp", "col"), "row"),
        P(None, "row", "col"),
        P(None, "col"),
        P("col", "row"),
        P("row"),
        P("row"),
        P("row"),
        P("row", "col"),
        P("col"),
        P("col", "row"),
        P("row"),
        P("row"),
        P("row"),
    )
    return jax.shard_map(
        per_device, mesh=mesh, in_specs=in_specs, out_specs=out_specs, check_vma=False
    )
```

profile of v0, /device:TPU:0, one launch (start us, length us, event | category | flops | bytes accessed | tf_op | source)
XLA Modules:
  0.0 437.3 jit_solution(14133880208688230231)
XLA Ops:
  10.3 4.2 all-to-all-start
  16.8 6.6 %all-to-all-done = bf16[4,256,256]{2,1,0:T(8,128)(2,1)S(1)} async-done(((bf16[4,256,256]{2,1,0:T(8,128)(2,1)}), bf16[4,256,256]{2,1,0:T(8,128)(2,1)S(1)}, u32[]{:S(2)}, u32[]{:S(2)}) %all-to-all-start) | async-done | bytes 524320 | tf_op jit(solution)/shard_map/all_to_all | solution.py:32
  29.1 5.5 %collective-permute-start.4 = (bf16[144,1024]{1,0:T(8,128)(2,1)S(1)}, bf16[144,1024]{1,0:T(8,128)(2,1)}, u32[]{:S(2)}, u32[]{:S(2)}) collective-permute-start(bf16[144,1024]{1,0:T(8,128)(2,1)S(1)} %fusion.65), channel_id=1, source_target_pairs={{0,1},{1,2},{2,3},{4,5},{5,6},{6,7},{8,9},{9,10},{10,11},{12,13},{... | collective-permute-start | bytes 884744 | tf_op jit(solution)/shard_map/ppermute | solution.py:65
  42.0 6.7 %all-to-all-start.2 = ((bf16[4,128,1024]{2,1,0:T(8,128)(2,1)}), bf16[4,128,1024]{2,1,0:T(8,128)(2,1)S(1)}, u32[]{:S(2)}, u32[]{:S(2)}) async-start(bf16[4,128,1024]{2,1,0:T(8,128)(2,1)} %broadcast_in_dim.124), calls=%async_computation.2 | async-start | bytes 2097152 | tf_op jit(solution)/shard_map/all_to_all | solution.py:32
  56.5 5.5 %collective-permute-done = bf16[1024,256]{1,0:T(8,128)(2,1)} collective-permute-done((bf16[1024,256]{1,0:T(8,128)(2,1)}, bf16[1024,256]{1,0:T(8,128)(2,1)}, u32[]{:S(2)}, u32[]{:S(2)}) %collective-permute-start) | collective-permute-done | bytes 524320 | tf_op jit(solution)/shard_map/ppermute | solution.py:18
  62.0 7.4 %collective-permute-done.5 = bf16[144,1024]{1,0:T(8,128)(2,1)} collective-permute-done((bf16[144,1024]{1,0:T(8,128)(2,1)}, bf16[144,1024]{1,0:T(8,128)(2,1)}, u32[]{:S(2)}, u32[]{:S(2)}) %collective-permute-start.5) | collective-permute-done | bytes 294944 | tf_op jit(solution)/shard_map/ppermute | solution.py:64
  77.1 11.5 %collective-permute-done.6 = bf16[144,1024]{1,0:T(8,128)(2,1)S(1)} collective-permute-done((bf16[144,1024]{1,0:T(8,128)(2,1)}, bf16[144,1024]{1,0:T(8,128)(2,1)S(1)}, u32[]{:S(2)}, u32[]{:S(2)}) %collective-permute-start.6) | collective-permute-done | bytes 294944 | tf_op jit(solution)/shard_map/ppermute | solution.py:64
  147.4 8.2 %collective-permute-done.13 = bf16[256,1024]{1,0:T(8,128)(2,1)S(1)} collective-permute-done((bf16[256,1024]{1,0:T(8,128)(2,1)S(1)}, bf16[256,1024]{1,0:T(8,128)(2,1)S(1)}, u32[]{:S(2)}, u32[]{:S(2)}) %collective-permute-start.13) | collective-permute-done | bytes 524320 | tf_op jit(solution)/shard_map/ppermute | solution.py:18
  158.4 11.8 %collective-permute-done.16 = bf16[256,1024]{1,0:T(8,128)(2,1)S(1)} collective-permute-done((bf16[256,1024]{1,0:T(8,128)(2,1)S(1)}, bf16[256,1024]{1,0:T(8,128)(2,1)S(1)}, u32[]{:S(2)}, u32[]{:S(2)}) %collective-permute-start.16) | collective-permute-done | bytes 524320 | tf_op jit(solution)/shard_map/ppermute | solution.py:18
  191.4 4.4 %all-to-all-done.4 = bf16[4,256,256]{2,1,0:T(8,128)(2,1)S(1)} async-done(((bf16[4,256,256]{2,1,0:T(8,128)(2,1)}), bf16[4,256,256]{2,1,0:T(8,128)(2,1)S(1)}, u32[]{:S(2)}, u32[]{:S(2)}) %all-to-all-start.4) | async-done | bytes 524320 | tf_op jit(solution)/shard_map/all_to_all | solution.py:32
  197.2 9.3 %collective-permute-done.19 = bf16[256,1024]{1,0:T(8,128)(2,1)S(1)} collective-permute-done((bf16[256,1024]{1,0:T(8,128)(2,1)}, bf16[256,1024]{1,0:T(8,128)(2,1)S(1)}, u32[]{:S(2)}, u32[]{:S(2)}) %collective-permute-start.19) | collective-permute-done | bytes 524320 | tf_op jit(solution)/shard_map/ppermute | solution.py:18
  212.0 13.1 %collective-permute-done.21 = bf16[256,1024]{1,0:T(8,128)(2,1)S(1)} collective-permute-done((bf16[256,1024]{1,0:T(8,128)(2,1)S(1)}, bf16[256,1024]{1,0:T(8,128)(2,1)S(1)}, u32[]{:S(2)}, u32[]{:S(2)}) %collective-permute-start.21) | collective-permute-done | bytes 524320 | tf_op jit(solution)/shard_map/ppermute | solution.py:18
  244.4 5.9 %all-to-all-start.5 = ((bf16[8,128,1024]{2,1,0:T(8,128)(2,1)}), bf16[8,128,1024]{2,1,0:T(8,128)(2,1)S(1)}, u32[]{:S(2)}, u32[]{:S(2)}) async-start(bf16[8,128,1024]{2,1,0:T(8,128)(2,1)} %bitcast.259), calls=%async_computation.5 | async-start | bytes 4194304 | tf_op jit(solution)/shard_map/all_to_all | solution.py:32
  252.8 12.9 %collective-permute-done.28 = bf16[256,1024]{1,0:T(8,128)(2,1)S(1)} collective-permute-done((bf16[256,1024]{1,0:T(8,128)(2,1)S(1)}, bf16[256,1024]{1,0:T(8,128)(2,1)S(1)}, u32[]{:S(2)}, u32[]{:S(2)}) %collective-permute-start.28) | collective-permute-done | bytes 524320 | tf_op jit(solution)/shard_map/ppermute | solution.py:18
  271.9 11.6 %collective-permute-done.29 = bf16[256,1024]{1,0:T(8,128)(2,1)S(1)} collective-permute-done((bf16[256,1024]{1,0:T(8,128)(2,1)}, bf16[256,1024]{1,0:T(8,128)(2,1)S(1)}, u32[]{:S(2)}, u32[]{:S(2)}) %collective-permute-start.29) | collective-permute-done | bytes 524320 | tf_op jit(solution)/shard_map/ppermute | solution.py:18
  290.5 12.0 %all-to-all-done.5 = bf16[8,128,1024]{2,1,0:T(8,128)(2,1)S(1)} async-done(((bf16[8,128,1024]{2,1,0:T(8,128)(2,1)}), bf16[8,128,1024]{2,1,0:T(8,128)(2,1)S(1)}, u32[]{:S(2)}, u32[]{:S(2)}) %all-to-all-start.5) | async-done | bytes 2097184 | tf_op jit(solution)/shard_map/all_to_all | solution.py:32
  309.6 4.2 all-to-all-start.7
  315.0 5.0 %fusion.32 = bf16[2,512,4,64]{1,3,2,0:T(8,128)(2,1)S(1)} fusion(bf16[2,512,4,64]{1,3,2,0:T(8,128)(2,1)S(1)} %copy.251, f32[2,4,512,512]{2,3,1,0:T(8,128)} %copy-done.2, f32[2,4,512]{2,1,0:T(4,128)S(1)} %bitcast.310), kind=kOutput, calls=%fused_computation.65 | convolution fusion | flops 274989056 | bytes 9453568 | tf_op jit(solution)/shard_map/shqk,sqhd->skhd/dot_general | solution.py:327
  321.1 4.9 %multiply_reduce_fusion = (f32[2,4,512]{2,1,0:T(4,128)S(1)}, f32[2,4,512,512]{2,3,1,0:T(8,128)S(1)}) fusion(f32[2,4,512,512]{2,3,1,0:T(8,128)} %copy-done.2, f32[2,4,512]{2,1,0:T(4,128)S(1)} %bitcast.311, bf16[2,512,4,64]{1,3,2,0:T(8,128)(2,1)S(1)} %copy.251, bf16[2,512,4,64]{1,3,2,0:T(8,128)(2,1)S(1)} %copy-done.20), kind=kOutput, calls=%fused_computation.1 | convolution fusion | flops 276819968 | bytes 17858560 | tf_op jit(solution)/shard_map/sqhd,skhd->shqk/dot_general | solution.py:330
  349.5 6.0 %all-to-all-start.6 = ((bf16[16,208,256]{2,1,0:T(8,128)(2,1)}), bf16[16,208,256]{2,1,0:T(8,128)(2,1)}, u32[]{:S(2)}, u32[]{:S(2)}) async-start(bf16[16,208,256]{2,1,0:T(8,128)(2,1)} %bitcast.61), calls=%async_computation.7 | async-start | bytes 3407872 | tf_op jit(solution)/shard_map/all_to_all | solution.py:32
  389.1 4.6 %collective-permute-done.25 = bf16[1,768,256]{2,1,0:T(8,128)(2,1)S(1)} collective-permute-done((bf16[1,768,256]{2,1,0:T(8,128)(2,1)S(1)}, bf16[1,768,256]{2,1,0:T(8,128)(2,1)S(1)}, u32[]{:S(2)}, u32[]{:S(2)}) %collective-permute-start.25) | collective-permute-done | bytes 393248 | tf_op jit(solution)/shard_map/ppermute | solution.py:18
  393.7 8.8 %collective-permute-done.26 = bf16[1,768,256]{2,1,0:T(8,128)(2,1)S(1)} collective-permute-done((bf16[1,768,256]{2,1,0:T(8,128)(2,1)S(1)}, bf16[1,768,256]{2,1,0:T(8,128)(2,1)S(1)}, u32[]{:S(2)}, u32[]{:S(2)}) %collective-permute-start.26) | collective-permute-done | bytes 393248 | tf_op jit(solution)/shard_map/ppermute | solution.py:18
  410.4 8.1 %all-to-all-start.8 = ((f32[32,8,256]{2,1,0:T(8,128)}), f32[32,8,256]{2,1,0:T(8,128)S(1)}, u32[]{:S(2)}, u32[]{:S(2)}) async-start(f32[32,8,256]{2,1,0:T(8,128)} %bitcast.80), calls=%async_computation.9 | async-start | bytes 524288 | tf_op jit(solution)/shard_map/all_to_all | solution.py:32
  424.2 4.6 %all-to-all-done.8 = f32[32,8,256]{2,1,0:T(8,128)S(1)} async-done(((f32[32,8,256]{2,1,0:T(8,128)}), f32[32,8,256]{2,1,0:T(8,128)S(1)}, u32[]{:S(2)}, u32[]{:S(2)}) %all-to-all-start.8) | async-done | bytes 262176 | tf_op jit(solution)/shard_map/all_to_all | solution.py:32
  (479 shorter events, 238.0 us)
Async XLA Ops:
  42.0 47.4 %all-to-all-start.2 = ((bf16[4,128,1024]{2,1,0:T(8,128)(2,1)}), bf16[4,128,1024]{2,1,0:T(8,128)(2,1)S(1)}, u32[]{:S(2)}, u32[]{:S(2)}) async-start(bf16[4,128,1024]{2,1,0:T(8,128)(2,1)} %broadcast_in_dim.124), calls=%async_computation.2 | async-start | bytes 2097152 | tf_op jit(solution)/shard_map/all_to_all | solution.py:32
  50.4 43.4 %collective-permute-start.1 = (bf16[1024,256]{1,0:T(8,128)(2,1)}, bf16[1024,256]{1,0:T(8,128)(2,1)}, u32[]{:S(2)}, u32[]{:S(2)}) collective-permute-start(bf16[1024,256]{1,0:T(8,128)(2,1)} %param.14), channel_id=1, source_target_pairs={{0,4},{4,0},{8,12},{12,8},{1,5},{5,1},{9,13},{13,9},{2,6},{6,2},{1... | collective-permute-start | bytes 1572872 | tf_op jit(solution)/shard_map/ppermute | solution.py:18
  52.6 16.7 %collective-permute-start.5 = (bf16[144,1024]{1,0:T(8,128)(2,1)}, bf16[144,1024]{1,0:T(8,128)(2,1)}, u32[]{:S(2)}, u32[]{:S(2)}) collective-permute-start(bf16[144,1024]{1,0:T(8,128)(2,1)} %collective-permute-done.3), channel_id=1, source_target_pairs={{1,0},{2,1},{5,4},{6,5},{9,8},{10,9},{13,12},{14,13},{17,16},{18,1... | collective-permute-start | bytes 884744 | tf_op jit(solution)/shard_map/ppermute | solution.py:64
  53.9 16.7 %collective-permute-start.7 = (bf16[144,1024]{1,0:T(8,128)(2,1)}, bf16[144,1024]{1,0:T(8,128)(2,1)}, u32[]{:S(2)}, u32[]{:S(2)}) collective-permute-start(bf16[144,1024]{1,0:T(8,128)(2,1)} %collective-permute-done.4), channel_id=1, source_target_pairs={{1,2},{2,3},{5,6},{6,7},{9,10},{10,11},{13,14},{14,15},{17,18},{18... | collective-permute-start | bytes 884744 | tf_op jit(solution)/shard_map/ppermute | solution.py:65
  61.9 33.7 %collective-permute-start.2 = (bf16[1024,256]{1,0:T(8,128)(2,1)}, bf16[1024,256]{1,0:T(8,128)(2,1)}, u32[]{:S(2)}, u32[]{:S(2)}) collective-permute-start(bf16[1024,256]{1,0:T(8,128)(2,1)} %collective-permute-done), channel_id=1, source_target_pairs={{0,4},{4,0},{8,12},{12,8},{1,5},{5,1},{9,13},{13,9},{2,6},{6,2},{1... | collective-permute-start | bytes 1572872 | tf_op jit(solution)/shard_map/ppermute | solution.py:18
  69.3 19.3 %collective-permute-start.6 = (bf16[144,1024]{1,0:T(8,128)(2,1)}, bf16[144,1024]{1,0:T(8,128)(2,1)S(1)}, u32[]{:S(2)}, u32[]{:S(2)}) collective-permute-start(bf16[144,1024]{1,0:T(8,128)(2,1)} %collective-permute-done.5), channel_id=1, source_target_pairs={{1,0},{5,4},{9,8},{13,12},{17,16},{21,20},{25,24},{29,28}} | collective-permute-start | bytes 884744 | tf_op jit(solution)/shard_map/ppermute | solution.py:64
  70.6 18.8 %collective-permute-start.8 = (bf16[144,1024]{1,0:T(8,128)(2,1)}, bf16[144,1024]{1,0:T(8,128)(2,1)}, u32[]{:S(2)}, u32[]{:S(2)}) collective-permute-start(bf16[144,1024]{1,0:T(8,128)(2,1)} %collective-permute-done.7), channel_id=1, source_target_pairs={{2,3},{6,7},{10,11},{14,15},{18,19},{22,23},{26,27},{30,31}} | collective-permute-start | bytes 884744 | tf_op jit(solution)/shard_map/ppermute | solution.py:65
  75.6 22.0 %collective-permute-start.10 = (bf16[144,1024]{1,0:T(8,128)(2,1)}, bf16[144,1024]{1,0:T(8,128)(2,1)}, u32[]{:S(2)}, u32[]{:S(2)}) collective-permute-start(bf16[144,1024]{1,0:T(8,128)(2,1)} %broadcast_select_fusion.6), channel_id=1, source_target_pairs={{0,16},{16,0},{1,17},{17,1},{2,18},{18,2},{3,19},{19,3},{4,20},{20... | collective-permute-start | bytes 884744 | tf_op jit(solution)/shard_map/ppermute | solution.py:18
  92.3 16.6 %collective-permute-start.9 = (bf16[2,144,1024]{2,1,0:T(8,128)(2,1)}, bf16[2,144,1024]{2,1,0:T(8,128)(2,1)}, u32[]{:S(2)}, u32[]{:S(2)}) collective-permute-start(bf16[2,144,1024]{2,1,0:T(8,128)(2,1)} %pad_maximum_fusion.14), channel_id=1, source_target_pairs={{0,16},{16,0},{1,17},{17,1},{2,18},{18,2},{3,19},{19,3},{4,20},{20... | collective-permute-start | bytes 1769480 | tf_op jit(solution)/shard_map/ppermute | solution.py:18
  104.0 33.4 %all-to-all-start.3 = ((bf16[4,128,1024]{2,1,0:T(8,128)(2,1)}), bf16[4,128,1024]{2,1,0:T(8,128)(2,1)}, u32[]{:S(2)}, u32[]{:S(2)}) async-start(bf16[4,128,1024]{2,1,0:T(8,128)(2,1)} %broadcast_in_dim.126), calls=%async_computation.3 | async-start | bytes 2097152 | tf_op jit(solution)/shard_map/all_to_all | solution.py:32
  108.3 26.3 %collective-permute-start.11 = (bf16[512,1024]{1,0:T(8,128)(2,1)S(1)}, bf16[512,1024]{1,0:T(8,128)(2,1)}, u32[]{:S(2)}, u32[]{:S(2)}) collective-permute-start(bf16[512,1024]{1,0:T(8,128)(2,1)S(1)} %bitcast.271), channel_id=1, source_target_pairs={{0,16},{16,0},{1,17},{17,1},{2,18},{18,2},{3,19},{19,3},{4,20},{20... | collective-permute-start | bytes 3145736 | tf_op jit(solution)/shard_map/ppermute | solution.py:18
  145.9 25.2 %collective-permute-start.15 = (bf16[512,1024]{1,0:T(8,128)(2,1)}, bf16[512,1024]{1,0:T(8,128)(2,1)S(1)}, u32[]{:S(2)}, u32[]{:S(2)}) collective-permute-start(bf16[512,1024]{1,0:T(8,128)(2,1)} %bitcast.28), channel_id=1, source_target_pairs={{0,16},{16,0},{1,17},{17,1},{2,18},{18,2},{3,19},{19,3},{4,20},{20... | collective-permute-start | bytes 3145736 | tf_op jit(solution)/shard_map/ppermute | solution.py:18
  189.4 17.1 %collective-permute-start.19 = (bf16[256,1024]{1,0:T(8,128)(2,1)}, bf16[256,1024]{1,0:T(8,128)(2,1)S(1)}, u32[]{:S(2)}, u32[]{:S(2)}) collective-permute-start(bf16[256,1024]{1,0:T(8,128)(2,1)} %fusion.41), channel_id=1, source_target_pairs={{0,8},{4,12},{8,0},{12,4},{1,9},{5,13},{9,1},{13,5},{2,10},{6,14},... | collective-permute-start | bytes 1572872 | tf_op jit(solution)/shard_map/ppermute | solution.py:18
  244.4 58.1 %all-to-all-start.5 = ((bf16[8,128,1024]{2,1,0:T(8,128)(2,1)}), bf16[8,128,1024]{2,1,0:T(8,128)(2,1)S(1)}, u32[]{:S(2)}, u32[]{:S(2)}) async-start(bf16[8,128,1024]{2,1,0:T(8,128)(2,1)} %bitcast.259), calls=%async_computation.5 | async-start | bytes 4194304 | tf_op jit(solution)/shard_map/all_to_all | solution.py:32
  250.3 108.8 %reduce-scatter.2.cloned.1.call-start = ((), (), s32[]{:S(2)}) async-start(), calls=%async_computation.10 | async-start | bytes 2359296 | tf_op jit(solution)/shard_map/reduce_scatter | solution.py:284
  271.9 15.7 %collective-permute-start.30 = (bf16[256,1024]{1,0:T(8,128)(2,1)}, bf16[256,1024]{1,0:T(8,128)(2,1)}, u32[]{:S(2)}, u32[]{:S(2)}) collective-permute-start(bf16[256,1024]{1,0:T(8,128)(2,1)} %get-tuple-element.122), channel_id=1, source_target_pairs={{0,4},{4,0},{8,12},{12,8},{1,5},{5,1},{9,13},{13,9},{2,6},{6,2},{1... | collective-permute-start | bytes 1572872 | tf_op jit(solution)/shard_map/ppermute | solution.py:18
  309.6 39.9 %all-to-all-start.7 = ((bf16[16,64,256]{2,1,0:T(8,128)(2,1)}), bf16[16,64,256]{2,1,0:T(8,128)(2,1)}, u32[]{:S(2)}, u32[]{:S(2)}) async-start(bf16[16,64,256]{2,1,0:T(8,128)(2,1)} %bitcast.68), calls=%async_computation.8 | async-start | bytes 1048576 | tf_op jit(solution)/shard_map/all_to_all | solution.py:32
  349.5 55.7 %all-to-all-start.6 = ((bf16[16,208,256]{2,1,0:T(8,128)(2,1)}), bf16[16,208,256]{2,1,0:T(8,128)(2,1)}, u32[]{:S(2)}, u32[]{:S(2)}) async-start(bf16[16,208,256]{2,1,0:T(8,128)(2,1)} %bitcast.61), calls=%async_computation.7 | async-start | bytes 3407872 | tf_op jit(solution)/shard_map/all_to_all | solution.py:32
  360.9 14.4 %collective-permute-start.23 = (bf16[1,2,128,1024]{3,2,1,0:T(8,128)(2,1)}, bf16[1,2,128,1024]{3,2,1,0:T(8,128)(2,1)}, u32[]{:S(2)}, u32[]{:S(2)}) collective-permute-start(bf16[1,2,128,1024]{3,2,1,0:T(8,128)(2,1)} %maximum_bitcast_fusion.2), channel_id=1, source_target_pairs={{0,16},{16,0},{1,17},{17,1},{2,18},{18,2},{3,19},{19,3},{4,20},{20... | collective-permute-start | bytes 1572872 | tf_op jit(solution)/shard_map/ppermute | solution.py:18
  368.2 15.4 %collective-permute-start.32 = (bf16[1024,512]{1,0:T(8,128)(2,1)}, bf16[1024,512]{1,0:T(8,128)(2,1)}, u32[]{:S(2)}, u32[]{:S(2)}) collective-permute-start(bf16[1024,512]{1,0:T(8,128)(2,1)} %fusion.20), channel_id=1, source_target_pairs={{0,4},{4,0},{8,12},{12,8},{1,5},{5,1},{9,13},{13,9},{2,6},{6,2},{1... | collective-permute-start | bytes 3145736 | tf_op jit(solution)/shard_map/ppermute | solution.py:18
  371.7 15.8 %collective-permute-start.35 = (bf16[4,64,256]{2,1,0:T(8,128)(2,1)S(1)}, bf16[4,64,256]{2,1,0:T(8,128)(2,1)}, u32[]{:S(2)}, u32[]{:S(2)}) collective-permute-start(bf16[4,64,256]{2,1,0:T(8,128)(2,1)S(1)} %bitcast_reduce_fusion.1), channel_id=1, source_target_pairs={{0,16},{16,0},{1,17},{17,1},{2,18},{18,2},{3,19},{19,3},{4,20},{20... | collective-permute-start | bytes 393224 | tf_op jit(solution)/shard_map/ppermute | solution.py:18
  383.5 19.0 %collective-permute-start.26 = (bf16[1,768,256]{2,1,0:T(8,128)(2,1)S(1)}, bf16[1,768,256]{2,1,0:T(8,128)(2,1)S(1)}, u32[]{:S(2)}, u32[]{:S(2)}) collective-permute-start(bf16[1,768,256]{2,1,0:T(8,128)(2,1)S(1)} %bitcast.306), channel_id=1, source_target_pairs={{0,12},{4,8},{8,4},{12,0},{1,13},{5,9},{9,5},{13,1},{2,14},{6,10},... | collective-permute-start | bytes 1179656 | tf_op jit(solution)/shard_map/ppermute | solution.py:18
  385.7 32.9 %collective-permute-start.33 = (bf16[1024,256]{1,0:T(8,128)(2,1)}, bf16[1024,256]{1,0:T(8,128)(2,1)}, u32[]{:S(2)}, u32[]{:S(2)}) collective-permute-start(bf16[1024,256]{1,0:T(8,128)(2,1)} %fusion.36), channel_id=1, source_target_pairs={{0,8},{4,12},{8,0},{12,4},{1,9},{5,13},{9,1},{13,5},{2,10},{6,14},... | collective-permute-start | bytes 1572872 | tf_op jit(solution)/shard_map/ppermute | solution.py:18
  410.4 18.3 %all-to-all-start.8 = ((f32[32,8,256]{2,1,0:T(8,128)}), f32[32,8,256]{2,1,0:T(8,128)S(1)}, u32[]{:S(2)}, u32[]{:S(2)}) async-start(f32[32,8,256]{2,1,0:T(8,128)} %bitcast.80), calls=%async_computation.9 | async-start | bytes 524288 | tf_op jit(solution)/shard_map/all_to_all | solution.py:32
  (111 other events, 779.9 us)
Sparse Core Ops, SparseCore 0:
  287.7 71.3 reduce-scatter.1
where the time goes:
time: 445 us; the launch traced here: 437 us
  waiting for transfers between devices  144 us (32%)
  starting transfers between devices  79 us (18%)
  local copies, waits for them, and re-layouts  76.1 us (17%)
  other arithmetic  67.1 us (15%)
  matrix products  54.7 us (12%)
  between operations  16.4 us (4%)
    ppermute x30, waiting for transfers between devices, swap(): return lax.ppermute(values, axis, [(i, i ^ bit) for i in range(size)])  91.3 us
    all_to_all x9, starting transfers between devices, trade(): return lax.all_to_all(values, axis, 0, 0, tiled=True)  46.4 us
    dot_general x20, matrix products, dot(): lax.dot_general(left, right, (((left_dim,), (right_dim,)), ((), ())), pre...  39.3 us
    all_to_all x9, waiting for transfers between devices, trade(): return lax.all_to_all(values, axis, 0, 0, tiled=True)  29 us
    unnamed x200, local copies, waits for them, and re-layouts  23 us
    ppermute x3, waiting for transfers between devices, line_step(): lax.ppermute(up, 'col', [(i, i - 1) for i in range(1, size - step + 1)])  22.3 us
    ppermute x30, starting transfers between devices, swap(): return lax.ppermute(values, axis, [(i, i ^ bit) for i in range(size)])  20.3 us
  transfers between devices with their start and end apart: 46, of which 23 were waited for; matrix products, arithmetic and copies ran while one was open for 37% of the time, Pallas kernels for 0%

commit v1 on v0

--- a/solution.py
+++ b/solution.py
@@ -1,6 +1,8 @@
 import jax
 import jax.numpy as jnp
 from jax import lax
+from jax.experimental import pallas as pl
+from jax.experimental.pallas import tpu as pltpu
 from jax.sharding import PartitionSpec as P
 
 HEAD_DIM = 64
@@ -111,6 +113,60 @@
         values = low.astype(f32) + swap(low, "dp", bit).astype(f32)
         bit *= 2
     return values
+
+
+def head_part(values, head, part):
+    start = (3 * head + part) * HEAD_DIM
+    return values[:, start : start + HEAD_DIM]
+
+
+def attend_kernel(qkv_ref, out_ref):
+    qkv = qkv_ref[...]
+    for head in range(out_ref.shape[1] // HEAD_DIM):
+        queries, keys, vals = [head_part(qkv, head, part) for part in range(3)]
+        scores = dot(queries, keys, 1, 1) * HEAD_DIM ** (-0.5)
+        expo = jnp.exp(scores - jnp.max(scores, 1, keepdims=True))
+        weights = expo / jnp.sum(expo, 1, keepdims=True)
+        context = dot(weights.astype(bf16), vals, 1, 0).astype(bf16)
+        out_ref[:, head * HEAD_DIM : (head + 1) * HEAD_DIM] = context
+
+
+def attend_back_kernel(qkv_ref, d_context_ref, out_ref):
+    qkv = qkv_ref[...]
+    scale = HEAD_DIM ** (-0.5)
+    for head in range(d_context_ref.shape[1] // HEAD_DIM):
+        queries, keys, vals = [head_part(qkv, head, part) for part in range(3)]
+        d_context = d_context_ref[:, head * HEAD_DIM : (head + 1) * HEAD_DIM]
+        scores = dot(keys, queries, 1, 1) * scale
+        expo = jnp.exp(scores - jnp.max(scores, 0, keepdims=True))
+        weights = expo / jnp.sum(expo, 0, keepdims=True)
+        d_value = dot(weights.astype(bf16), d_context, 1, 0)
+        d_weights = dot(vals, d_context, 1, 1)
+        inner = jnp.sum(d_weights * weights, 0, keepdims=True)
+        d_scores = (weights * (d_weights - inner)).astype(bf16)
+        d_key = dot(d_scores, queries, 1, 0) * scale
+        d_query = dot(d_scores, keys, 0, 0) * scale
+        for part, grad in enumerate((d_query, d_key, d_value)):
+            start = (3 * head + part) * HEAD_DIM
+            out_ref[:, start : start + HEAD_DIM] = grad.astype(bf16)
+
+
+def by_sequence(kernel, operands, width, flops):
+    tokens = operands[0].shape[0]
+    heads = operands[0].shape[1] // (3 * HEAD_DIM)
+    return pl.pallas_call(
+        kernel,
+        grid=(tokens // SEQ_LEN,),
+        in_specs=[pl.BlockSpec((SEQ_LEN, v.shape[1]), lambda i: (i, 0)) for v in operands],
+        out_specs=pl.BlockSpec((SEQ_LEN, width), lambda i: (i, 0)),
+        out_shape=jax.ShapeDtypeStruct((tokens, width), bf16),
+        compiler_params=pltpu.CompilerParams(vmem_limit_bytes=40 * 2**20),
+        cost_estimate=pl.CostEstimate(
+            flops=flops * tokens * SEQ_LEN * heads * HEAD_DIM,
+            bytes_accessed=2 * tokens * (width + sum(v.shape[1] for v in operands)),
+            transcendentals=tokens * SEQ_LEN * heads,
+        ),
+    )(*operands)
 
 
 def per_device(
@@ -142,10 +198,6 @@
     hid_piece = hid_tile // rows
     half = hid_piece // 2
     hid_half = cols * half
-    seq_count = group // SEQ_LEN
-    head_count = heads_width // HEAD_DIM
-    score_scale = HEAD_DIM ** (-0.5)
-    seq_shape = (seq_count, SEQ_LEN, head_count, HEAD_DIM)
 
     heads_rows = 3 * head_piece
     wq = jnp.transpose(w_qkv, (2, 0, 1)).reshape(rows, head_piece, 3, width_local)
@@ -185,9 +237,11 @@
     steps.append(line_step(mine, mine, 1))
     steps[1], wi = lax.optimization_barrier((steps[1], wi))
     steps.append(line_step(*steps[1], 2))
+    wi = spread(wi, "col").reshape(hid_half, width)
+    steps[2], wi = lax.optimization_barrier((steps[2], wi))
     steps.append(line_step(*steps[2], 3))
-    wi = spread(wi, "col").reshape(hid_half, width)
-    steps[3], wi = lax.optimization_barrier((steps[3], wi))
+    wb = spread(after(wb, wi), "col").reshape(hid_half, width)
+    steps[3], wb = lax.optimization_barrier((steps[3], wb))
     ours = line_blocks(steps)
     middle = swap(ours[1], "dp", 1)
     ends = swap(jnp.stack([ours[0], ours[2]]), "dp", 1)
@@ -195,13 +249,13 @@
     for our, their in zip(ours, [ends[0], middle, ends[1]]):
         both = [jnp.where(n == 0, our, their), jnp.where(n == 0, their, our)]
         line.append(jnp.concatenate(both, 0))
-    wq_all = in_col_order([b[:heads_rows].reshape(3, head_piece, width) for b in line])
-    wq_all = jnp.transpose(wq_all, (1, 0, 2, 3)).reshape(3 * heads_width, width)
+    wq_all = in_col_order([b[:heads_rows] for b in line]).reshape(3 * heads_width, width)
     bias_at = heads_rows + head_piece
     wo_all = in_col_order([b[heads_rows:bias_at] for b in line]).reshape(heads_width, width)
     col_bias = in_col_order([b[bias_at, : bias_row.shape[0]] for b in line]).astype(f32)
-    bias_q = col_bias[:, hid_piece : hid_piece + head_piece].reshape(-1)
-    bias_v = col_bias[:, hid_piece + head_piece :].reshape(-1)
+    bias_q = col_bias[:, hid_piece : hid_piece + head_piece]
+    bias_v = col_bias[:, hid_piece + head_piece :]
+    bias_qkv = jnp.concatenate([bias_q, jnp.zeros_like(bias_q), bias_v], 1).reshape(-1)
     bias_in_f = jnp.transpose(col_bias[:, :hid_piece].reshape(cols, 2, half), (1, 0, 2)).reshape(-1)
 
     across = swap(tokens, "row", 2)
@@ -209,29 +263,15 @@
     diagonal = swap(across, "row", 1)
     tokens_all = jnp.concatenate([tokens, across, beside, diagonal], 1)
 
-    wb = spread(after(wb, steps[3]), "col").reshape(hid_half, width)
     wi_all = both_halves(wi)
     cot = after(cotangent, wb).reshape(rows, block, width_local)
     cot = jnp.transpose(trade(cot, "row"), (1, 0, 2)).reshape(block, width).astype(f32)
 
-    joined = dot(tokens_all, wq_all, 1, 1)
-    queries = (joined[:, :heads_width] + bias_q).astype(bf16).reshape(seq_shape)
-    key_rows = joined[:, heads_width : 2 * heads_width].astype(bf16).reshape(seq_shape)
-    value_rows = (joined[:, 2 * heads_width :] + bias_v).astype(bf16).reshape(seq_shape)
-    scores = (
-        jnp.einsum("sqhd,skhd->shqk", queries, key_rows, preferred_element_type=f32) * score_scale
-    )
-    row_peak = jnp.max(scores, -1, keepdims=True)
-    expo_scores = jnp.exp(scores - row_peak)
-    row_total = jnp.sum(expo_scores, -1, keepdims=True)
-    attn_weights = expo_scores / row_total
-    log_total = row_peak + jnp.log(row_total)
-    context = jnp.einsum(
-        "shqk,skhd->sqhd", attn_weights.astype(bf16), value_rows, preferred_element_type=f32
-    )
+    joined = (dot(tokens_all, wq_all, 1, 1) + bias_qkv).astype(bf16)
+    context = by_sequence(attend_kernel, [joined], heads_width, 4)
     context, wb, wi_all = lax.optimization_barrier((context, wb, wi_all))
     wb_all = both_halves(wb)
-    context = to_rel(context.reshape(group, heads_width).astype(bf16), 0)
+    context = to_rel(context, 0)
 
     send = dot(context[2 * block :], wo_all, 1, 0).astype(bf16)
     keep = dot(context[: 2 * block], wo_all, 1, 0)
@@ -270,18 +310,101 @@
         pdf = jnp.exp(-0.5 * pre_act[k] * pre_act[k]) * 0.3989422804014327
         d_pre.append((d_activated * (cdf[k] + pre_act[k] * pdf)).astype(bf16))
         d_hid.append(dot(d_pre[k], wi_all, 1, 0))
+    grad_wb = sum(dot(a, b, 0, 0) for a, b in zip(activated, d_mlp)).astype(bf16)
     d_hidden = d_two + reduce_chips(*d_hid)
-    def hidden_grad(left, right):
-        return sum(dot(a, b, 0, 0) for a, b in zip(left, right)).astype(bf16)
-
-    grad_wb = hidden_grad(activated, d_mlp)
-    grad_wi = hidden_grad(d_pre, hidden)
-    hid_grads_gate = None
+    d_hidden, _ = lax.optimization_barrier((d_hidden, grad_wb))
+    grad_wi = sum(dot(a, b, 0, 0) for a, b in zip(d_pre, hidden)).astype(bf16)
+    grad_wi_ready, hid_grads_gate = grad_wi, None
     if dp_size == 2:
         grad_wb = trade(grad_wb.reshape(2 * cols, half, width), ("dp", "col"))
         hid_grads_gate = grad_wb
+        grad_wi = lax.psum_scatter(grad_wi, ("dp", "col"), scatter_dimension=0, tiled=True)
+
+    d_one = norm_backward(d_hidden, normed_one, inv_one, gain_one_f)
+    d_att = d_one.astype(bf16)
+    over = swap(d_att, "row", 2)
+    over, _ = lax.optimization_barrier((over, grad_wi_ready))
+    d_att_all = jnp.concatenate([d_att, over, swap(d_att, "row", 1), swap(over, "row", 1)], 0)
+
+    def by_owner(values):
+        each = values.shape[2]
+        raw = trade(values.reshape(-1, each, width_local), ("row", "col"))
+        got = jnp.sum(raw.reshape(rows, cols, each, width_local).astype(f32), 1)
+        return dp_sum(got, 1), raw
+
+    grad_wo = dot(context, d_att_all, 0, 0).astype(bf16).reshape(cols, head_piece, rows, width_local)
+    grad_wo = jnp.transpose(grad_wo, (2, 0, 1, 3))
+
+    d_context = from_rel(dot(d_att_all, wo_all, 1, 1).astype(bf16), 0)
+    d_joined = by_sequence(attend_back_kernel, [joined, d_context], 3 * heads_width, 10)
+    d_joined, _ = lax.optimization_barrier((d_joined, hid_grads_gate))
+    grad_wq = []
+    for a in range(rows):
+        j = r ^ a
+        place = (((j & 1) << 1) | (j >> 1)) * width_local
+        owned = lax.dynamic_slice_in_dim(tokens_all, place, width_local, 1)
+        grad_wq.append(dot(d_joined, owned, 0, 0).astype(bf16).reshape(cols, heads_rows, -1))
+    grad_wq = jnp.concatenate([jnp.stack(grad_wq), grad_wo], 2)
+    d_joined_late = after(d_joined, grad_wq)
+    grad_wq, arrived = by_owner(grad_wq)
+    grad_w_out = grad_wq[:, heads_rows:].reshape(heads_tile, width_local)
+    grad_wq = grad_wq[:, :heads_rows].reshape(rows, 3, head_piece, width_local)
+    grad_w_qkv = jnp.transpose(grad_wq, (1, 3, 0, 2)).reshape(3, width_local, heads_tile)
+
+    split = 2 * width_local
+    d_one_rel = to_rel(d_one, 1)
+    own_rows = (jnp.arange(rows) == r)[:, None, None]
+
+    def with_own(values, own):
+        values = values.reshape(rows, block, split)
+        return (values + jnp.where(own_rows, own[None], 0.0)).reshape(group, split)
+
+    keep = with_own(dot(d_joined_late, wq_all[:, :split], 1, 0), d_one_rel[:, :split])
+    send = with_own(dot(d_joined_late, wq_all[:, split:], 1, 0), d_one_rel[:, split:]).astype(bf16)
+    grad_tokens = row_reduce(
+        keep[:, :width_local],
+        keep[:, width_local:],
+        send[:, :width_local],
+        send[:, width_local:],
+        1,
+    )
+
+    vector_grads = jnp.stack(
+        [
+            jnp.sum(d_att, 0, dtype=f32),
+            jnp.sum(d_hidden * normed_one, 0),
+            jnp.sum(d_hidden, 0),
+            jnp.sum(d_mlp_low, 0, dtype=f32),
+            jnp.sum(cot * normed_two, 0),
+            jnp.sum(cot, 0),
+        ]
+    )
+    vector_grads = jnp.transpose(vector_grads.reshape(6, rows, width_local), (1, 0, 2))
+    hid_sums = sum(jnp.sum(d, 0, dtype=f32) for d in d_pre).reshape(2, cols, half)
+    hid_sums = jnp.transpose(hid_sums, (1, 0, 2)).reshape(1, cols, 1, hid_piece)
+    head_sums = jnp.sum(d_joined, 0, dtype=f32).reshape(cols, 3, head_piece)
+    head_sums = jnp.concatenate([head_sums[:, 0], head_sums[:, 2]], 1)
+    head_sums = jnp.pad(head_sums, ((0, 0), (0, width_local - 2 * head_piece)))
+    col_sums = jnp.concatenate([hid_sums, head_sums[None, :, None]], 2)
+    small = jnp.concatenate(
+        [
+            jnp.broadcast_to(vector_grads[:, None], (rows, cols, 6, width_local)),
+            jnp.broadcast_to(col_sums, (rows, cols, 2, width_local)),
+        ],
+        2,
+    )
+    small = jnp.broadcast_to(small[None], (dp_size,) + small.shape)
+    small = after(small, arrived)
+    small = trade(small.reshape(-1, 8, width_local), ("dp", "row", "col"))
+    small = small.reshape(dp_size, rows, cols, 8, width_local)
+    vector_grads = jnp.sum(small[:, :, :, :6], (0, 1, 2))
+    grad_bias_in = jnp.sum(small[:, :, :, 6], (0, 2)).reshape(hid_tile)
+    head_sums = jnp.sum(small[:, :, :, 7, : 2 * head_piece], (0, 2)).reshape(rows, 2, head_piece)
+    grad_bias_qv = jnp.transpose(head_sums, (1, 0, 2)).reshape(2, heads_tile)
+
+    if dp_size == 2:
         grad_wb = jnp.sum(grad_wb.astype(f32), 0).astype(bf16)
-        grad_wi = lax.psum_scatter(grad_wi, ("dp", "col"), scatter_dimension=0, tiled=True)
+        grad_wi = after(grad_wi, send)
         hid_grads = both_halves(jnp.stack([grad_wb, grad_wi])[None])
     else:
         hid_grads = jnp.stack([grad_wb, grad_wi]).reshape(2, 2, cols, half, width)
@@ -302,105 +425,6 @@
     grad_w_back = hid_grads[:, :hid_piece].reshape(hid_tile, width_local).astype(f32)
     grad_w_in = hid_grads[:, hid_piece : 2 * hid_piece].reshape(hid_tile, width_local)
     grad_w_in = jnp.transpose(grad_w_in).astype(f32)
-
-    d_one = norm_backward(d_hidden, normed_one, inv_one, gain_one_f)
-    d_att = d_one.astype(bf16)
-    over = swap(d_att, "row", 2)
-    d_att_all = jnp.concatenate([d_att, over, swap(d_att, "row", 1), swap(over, "row", 1)], 0)
-    d_att_all, _ = lax.optimization_barrier((d_att_all, hid_grads_gate))
-
-    def by_owner(values):
-        each = values.shape[1]
-        got = jnp.transpose(values, (2, 0, 1, 3)).reshape(-1, each, width_local)
-        raw = trade(got, ("row", "col"))
-        got = jnp.sum(raw.reshape(rows, cols, each, width_local).astype(f32), 1)
-        return dp_sum(got, 1), raw
-
-    grad_wo = dot(context, d_att_all, 0, 0).astype(bf16).reshape(cols, head_piece, rows, width_local)
-    grad_w_out = by_owner(grad_wo)[0].reshape(heads_tile, width_local)
-
-    d_context = from_rel(dot(d_att_all, wo_all, 1, 1).astype(bf16), 0).reshape(seq_shape)
-    scores_again = (
-        jnp.einsum("sqhd,skhd->shqk", queries, key_rows, preferred_element_type=f32) * score_scale
-    )
-    weights_again = jnp.exp(scores_again - log_total)
-    d_value = jnp.einsum(
-        "shqk,sqhd->skhd", weights_again.astype(bf16), d_context, preferred_element_type=f32
-    )
-    d_weights = jnp.einsum("sqhd,skhd->shqk", d_context, value_rows, preferred_element_type=f32)
-    row_inner = jnp.sum(d_weights * weights_again, -1, keepdims=True)
-    d_scores = (weights_again * (d_weights - row_inner)).astype(bf16)
-    d_query = (
-        jnp.einsum("shqk,skhd->sqhd", d_scores, key_rows, preferred_element_type=f32) * score_scale
-    )
-    d_key = (
-        jnp.einsum("shqk,sqhd->skhd", d_scores, queries, preferred_element_type=f32) * score_scale
-    )
-    d_joined = jnp.concatenate(
-        [
-            d_query.reshape(group, heads_width),
-            d_key.reshape(group, heads_width),
-            d_value.reshape(group, heads_width),
-        ],
-        1,
-    ).astype(bf16)
-    grad_wq = dot(d_joined, tokens_all, 0, 0).astype(bf16)
-    grad_wq = from_rel(grad_wq, 1).reshape(3, cols, head_piece, width)
-    grad_wq = jnp.transpose(grad_wq, (1, 0, 2, 3)).reshape(cols, heads_rows, rows, width_local)
-    head_sums = jnp.sum(d_joined.reshape(group, 3, cols, head_piece), 0, dtype=f32)
-    head_sums = jnp.concatenate([head_sums[0], head_sums[2]], 1).astype(bf16)
-    head_sums = jnp.pad(head_sums, ((0, 0), (0, width_local - 2 * head_piece)))
-    head_sums = jnp.broadcast_to(head_sums[:, None, None], (cols, 16, rows, width_local))
-    grad_wq, arrived = by_owner(jnp.concatenate([grad_wq, head_sums], 1))
-    head_sums = grad_wq[:, heads_rows, : 2 * head_piece].reshape(rows, 2, head_piece)
-    grad_bias_qv = jnp.transpose(head_sums, (1, 0, 2)).reshape(2, heads_tile)
-    grad_wq = grad_wq[:, :heads_rows].reshape(rows, 3, head_piece, width_local)
-    grad_w_qkv = jnp.transpose(grad_wq, (1, 3, 0, 2)).reshape(3, width_local, heads_tile)
-
-    split = 2 * width_local
-    d_one_rel = to_rel(d_one, 1)
-    own_rows = (jnp.arange(rows) == r)[:, None, None]
-
-    def with_own(values, own):
-        values = values.reshape(rows, block, split)
-        return (values + jnp.where(own_rows, own[None], 0.0)).reshape(group, split)
-
-    keep = with_own(dot(d_joined, wq_all[:, :split], 1, 0), d_one_rel[:, :split])
-    send = with_own(dot(d_joined, wq_all[:, split:], 1, 0), d_one_rel[:, split:]).astype(bf16)
-    grad_tokens = row_reduce(
-        keep[:, :width_local],
-        keep[:, width_local:],
-        send[:, :width_local],
-        send[:, width_local:],
-        1,
-    )
-
-    vector_grads = jnp.stack(
-        [
-            jnp.sum(d_att, 0, dtype=f32),
-            jnp.sum(d_hidden * normed_one, 0),
-            jnp.sum(d_hidden, 0),
-            jnp.sum(d_mlp_low, 0, dtype=f32),
-            jnp.sum(cot * normed_two, 0),
-            jnp.sum(cot, 0),
-        ]
-    )
-    vector_grads = jnp.transpose(vector_grads.reshape(6, rows, width_local), (1, 0, 2))
-    hid_sums = sum(jnp.sum(d, 0, dtype=f32) for d in d_pre).reshape(2, cols, half)
-    hid_sums = jnp.transpose(hid_sums, (1, 0, 2)).reshape(1, cols, 1, hid_piece)
-    small = jnp.concatenate(
-        [
-            jnp.broadcast_to(vector_grads[:, None], (rows, cols, 6, width_local)),
-            jnp.broadcast_to(hid_sums, (rows, cols, 2, width_local)),
-        ],
-        2,
-    )
-    small = jnp.broadcast_to(small[None], (dp_size,) + small.shape)
-    small = after(small, arrived)
-    small = trade(small.reshape(-1, 8, width_local), ("dp", "row", "col"))
-    small = small.reshape(dp_size, rows, cols, 8, width_local)
-    vector_grads = jnp.sum(small[:, :, :, :6], (0, 1, 2))
-    grad_bias_in = jnp.sum(small[:, :, :, 6], (0, 2)).reshape(hid_tile)
 
     return (
         output,

time: 445 us -> 494 us (1.11)
  waiting for transfers between devices: 144 us -> 241 us
  local copies, waits for them, and re-layouts: 76.1 us -> 47.1 us
  other arithmetic: 67.1 us -> 49.4 us
  Pallas kernels: 0 us -> 15.7 us
  matrix products: 54.7 us -> 42.1 us
    ppermute x30 -> x29, waiting for transfers between devices: 91.3 us -> 128 us  [swap(): return lax.ppermute(values, axis, [(i, i ^ bit) for i in range(size)])]
    reduce_scatter x1, waiting for transfers between devices: 0.25 us -> 35.2 us  [per_device(): lax.psum_scatter(grad_wi, ('dp', 'col'), scatter_dimension=0, tiled=True)]
    all_to_all x9 -> x8, waiting for transfers between devices: 29 us -> 48.8 us  [trade(): return lax.all_to_all(values, axis, 0, 0, tiled=True)]
    pallas_call x0 -> x2, Pallas kernels: none -> 15.7 us  [by_sequence(): pl.pallas_call(kernel, grid=(tokens // SEQ_LEN,), in_specs=[pl.BlockSpec(...]
    dot_general x6 -> x0, matrix products: 15.4 us -> none  [the longest x1 5.04 us: per_device(): jnp.einsum('shqk,sqhd->skhd', weights_again.astype(bf16), d_context, pref...]
    reshape x10 -> x2, local copies, waits for them, and re-layouts: 12.6 us -> 0.16 us  [the longest x1 0.08 us: per_device(): jnp.sum(small[:, :, :, 7, :2 * head_piece], (0, 2))]
    ppermute x3, waiting for transfers between devices: 22.3 us -> 27.9 us  [line_step(): lax.ppermute(up, 'col', [(i, i - 1) for i in range(1, size - step + 1)])]
    all_to_all x9 -> x8, starting transfers between devices: 46.4 us -> 43.1 us  [trade(): return lax.all_to_all(values, axis, 0, 0, tiled=True)]
  transfers between devices with their start and end apart: 46 -> 44, of which waited for: 23 -> 26; matrix products, arithmetic and copies ran while one was open for 37% -> 19% of each run, Pallas kernels for 0% -> 2%
where the time goes in v1:
time: 494 us; the launch traced here: 488 us
  waiting for transfers between devices  241 us (49%)
  starting transfers between devices  75.9 us (15%)
  other arithmetic  49.4 us (10%)
  local copies, waits for them, and re-layouts  47.1 us (10%)
  matrix products  42.1 us (9%)
  between operations  16.2 us (3%)
  Pallas kernels  15.7 us (3%)
    ppermute x29, waiting for transfers between devices, swap(): return lax.ppermute(values, axis, [(i, i ^ bit) for i in range(size)])  128 us
    all_to_all x8, waiting for transfers between devices, trade(): return lax.all_to_all(values, axis, 0, 0, tiled=True)  48.8 us
    all_to_all x8, starting transfers between devices, trade(): return lax.all_to_all(values, axis, 0, 0, tiled=True)  43.1 us
    dot_general x23, matrix products, dot(): lax.dot_general(left, right, (((left_dim,), (right_dim,)), ((), ())), pre...  42.1 us
    reduce_scatter x1, waiting for transfers between devices, per_device(): lax.psum_scatter(grad_wi, ('dp', 'col'), scatter_dimension=0, tiled=True)  35.2 us
    ppermute x3, waiting for transfers between devices, line_step(): lax.ppermute(up, 'col', [(i, i - 1) for i in range(1, size - step + 1)])  27.9 us
    ppermute x29, starting transfers between devices, swap(): return lax.ppermute(values, axis, [(i, i ^ bit) for i in range(size)])  21.8 us
    unnamed x180, local copies, waits for them, and re-layouts  20.7 us
  transfers between devices with their start and end apart: 44, of which 26 were waited for; matrix products, arithmetic and copies ran while one was open for 19% of the time, Pallas kernels for 2%

profile of v1, /device:TPU:0, one launch (start us, length us, event | category | flops | bytes accessed | tf_op | source)
XLA Modules:
  0.0 487.6 jit_solution(13094327501617312987)
XLA Ops:
  16.8 6.6 %all-to-all-done = bf16[4,256,256]{2,1,0:T(8,128)(2,1)S(1)} async-done(((bf16[4,256,256]{2,1,0:T(8,128)(2,1)}), bf16[4,256,256]{2,1,0:T(8,128)(2,1)S(1)}, u32[]{:S(2)}, u32[]{:S(2)}) %all-to-all-start) | async-done | bytes 524320 | tf_op jit(solution)/shard_map/all_to_all | solution.py:34
  42.0 5.9 %all-to-all-start.2 = ((bf16[4,128,1024]{2,1,0:T(8,128)(2,1)}), bf16[4,128,1024]{2,1,0:T(8,128)(2,1)}, u32[]{:S(2)}, u32[]{:S(2)}) async-start(bf16[4,128,1024]{2,1,0:T(8,128)(2,1)} %broadcast_in_dim.134), calls=%async_computation.2 | async-start | bytes 2097152 | tf_op jit(solution)/shard_map/all_to_all | solution.py:34
  50.1 18.3 %collective-permute-done.5 = bf16[144,1024]{1,0:T(8,128)(2,1)S(1)} collective-permute-done((bf16[144,1024]{1,0:T(8,128)(2,1)S(1)}, bf16[144,1024]{1,0:T(8,128)(2,1)S(1)}, u32[]{:S(2)}, u32[]{:S(2)}) %collective-permute-start.5) | collective-permute-done | bytes 294944 | tf_op jit(solution)/shard_map/ppermute | solution.py:66
  68.4 5.9 %all-to-all-done.2 = bf16[4,128,1024]{2,1,0:T(8,128)(2,1)} async-done(((bf16[4,128,1024]{2,1,0:T(8,128)(2,1)}), bf16[4,128,1024]{2,1,0:T(8,128)(2,1)}, u32[]{:S(2)}, u32[]{:S(2)}) %all-to-all-start.2) | async-done | bytes 1048608 | tf_op jit(solution)/shard_map/all_to_all | solution.py:34
  75.6 7.0 %all-to-all-start.3 = ((bf16[4,128,1024]{2,1,0:T(8,128)(2,1)}), bf16[4,128,1024]{2,1,0:T(8,128)(2,1)S(1)}, u32[]{:S(2)}, u32[]{:S(2)}) async-start(bf16[4,128,1024]{2,1,0:T(8,128)(2,1)} %broadcast_in_dim.135), calls=%async_computation.3 | async-start | bytes 2097152 | tf_op jit(solution)/shard_map/all_to_all | solution.py:34
  84.0 11.6 %collective-permute-done = bf16[1024,256]{1,0:T(8,128)(2,1)} collective-permute-done((bf16[1024,256]{1,0:T(8,128)(2,1)}, bf16[1024,256]{1,0:T(8,128)(2,1)}, u32[]{:S(2)}, u32[]{:S(2)}) %collective-permute-start) | collective-permute-done | bytes 524320 | tf_op jit(solution)/shard_map/ppermute | solution.py:20
  107.6 6.2 %collective-permute-done.7 = bf16[144,1024]{1,0:T(8,128)(2,1)S(1)} collective-permute-done((bf16[144,1024]{1,0:T(8,128)(2,1)S(1)}, bf16[144,1024]{1,0:T(8,128)(2,1)S(1)}, u32[]{:S(2)}, u32[]{:S(2)}) %collective-permute-start.7) | collective-permute-done | bytes 294944 | tf_op jit(solution)/shard_map/ppermute | solution.py:66
  118.5 19.6 %collective-permute-done.10 = bf16[144,1024]{1,0:T(8,128)(2,1)} collective-permute-done((bf16[144,1024]{1,0:T(8,128)(2,1)S(1)}, bf16[144,1024]{1,0:T(8,128)(2,1)}, u32[]{:S(2)}, u32[]{:S(2)}) %collective-permute-start.10) | collective-permute-done | bytes 294944 | tf_op jit(solution)/shard_map/ppermute | solution.py:20
  143.1 7.1 %collective-permute-done.9 = bf16[2,144,1024]{2,1,0:T(8,128)(2,1)S(1)} collective-permute-done((bf16[2,144,1024]{2,1,0:T(8,128)(2,1)S(1)}, bf16[2,144,1024]{2,1,0:T(8,128)(2,1)S(1)}, u32[]{:S(2)}, u32[]{:S(2)}) %collective-permute-start.9) | collective-permute-done | bytes 589856 | tf_op jit(solution)/shard_map/ppermute | solution.py:20
  156.0 6.5 %shard_map.245 = bf16[1024,256]{1,0:T(8,128)(2,1)S(1)} custom-call(bf16[1024,768]{1,0:T(8,128)(2,1)S(1)} %add_convert_fusion.2.qkv_ref), custom_call_target="tpu_custom_call" | custom-call | flops 536870912 | bytes 2097152 | tf_op jit(solution)/shard_map/pallas_call | solution.py:157
  173.6 8.1 %collective-permute-done.13 = bf16[256,1024]{1,0:T(8,128)(2,1)S(1)} collective-permute-done((bf16[256,1024]{1,0:T(8,128)(2,1)S(1)}, bf16[256,1024]{1,0:T(8,128)(2,1)S(1)}, u32[]{:S(2)}, u32[]{:S(2)}) %collective-permute-start.13) | collective-permute-done | bytes 524320 | tf_op jit(solution)/shard_map/ppermute | solution.py:20
  185.6 11.8 %collective-permute-done.16 = bf16[256,1024]{1,0:T(8,128)(2,1)S(1)} collective-permute-done((bf16[256,1024]{1,0:T(8,128)(2,1)S(1)}, bf16[256,1024]{1,0:T(8,128)(2,1)S(1)}, u32[]{:S(2)}, u32[]{:S(2)}) %collective-permute-start.16) | collective-permute-done | bytes 524320 | tf_op jit(solution)/shard_map/ppermute | solution.py:20
  223.9 9.4 %collective-permute-done.19 = bf16[256,1024]{1,0:T(8,128)(2,1)} collective-permute-done((bf16[256,1024]{1,0:T(8,128)(2,1)}, bf16[256,1024]{1,0:T(8,128)(2,1)}, u32[]{:S(2)}, u32[]{:S(2)}) %collective-permute-start.19) | collective-permute-done | bytes 524320 | tf_op jit(solution)/shard_map/ppermute | solution.py:20
  238.9 13.1 %collective-permute-done.21 = bf16[256,1024]{1,0:T(8,128)(2,1)S(1)} collective-permute-done((bf16[256,1024]{1,0:T(8,128)(2,1)S(1)}, bf16[256,1024]{1,0:T(8,128)(2,1)S(1)}, u32[]{:S(2)}, u32[]{:S(2)}) %collective-permute-start.21) | collective-permute-done | bytes 524320 | tf_op jit(solution)/shard_map/ppermute | solution.py:20
  274.3 6.7 %all-to-all-start.5 = ((bf16[8,128,1024]{2,1,0:T(8,128)(2,1)}), bf16[8,128,1024]{2,1,0:T(8,128)(2,1)}, u32[]{:S(2)}, u32[]{:S(2)}) async-start(bf16[8,128,1024]{2,1,0:T(8,128)(2,1)} %bitcast.212), calls=%async_computation.5 | async-start | bytes 4194304 | tf_op jit(solution)/shard_map/all_to_all | solution.py:34
  281.2 5.5 %add_convert_fusion = bf16[1024,1024]{1,0:T(8,128)(2,1)} fusion(f32[1024,1024]{1,0:T(8,128)} %fusion.35, bf16[512,1024]{1,0:T(8,128)(2,1)} %copy-done.36, bf16[512,1024]{1,0:T(8,128)(2,1)} %copy-done.12), kind=kOutput, calls=%fused_computation | convolution fusion | flops 1075838976 | bytes 8388608 | tf_op jit(solution)/shard_map/dot_general | solution.py:24
  292.5 13.4 %collective-permute-done.25 = bf16[256,1024]{1,0:T(8,128)(2,1)S(1)} collective-permute-done((bf16[256,1024]{1,0:T(8,128)(2,1)S(1)}, bf16[256,1024]{1,0:T(8,128)(2,1)S(1)}, u32[]{:S(2)}, u32[]{:S(2)}) %collective-permute-start.25) | collective-permute-done | bytes 524320 | tf_op jit(solution)/shard_map/ppermute | solution.py:20
  313.0 9.2 %shard_map.246 = bf16[1024,768]{1,0:T(8,128)(2,1)S(1)} custom-call(bf16[1024,768]{1,0:T(8,128)(2,1)S(1)} %add_convert_fusion.2.qkv_ref, bf16[1024,256]{1,0:T(8,128)(2,1)S(1)} %pad_maximum_fusion.17.d_context_ref), custom_call_target="tpu_custom_call" | custom-call | flops 1342177280 | bytes 3670016 | tf_op jit(solution)/shard_map/pallas_call | solution.py:157
  322.3 25.4 %all-to-all-done.5 = bf16[8,128,1024]{2,1,0:T(8,128)(2,1)} async-done(((bf16[8,128,1024]{2,1,0:T(8,128)(2,1)}), bf16[8,128,1024]{2,1,0:T(8,128)(2,1)}, u32[]{:S(2)}, u32[]{:S(2)}) %all-to-all-start.5) | async-done | bytes 2097184 | tf_op jit(solution)/shard_map/all_to_all | solution.py:34
  366.3 35.2 %reduce-scatter.2.cloned.1.call-done = bf16[128,1024]{1,0:T(8,128)(2,1)} async-done(((bf16[1024,1024]{1,0:T(8,128)(2,1)}), bf16[128,1024]{1,0:T(8,128)(2,1)}) %reduce-scatter.2.cloned.1.call-update) | async-done | bytes 262160 | tf_op jit(solution)/shard_map/reduce_scatter | solution.py:321
  405.1 12.4 %collective-permute-done.28 = bf16[1,2,128,1024]{3,2,1,0:T(8,128)(2,1)} collective-permute-done((bf16[1,2,128,1024]{3,2,1,0:T(8,128)(2,1)}, bf16[1,2,128,1024]{3,2,1,0:T(8,128)(2,1)}, u32[]{:S(2)}, u32[]{:S(2)}) %collective-permute-start.28) | collective-permute-done | bytes 524320 | tf_op jit(solution)/shard_map/ppermute | solution.py:20
  440.0 7.5 %collective-permute-done.31 = bf16[1,768,256]{2,1,0:T(8,128)(2,1)S(1)} collective-permute-done((bf16[1,768,256]{2,1,0:T(8,128)(2,1)S(1)}, bf16[1,768,256]{2,1,0:T(8,128)(2,1)S(1)}, u32[]{:S(2)}, u32[]{:S(2)}) %collective-permute-start.31) | collective-permute-done | bytes 393248 | tf_op jit(solution)/shard_map/ppermute | solution.py:20
  452.2 7.3 %all-to-all-start.7 = ((f32[32,8,256]{2,1,0:T(8,128)}), f32[32,8,256]{2,1,0:T(8,128)S(1)}, u32[]{:S(2)}, u32[]{:S(2)}) async-start(f32[32,8,256]{2,1,0:T(8,128)} %bitcast.69), calls=%async_computation.8 | async-start | bytes 524288 | tf_op jit(solution)/shard_map/all_to_all | solution.py:34
  471.8 5.4 %collective-permute-done.34 = bf16[4,256,256]{2,1,0:T(8,128)(2,1)} collective-permute-done((bf16[4,256,256]{2,1,0:T(8,128)(2,1)S(1)}, bf16[4,256,256]{2,1,0:T(8,128)(2,1)}, u32[]{:S(2)}, u32[]{:S(2)}) %collective-permute-start.34) | collective-permute-done | bytes 524320 | tf_op jit(solution)/shard_map/ppermute | solution.py:20
  (427 shorter events, 206.1 us)
Async XLA Ops:
  42.0 32.4 %all-to-all-start.2 = ((bf16[4,128,1024]{2,1,0:T(8,128)(2,1)}), bf16[4,128,1024]{2,1,0:T(8,128)(2,1)}, u32[]{:S(2)}, u32[]{:S(2)}) async-start(bf16[4,128,1024]{2,1,0:T(8,128)(2,1)} %broadcast_in_dim.134), calls=%async_computation.2 | async-start | bytes 2097152 | tf_op jit(solution)/shard_map/all_to_all | solution.py:34
  48.0 20.5 %collective-permute-start.5 = (bf16[144,1024]{1,0:T(8,128)(2,1)S(1)}, bf16[144,1024]{1,0:T(8,128)(2,1)S(1)}, u32[]{:S(2)}, u32[]{:S(2)}) collective-permute-start(bf16[144,1024]{1,0:T(8,128)(2,1)S(1)} %collective-permute-done.3), channel_id=1, source_target_pairs={{1,0},{2,1},{5,4},{6,5},{9,8},{10,9},{13,12},{14,13},{17,16},{18,1... | collective-permute-start | bytes 884744 | tf_op jit(solution)/shard_map/ppermute | solution.py:66
  49.2 19.2 %collective-permute-start.6 = (bf16[144,1024]{1,0:T(8,128)(2,1)S(1)}, bf16[144,1024]{1,0:T(8,128)(2,1)S(1)}, u32[]{:S(2)}, u32[]{:S(2)}) collective-permute-start(bf16[144,1024]{1,0:T(8,128)(2,1)S(1)} %collective-permute-done.4), channel_id=1, source_target_pairs={{1,2},{2,3},{5,6},{6,7},{9,10},{10,11},{13,14},{14,15},{17,18},{18... | collective-permute-start | bytes 884744 | tf_op jit(solution)/shard_map/ppermute | solution.py:67
  75.6 39.0 %all-to-all-start.3 = ((bf16[4,128,1024]{2,1,0:T(8,128)(2,1)}), bf16[4,128,1024]{2,1,0:T(8,128)(2,1)S(1)}, u32[]{:S(2)}, u32[]{:S(2)}) async-start(bf16[4,128,1024]{2,1,0:T(8,128)(2,1)} %broadcast_in_dim.135), calls=%async_computation.3 | async-start | bytes 2097152 | tf_op jit(solution)/shard_map/all_to_all | solution.py:34
  84.0 16.5 %collective-permute-start.1 = (bf16[1024,256]{1,0:T(8,128)(2,1)}, bf16[1024,256]{1,0:T(8,128)(2,1)}, u32[]{:S(2)}, u32[]{:S(2)}) collective-permute-start(bf16[1024,256]{1,0:T(8,128)(2,1)} %param.14), channel_id=1, source_target_pairs={{0,4},{4,0},{8,12},{12,8},{1,5},{5,1},{9,13},{13,9},{2,6},{6,2},{1... | collective-permute-start | bytes 1572872 | tf_op jit(solution)/shard_map/ppermute | solution.py:20
  105.4 34.5 %collective-permute-start.11 = (bf16[512,1024]{1,0:T(8,128)(2,1)}, bf16[512,1024]{1,0:T(8,128)(2,1)}, u32[]{:S(2)}, u32[]{:S(2)}) collective-permute-start(bf16[512,1024]{1,0:T(8,128)(2,1)} %bitcast.12), channel_id=1, source_target_pairs={{0,16},{16,0},{1,17},{17,1},{2,18},{18,2},{3,19},{19,3},{4,20},{20... | collective-permute-start | bytes 3145736 | tf_op jit(solution)/shard_map/ppermute | solution.py:20
  107.0 31.1 %collective-permute-start.10 = (bf16[144,1024]{1,0:T(8,128)(2,1)S(1)}, bf16[144,1024]{1,0:T(8,128)(2,1)}, u32[]{:S(2)}, u32[]{:S(2)}) collective-permute-start(bf16[144,1024]{1,0:T(8,128)(2,1)S(1)} %broadcast_select_fusion.6), channel_id=1, source_target_pairs={{0,16},{16,0},{1,17},{17,1},{2,18},{18,2},{3,19},{19,3},{4,20},{20... | collective-permute-start | bytes 884744 | tf_op jit(solution)/shard_map/ppermute | solution.py:20
  116.9 33.3 %collective-permute-start.9 = (bf16[2,144,1024]{2,1,0:T(8,128)(2,1)S(1)}, bf16[2,144,1024]{2,1,0:T(8,128)(2,1)S(1)}, u32[]{:S(2)}, u32[]{:S(2)}) collective-permute-start(bf16[2,144,1024]{2,1,0:T(8,128)(2,1)S(1)} %pad_maximum_fusion.14), channel_id=1, source_target_pairs={{0,16},{16,0},{1,17},{17,1},{2,18},{18,2},{3,19},{19,3},{4,20},{20... | collective-permute-start | bytes 1769480 | tf_op jit(solution)/shard_map/ppermute | solution.py:20
  167.7 14.0 %collective-permute-start.13 = (bf16[256,1024]{1,0:T(8,128)(2,1)S(1)}, bf16[256,1024]{1,0:T(8,128)(2,1)S(1)}, u32[]{:S(2)}, u32[]{:S(2)}) collective-permute-start(bf16[256,1024]{1,0:T(8,128)(2,1)S(1)} %fusion.27), channel_id=1, source_target_pairs={{0,8},{4,12},{8,0},{12,4},{1,9},{5,13},{9,1},{13,5},{2,10},{6,14},... | collective-permute-start | bytes 1572872 | tf_op jit(solution)/shard_map/ppermute | solution.py:20
  172.0 25.5 %collective-permute-start.15 = (bf16[512,1024]{1,0:T(8,128)(2,1)S(1)}, bf16[512,1024]{1,0:T(8,128)(2,1)S(1)}, u32[]{:S(2)}, u32[]{:S(2)}) collective-permute-start(bf16[512,1024]{1,0:T(8,128)(2,1)S(1)} %bitcast.219), channel_id=1, source_target_pairs={{0,16},{16,0},{1,17},{17,1},{2,18},{18,2},{3,19},{19,3},{4,20},{20... | collective-permute-start | bytes 3145736 | tf_op jit(solution)/shard_map/ppermute | solution.py:20
  216.0 17.2 %collective-permute-start.19 = (bf16[256,1024]{1,0:T(8,128)(2,1)}, bf16[256,1024]{1,0:T(8,128)(2,1)}, u32[]{:S(2)}, u32[]{:S(2)}) collective-permute-start(bf16[256,1024]{1,0:T(8,128)(2,1)} %fusion.23), channel_id=1, source_target_pairs={{0,8},{4,12},{8,0},{12,4},{1,9},{5,13},{9,1},{13,5},{2,10},{6,14},... | collective-permute-start | bytes 1572872 | tf_op jit(solution)/shard_map/ppermute | solution.py:20
  238.5 13.5 %collective-permute-start.21 = (bf16[256,1024]{1,0:T(8,128)(2,1)S(1)}, bf16[256,1024]{1,0:T(8,128)(2,1)S(1)}, u32[]{:S(2)}, u32[]{:S(2)}) collective-permute-start(bf16[256,1024]{1,0:T(8,128)(2,1)S(1)} %get-tuple-element.133), channel_id=1, source_target_pairs={{0,8},{4,12},{8,0},{12,4},{1,9},{5,13},{9,1},{13,5},{2,10},{6,14},... | collective-permute-start | bytes 1572872 | tf_op jit(solution)/shard_map/ppermute | solution.py:20
  270.2 16.5 %collective-permute-start.24 = (bf16[256,1024]{1,0:T(8,128)(2,1)S(1)}, bf16[256,1024]{1,0:T(8,128)(2,1)}, u32[]{:S(2)}, u32[]{:S(2)}) collective-permute-start(bf16[256,1024]{1,0:T(8,128)(2,1)S(1)} %fusion.20), channel_id=1, source_target_pairs={{0,8},{4,12},{8,0},{12,4},{1,9},{5,13},{9,1},{13,5},{2,10},{6,14},... | collective-permute-start | bytes 1572872 | tf_op jit(solution)/shard_map/ppermute | solution.py:20
  274.3 73.4 %all-to-all-start.5 = ((bf16[8,128,1024]{2,1,0:T(8,128)(2,1)}), bf16[8,128,1024]{2,1,0:T(8,128)(2,1)}, u32[]{:S(2)}, u32[]{:S(2)}) async-start(bf16[8,128,1024]{2,1,0:T(8,128)(2,1)} %bitcast.212), calls=%async_computation.5 | async-start | bytes 4194304 | tf_op jit(solution)/shard_map/all_to_all | solution.py:34
  280.9 120.6 %reduce-scatter.2.cloned.1.call-start = ((), (), s32[]{:S(2)}) async-start(), calls=%async_computation.9 | async-start | bytes 2359296 | tf_op jit(solution)/shard_map/reduce_scatter | solution.py:321
  291.8 14.1 %collective-permute-start.25 = (bf16[256,1024]{1,0:T(8,128)(2,1)S(1)}, bf16[256,1024]{1,0:T(8,128)(2,1)S(1)}, u32[]{:S(2)}, u32[]{:S(2)}) collective-permute-start(bf16[256,1024]{1,0:T(8,128)(2,1)S(1)} %get-tuple-element.136), channel_id=1, source_target_pairs={{0,8},{4,12},{8,0},{12,4},{1,9},{5,13},{9,1},{13,5},{2,10},{6,14},... | collective-permute-start | bytes 1572872 | tf_op jit(solution)/shard_map/ppermute | solution.py:20
  292.5 13.4 %collective-permute-start.26 = (bf16[256,1024]{1,0:T(8,128)(2,1)S(1)}, bf16[256,1024]{1,0:T(8,128)(2,1)S(1)}, u32[]{:S(2)}, u32[]{:S(2)}) collective-permute-start(bf16[256,1024]{1,0:T(8,128)(2,1)S(1)} %get-tuple-element.136), channel_id=1, source_target_pairs={{0,4},{4,0},{8,12},{12,8},{1,5},{5,1},{9,13},{13,9},{2,6},{6,2},{1... | collective-permute-start | bytes 1572872 | tf_op jit(solution)/shard_map/ppermute | solution.py:20
  353.3 98.1 %all-to-all-start.6 = ((bf16[16,256,256]{2,1,0:T(8,128)(2,1)}), bf16[16,256,256]{2,1,0:T(8,128)(2,1)}, u32[]{:S(2)}, u32[]{:S(2)}) async-start(bf16[16,256,256]{2,1,0:T(8,128)(2,1)} %bitcast.211), calls=%async_computation.7 | async-start | bytes 4194304 | tf_op jit(solution)/shard_map/all_to_all | solution.py:34
  363.9 67.1 %collective-permute-start.32 = (bf16[1024,512]{1,0:T(8,128)(2,1)}, bf16[1024,512]{1,0:T(8,128)(2,1)}, u32[]{:S(2)}, u32[]{:S(2)}) collective-permute-start(bf16[1024,512]{1,0:T(8,128)(2,1)} %fusion.14), channel_id=1, source_target_pairs={{0,4},{4,0},{8,12},{12,8},{1,5},{5,1},{9,13},{13,9},{2,6},{6,2},{1... | collective-permute-start | bytes 3145736 | tf_op jit(solution)/shard_map/ppermute | solution.py:20
  403.3 14.3 %collective-permute-start.28 = (bf16[1,2,128,1024]{3,2,1,0:T(8,128)(2,1)}, bf16[1,2,128,1024]{3,2,1,0:T(8,128)(2,1)}, u32[]{:S(2)}, u32[]{:S(2)}) collective-permute-start(bf16[1,2,128,1024]{3,2,1,0:T(8,128)(2,1)} %maximum_bitcast_fusion.1), channel_id=1, source_target_pairs={{0,16},{16,0},{1,17},{17,1},{2,18},{18,2},{3,19},{19,3},{4,20},{20... | collective-permute-start | bytes 1572872 | tf_op jit(solution)/shard_map/ppermute | solution.py:20
  429.6 17.9 %collective-permute-start.31 = (bf16[1,768,256]{2,1,0:T(8,128)(2,1)S(1)}, bf16[1,768,256]{2,1,0:T(8,128)(2,1)S(1)}, u32[]{:S(2)}, u32[]{:S(2)}) collective-permute-start(bf16[1,768,256]{2,1,0:T(8,128)(2,1)S(1)} %bitcast.252), channel_id=1, source_target_pairs={{0,12},{4,8},{8,4},{12,0},{1,13},{5,9},{9,5},{13,1},{2,14},{6,10},... | collective-permute-start | bytes 1179656 | tf_op jit(solution)/shard_map/ppermute | solution.py:20
  434.3 28.9 %collective-permute-start.33 = (bf16[1024,256]{1,0:T(8,128)(2,1)}, bf16[1024,256]{1,0:T(8,128)(2,1)S(1)}, u32[]{:S(2)}, u32[]{:S(2)}) collective-permute-start(bf16[1024,256]{1,0:T(8,128)(2,1)} %fusion.18), channel_id=1, source_target_pairs={{0,8},{4,12},{8,0},{12,4},{1,9},{5,13},{9,1},{13,5},{2,10},{6,14},... | collective-permute-start | bytes 1572872 | tf_op jit(solution)/shard_map/ppermute | solution.py:20
  452.2 17.5 %all-to-all-start.7 = ((f32[32,8,256]{2,1,0:T(8,128)}), f32[32,8,256]{2,1,0:T(8,128)S(1)}, u32[]{:S(2)}, u32[]{:S(2)}) async-start(f32[32,8,256]{2,1,0:T(8,128)} %bitcast.69), calls=%async_computation.8 | async-start | bytes 524288 | tf_op jit(solution)/shard_map/all_to_all | solution.py:34
  461.4 15.8 %collective-permute-start.34 = (bf16[4,256,256]{2,1,0:T(8,128)(2,1)S(1)}, bf16[4,256,256]{2,1,0:T(8,128)(2,1)}, u32[]{:S(2)}, u32[]{:S(2)}) collective-permute-start(bf16[4,256,256]{2,1,0:T(8,128)(2,1)S(1)} %bitcast_reduce_fusion), channel_id=1, source_target_pairs={{0,16},{16,0},{1,17},{17,1},{2,18},{18,2},{3,19},{19,3},{4,20},{20... | collective-permute-start | bytes 1572872 | tf_op jit(solution)/shard_map/ppermute | solution.py:20
  (102 other events, 688.3 us)
Sparse Core Ops, SparseCore 0:
  286.8 114.6 reduce-scatter.1

commit v2 on v1

--- a/solution.py
+++ b/solution.py
@@ -209,7 +209,7 @@
     hid_bias = lax.dynamic_slice(bias_in, (r * hid_piece,), (hid_piece,))
     head_bias = lax.dynamic_slice(bias_qv, (0, r * head_piece), (2, head_piece)).reshape(-1)
     bias_row = jnp.concatenate([hid_bias, head_bias])
-    bias_rows = jnp.pad(bias_row[None], ((0, 31), (0, width - bias_row.shape[0])))
+    bias_rows = jnp.pad(bias_row[None], ((0, 15), (0, width - bias_row.shape[0])))
 
     wi = jnp.transpose(w_in).reshape(rows, hid_piece, width_local)
     wi = lax.dynamic_slice_in_dim(wi, n * half, half, 1)
@@ -231,24 +231,13 @@
         return jnp.concatenate([jnp.where(n == 0, mine, other), jnp.where(n == 0, other, mine)], 0)
 
     begin = jnp.concatenate([first, bias_rows], 0)
-    line_half = begin.shape[0] // 2
-    mine = lax.dynamic_slice_in_dim(begin, n * line_half, line_half, 0)
-    steps = [(mine, mine)]
-    steps.append(line_step(mine, mine, 1))
-    steps[1], wi = lax.optimization_barrier((steps[1], wi))
+    steps = [(begin, begin)]
+    steps.append(line_step(begin, begin, 1))
+    steps[1], _ = lax.optimization_barrier((steps[1], wi))
+    wi = spread(wi, "col").reshape(hid_half, width)
     steps.append(line_step(*steps[1], 2))
-    wi = spread(wi, "col").reshape(hid_half, width)
-    steps[2], wi = lax.optimization_barrier((steps[2], wi))
     steps.append(line_step(*steps[2], 3))
-    wb = spread(after(wb, wi), "col").reshape(hid_half, width)
-    steps[3], wb = lax.optimization_barrier((steps[3], wb))
-    ours = line_blocks(steps)
-    middle = swap(ours[1], "dp", 1)
-    ends = swap(jnp.stack([ours[0], ours[2]]), "dp", 1)
-    line = [begin]
-    for our, their in zip(ours, [ends[0], middle, ends[1]]):
-        both = [jnp.where(n == 0, our, their), jnp.where(n == 0, their, our)]
-        line.append(jnp.concatenate(both, 0))
+    line = [begin] + line_blocks(steps)
     wq_all = in_col_order([b[:heads_rows] for b in line]).reshape(3 * heads_width, width)
     bias_at = heads_rows + head_piece
     wo_all = in_col_order([b[heads_rows:bias_at] for b in line]).reshape(heads_width, width)
@@ -263,6 +252,8 @@
     diagonal = swap(across, "row", 1)
     tokens_all = jnp.concatenate([tokens, across, beside, diagonal], 1)
 
+    wb = spread(after(wb, line[-1]), "col").reshape(hid_half, width)
+    tokens_all, wi = lax.optimization_barrier((tokens_all, wi))
     wi_all = both_halves(wi)
     cot = after(cotangent, wb).reshape(rows, block, width_local)
     cot = jnp.transpose(trade(cot, "row"), (1, 0, 2)).reshape(block, width).astype(f32)
@@ -313,31 +304,50 @@
     grad_wb = sum(dot(a, b, 0, 0) for a, b in zip(activated, d_mlp)).astype(bf16)
     d_hidden = d_two + reduce_chips(*d_hid)
     d_hidden, _ = lax.optimization_barrier((d_hidden, grad_wb))
+
+    def row_trade(values):
+        sent = [lax.dynamic_slice_in_dim(values, r ^ j, 1, 0) for j in range(rows)]
+        got = jnp.concatenate([sent[0]] + [swap(sent[j], "row", j) for j in range(1, rows)], 0)
+        return jnp.concatenate(
+            [lax.dynamic_slice_in_dim(got, r ^ a, 1, 0) for a in range(rows)], 0
+        )
+
+    output = jnp.transpose(output.reshape(block, rows, width_local), (1, 0, 2))
+    output = row_trade(output).reshape(group, width_local)
     grad_wi = sum(dot(a, b, 0, 0) for a, b in zip(d_pre, hidden)).astype(bf16)
-    grad_wi_ready, hid_grads_gate = grad_wi, None
-    if dp_size == 2:
-        grad_wb = trade(grad_wb.reshape(2 * cols, half, width), ("dp", "col"))
-        hid_grads_gate = grad_wb
-        grad_wi = lax.psum_scatter(grad_wi, ("dp", "col"), scatter_dimension=0, tiled=True)
+    grad_wi_ready = grad_wi
+
+    def half_of(grad, k):
+        return lax.dynamic_slice_in_dim(grad, k * hid_half, hid_half, 0)
+
+    wb_other = swap(half_of(grad_wb, 1 - n), "dp", 1)
+    wi_other = swap(half_of(grad_wi, 1 - n), "dp", 1)
 
     d_one = norm_backward(d_hidden, normed_one, inv_one, gain_one_f)
     d_att = d_one.astype(bf16)
     over = swap(d_att, "row", 2)
     over, _ = lax.optimization_barrier((over, grad_wi_ready))
     d_att_all = jnp.concatenate([d_att, over, swap(d_att, "row", 1), swap(over, "row", 1)], 0)
+    d_att_all, wb_other = lax.optimization_barrier((d_att_all, wb_other))
 
     def by_owner(values):
         each = values.shape[2]
-        raw = trade(values.reshape(-1, each, width_local), ("row", "col"))
-        got = jnp.sum(raw.reshape(rows, cols, each, width_local).astype(f32), 1)
-        return dp_sum(got, 1), raw
+        got = trade(values.reshape(-1, each, width_local), ("row", "col"))
+        got = jnp.sum(got.reshape(rows, cols, each, width_local).astype(f32), 1)
+        return dp_sum(got, 1)
 
     grad_wo = dot(context, d_att_all, 0, 0).astype(bf16).reshape(cols, head_piece, rows, width_local)
     grad_wo = jnp.transpose(grad_wo, (2, 0, 1, 3))
 
     d_context = from_rel(dot(d_att_all, wo_all, 1, 1).astype(bf16), 0)
     d_joined = by_sequence(attend_back_kernel, [joined, d_context], 3 * heads_width, 10)
-    d_joined, _ = lax.optimization_barrier((d_joined, hid_grads_gate))
+    d_joined, wi_other = lax.optimization_barrier((d_joined, wi_other))
+    hid_grads = [
+        (half_of(grad, n).astype(f32) + other.astype(f32)).astype(bf16).reshape(cols, half, width)
+        for grad, other in ((grad_wb, wb_other), (grad_wi, wi_other))
+    ]
+    hid_grads = jnp.concatenate(hid_grads, 1).reshape(-1, width)
+    hid_grads = lax.psum_scatter(hid_grads, "col", scatter_dimension=0, tiled=True)
     grad_wq = []
     for a in range(rows):
         j = r ^ a
@@ -346,7 +356,7 @@
         grad_wq.append(dot(d_joined, owned, 0, 0).astype(bf16).reshape(cols, heads_rows, -1))
     grad_wq = jnp.concatenate([jnp.stack(grad_wq), grad_wo], 2)
     d_joined_late = after(d_joined, grad_wq)
-    grad_wq, arrived = by_owner(grad_wq)
+    grad_wq = by_owner(grad_wq)
     grad_w_out = grad_wq[:, heads_rows:].reshape(heads_tile, width_local)
     grad_wq = grad_wq[:, :heads_rows].reshape(rows, 3, head_piece, width_local)
     grad_w_qkv = jnp.transpose(grad_wq, (1, 3, 0, 2)).reshape(3, width_local, heads_tile)
@@ -379,52 +389,40 @@
             jnp.sum(cot, 0),
         ]
     )
-    vector_grads = jnp.transpose(vector_grads.reshape(6, rows, width_local), (1, 0, 2))
     hid_sums = sum(jnp.sum(d, 0, dtype=f32) for d in d_pre).reshape(2, cols, half)
-    hid_sums = jnp.transpose(hid_sums, (1, 0, 2)).reshape(1, cols, 1, hid_piece)
-    head_sums = jnp.sum(d_joined, 0, dtype=f32).reshape(cols, 3, head_piece)
-    head_sums = jnp.concatenate([head_sums[:, 0], head_sums[:, 2]], 1)
-    head_sums = jnp.pad(head_sums, ((0, 0), (0, width_local - 2 * head_piece)))
-    col_sums = jnp.concatenate([hid_sums, head_sums[None, :, None]], 2)
-    small = jnp.concatenate(
-        [
-            jnp.broadcast_to(vector_grads[:, None], (rows, cols, 6, width_local)),
-            jnp.broadcast_to(col_sums, (rows, cols, 2, width_local)),
-        ],
-        2,
-    )
-    small = jnp.broadcast_to(small[None], (dp_size,) + small.shape)
-    small = after(small, arrived)
-    small = trade(small.reshape(-1, 8, width_local), ("dp", "row", "col"))
-    small = small.reshape(dp_size, rows, cols, 8, width_local)
-    vector_grads = jnp.sum(small[:, :, :, :6], (0, 1, 2))
-    grad_bias_in = jnp.sum(small[:, :, :, 6], (0, 2)).reshape(hid_tile)
-    head_sums = jnp.sum(small[:, :, :, 7, : 2 * head_piece], (0, 2)).reshape(rows, 2, head_piece)
+    hid_sums = jnp.transpose(hid_sums, (1, 0, 2)).reshape(cols, hid_piece)
+    head_sums = jnp.sum(d_joined, 0, dtype=f32).reshape(cols, 3 * head_piece)
+    col_sums = jnp.concatenate(
+        [hid_sums, head_sums[:, :head_piece], head_sums[:, 2 * head_piece :]], 1
+    )
+    col_sums = jnp.where((jnp.arange(rows) == r)[None, :, None], col_sums[:, None], 0.0)
+    small = jnp.concatenate([vector_grads, col_sums.reshape(-1, width)], 0)
+    for axis in ("row", "col", "dp"):
+        bit = 1
+        while bit < lax.axis_size(axis):
+            small = small + swap(small, axis, bit)
+            bit *= 2
+    vector_grads = lax.dynamic_slice_in_dim(small[:6], r * width_local, width_local, 1)
+    col_sums = small[6:].reshape(cols, rows, hid_piece + 2 * head_piece)
+    col_sums = lax.dynamic_slice_in_dim(col_sums, lax.axis_index("col"), 1, 0)[0]
+    grad_bias_in = col_sums[:, :hid_piece].reshape(hid_tile)
+    head_sums = col_sums[:, hid_piece:].reshape(rows, 2, head_piece)
     grad_bias_qv = jnp.transpose(head_sums, (1, 0, 2)).reshape(2, heads_tile)
 
+    hid_grads = dp_sum(after(hid_grads, send), 2).astype(bf16)
     if dp_size == 2:
-        grad_wb = jnp.sum(grad_wb.astype(f32), 0).astype(bf16)
-        grad_wi = after(grad_wi, send)
-        hid_grads = both_halves(jnp.stack([grad_wb, grad_wi])[None])
+        hid_grads = jnp.transpose(hid_grads.reshape(2 * half, rows, width_local), (1, 0, 2))
+        hid_grads = jnp.broadcast_to(hid_grads[None], (2,) + hid_grads.shape)
+        hid_grads = trade(hid_grads.reshape(2 * rows, 2 * half, width_local), ("dp", "row"))
+        hid_grads = hid_grads.reshape(2, rows, 2, half, width_local)
     else:
-        hid_grads = jnp.stack([grad_wb, grad_wi]).reshape(2, 2, cols, half, width)
-        hid_grads = jnp.transpose(hid_grads, (2, 1, 0, 3, 4)).reshape(-1, width)
-        hid_grads = lax.psum_scatter(hid_grads, "col", scatter_dimension=0, tiled=True)
-        hid_grads = lax.psum(hid_grads.astype(f32), "dp").astype(bf16).reshape(2, 2, half, width)
-    hid_grads = jnp.transpose(hid_grads, (1, 0, 2, 3)).reshape(2 * hid_piece, width)
-    hid_grads = jnp.concatenate([hid_grads, output], 0).reshape(-1, rows, width_local)
-    hid_grads = jnp.transpose(hid_grads, (1, 0, 2))
-    pieces = [lax.dynamic_slice_in_dim(hid_grads, r ^ j, 1, 0) for j in range(rows)]
-    pieces = jnp.concatenate(
-        [pieces[0]] + [swap(pieces[j], "row", j) for j in range(1, rows)], 0
-    )
-    hid_grads = jnp.concatenate(
-        [lax.dynamic_slice_in_dim(pieces, r ^ a, 1, 0) for a in range(rows)], 0
-    )
-    output = hid_grads[:, 2 * hid_piece :].reshape(group, width_local)
-    grad_w_back = hid_grads[:, :hid_piece].reshape(hid_tile, width_local).astype(f32)
-    grad_w_in = hid_grads[:, hid_piece : 2 * hid_piece].reshape(hid_tile, width_local)
-    grad_w_in = jnp.transpose(grad_w_in).astype(f32)
+        hid_grads = both_halves(hid_grads.reshape(1, 2 * half, width))
+        hid_grads = jnp.transpose(hid_grads.reshape(4 * half, rows, width_local), (1, 0, 2))
+        hid_grads = trade(hid_grads, "row").reshape(rows, 2, 2, half, width_local)
+        hid_grads = jnp.transpose(hid_grads, (1, 0, 2, 3, 4))
+    hid_grads = jnp.transpose(hid_grads, (2, 1, 0, 3, 4)).reshape(2, hid_tile, width_local)
+    grad_w_back = hid_grads[0].astype(f32)
+    grad_w_in = jnp.transpose(hid_grads[1]).astype(f32)
 
     return (
         output,

time: 494 us -> 457 us (0.925)
  waiting for transfers between devices: 241 us -> 215 us
  local copies, waits for them, and re-layouts: 47.1 us -> 37.7 us
  starting transfers between devices: 75.9 us -> 69.5 us
  other arithmetic: 49.4 us -> 54.8 us
    reduce_scatter x1, waiting for transfers between devices: 35.2 us -> 0.01 us  [per_device(): lax.psum_scatter(hid_grads, 'col', scatter_dimension=0, tiled=True)]
    ppermute x29 -> x33, waiting for transfers between devices: 128 us -> 155 us  [swap(): return lax.ppermute(values, axis, [(i, i ^ bit) for i in range(size)])]
    all_to_all x8 -> x7, waiting for transfers between devices: 48.8 us -> 26.2 us  [trade(): return lax.all_to_all(values, axis, 0, 0, tiled=True)]
    all_to_all x8 -> x7, starting transfers between devices: 43.1 us -> 29.5 us  [trade(): return lax.all_to_all(values, axis, 0, 0, tiled=True)]
    concatenate x3 -> x6, other arithmetic: 0.43 us -> 8.11 us  [the longest x1 2.97 us: per_device(): tokens_all = jnp.concatenate([tokens, across, beside, diagonal], 1)]
    unnamed x180 -> x176, local copies, waits for them, and re-layouts: 20.7 us -> 14 us
    ppermute x29 -> x33, starting transfers between devices: 21.8 us -> 27.5 us  [swap(): return lax.ppermute(values, axis, [(i, i ^ bit) for i in range(size)])]
    dynamic_update_slice x8 -> x11, local copies, waits for them, and re-layouts: 0.67 us -> 5.64 us  [in_col_order(): out = lax.dynamic_update_slice_in_dim(out, b[None], place, 0)]
  transfers between devices with their start and end apart: 44 -> 47, of which waited for: 26 -> 28; matrix products, arithmetic and copies ran while one was open for 19% -> 19% of each run, Pallas kernels for 2% -> 4%
where the time goes in v2:
time: 457 us; the launch traced here: 451 us
  waiting for transfers between devices  215 us (47%)
  starting transfers between devices  69.5 us (15%)
  other arithmetic  54.8 us (12%)
  matrix products  42.7 us (9%)
  local copies, waits for them, and re-layouts  37.7 us (8%)
  between operations  16 us (4%)
  Pallas kernels  15.9 us (3%)
    ppermute x33, waiting for transfers between devices, swap(): return lax.ppermute(values, axis, [(i, i ^ bit) for i in range(size)])  155 us
    dot_general x23, matrix products, dot(): lax.dot_general(left, right, (((left_dim,), (right_dim,)), ((), ())), pre...  42.7 us
    ppermute x3, waiting for transfers between devices, line_step(): lax.ppermute(up, 'col', [(i, i - 1) for i in range(1, size - step + 1)])  31.8 us
    all_to_all x7, starting transfers between devices, trade(): return lax.all_to_all(values, axis, 0, 0, tiled=True)  29.5 us
    ppermute x33, starting transfers between devices, swap(): return lax.ppermute(values, axis, [(i, i ^ bit) for i in range(size)])  27.5 us
    all_to_all x7, waiting for transfers between devices, trade(): return lax.all_to_all(values, axis, 0, 0, tiled=True)  26.2 us
    pallas_call x2, Pallas kernels, by_sequence(): pl.pallas_call(kernel, grid=(tokens // SEQ_LEN,), in_specs=[pl.BlockSpec(...  15.9 us
    unnamed x176, local copies, waits for them, and re-layouts  14 us
  transfers between devices with their start and end apart: 47, of which 28 were waited for; matrix products, arithmetic and copies ran while one was open for 19% of the time, Pallas kernels for 4%

profile of v2, /device:TPU:0, one launch (start us, length us, event | category | flops | bytes accessed | tf_op | source)
XLA Modules:
  0.0 451.4 jit_solution(12827263848270566174)
XLA Ops:
  16.8 6.6 %all-to-all-done.2 = bf16[4,256,256]{2,1,0:T(8,128)(2,1)S(1)} async-done(((bf16[4,256,256]{2,1,0:T(8,128)(2,1)}), bf16[4,256,256]{2,1,0:T(8,128)(2,1)S(1)}, u32[]{:S(2)}, u32[]{:S(2)}) %all-to-all-start.2) | async-done | bytes 524320 | tf_op jit(solution)/shard_map/all_to_all | solution.py:34
  28.5 5.6 %collective-permute-start.4 = (bf16[272,1024]{1,0:T(8,128)(2,1)S(1)}, bf16[272,1024]{1,0:T(8,128)(2,1)}, u32[]{:S(2)}, u32[]{:S(2)}) collective-permute-start(bf16[272,1024]{1,0:T(8,128)(2,1)S(1)} %fusion.38), channel_id=1, source_target_pairs={{0,1},{1,2},{2,3},{4,5},{5,6},{6,7},{8,9},{9,10},{10,11},{12,13},{... | collective-permute-start | bytes 1671176 | tf_op jit(solution)/shard_map/ppermute | solution.py:67
  37.6 5.5 %all-to-all-start.1 = ((bf16[4,128,1024]{2,1,0:T(8,128)(2,1)}), bf16[4,128,1024]{2,1,0:T(8,128)(2,1)}, u32[]{:S(2)}, u32[]{:S(2)}) async-start(bf16[4,128,1024]{2,1,0:T(8,128)(2,1)} %broadcast_in_dim.137), calls=%async_computation.1 | async-start | bytes 2097152 | tf_op jit(solution)/shard_map/all_to_all | solution.py:34
  49.0 7.5 %collective-permute-done = bf16[1024,256]{1,0:T(8,128)(2,1)S(1)} collective-permute-done((bf16[1024,256]{1,0:T(8,128)(2,1)}, bf16[1024,256]{1,0:T(8,128)(2,1)S(1)}, u32[]{:S(2)}, u32[]{:S(2)}) %collective-permute-start) | collective-permute-done | bytes 524320 | tf_op jit(solution)/shard_map/ppermute | solution.py:20
  60.3 13.9 %collective-permute-done.7 = bf16[272,1024]{1,0:T(8,128)(2,1)} collective-permute-done((bf16[272,1024]{1,0:T(8,128)(2,1)}, bf16[272,1024]{1,0:T(8,128)(2,1)}, u32[]{:S(2)}, u32[]{:S(2)}) %collective-permute-start.7) | collective-permute-done | bytes 557088 | tf_op jit(solution)/shard_map/ppermute | solution.py:66
  82.3 16.7 %collective-permute-done.8 = bf16[272,1024]{1,0:T(8,128)(2,1)} collective-permute-done((bf16[272,1024]{1,0:T(8,128)(2,1)}, bf16[272,1024]{1,0:T(8,128)(2,1)}, u32[]{:S(2)}, u32[]{:S(2)}) %collective-permute-start.8) | collective-permute-done | bytes 557088 | tf_op jit(solution)/shard_map/ppermute | solution.py:66
  102.5 4.5 all-to-all-start.3
  110.5 6.5 %shard_map.245 = bf16[1024,256]{1,0:T(8,128)(2,1)S(1)} custom-call(bf16[1024,768]{1,0:T(8,128)(2,1)S(1)} %add_convert_fusion.2.qkv_ref), custom_call_target="tpu_custom_call" | custom-call | flops 536870912 | bytes 2097152 | tf_op jit(solution)/shard_map/pallas_call | solution.py:157
  124.8 7.1 %all-to-all-done.3 = bf16[4,128,1024]{2,1,0:T(8,128)(2,1)} async-done(((bf16[4,128,1024]{2,1,0:T(8,128)(2,1)}), bf16[4,128,1024]{2,1,0:T(8,128)(2,1)}, u32[]{:S(2)}, u32[]{:S(2)}) %all-to-all-start.3) | async-done | bytes 1048608 | tf_op jit(solution)/shard_map/all_to_all | solution.py:34
  143.1 8.5 %collective-permute-done.11 = bf16[256,1024]{1,0:T(8,128)(2,1)S(1)} collective-permute-done((bf16[256,1024]{1,0:T(8,128)(2,1)S(1)}, bf16[256,1024]{1,0:T(8,128)(2,1)S(1)}, u32[]{:S(2)}, u32[]{:S(2)}) %collective-permute-start.11) | collective-permute-done | bytes 524320 | tf_op jit(solution)/shard_map/ppermute | solution.py:20
  155.2 12.2 %collective-permute-done.14 = bf16[256,1024]{1,0:T(8,128)(2,1)S(1)} collective-permute-done((bf16[256,1024]{1,0:T(8,128)(2,1)S(1)}, bf16[256,1024]{1,0:T(8,128)(2,1)S(1)}, u32[]{:S(2)}, u32[]{:S(2)}) %collective-permute-start.14) | collective-permute-done | bytes 524320 | tf_op jit(solution)/shard_map/ppermute | solution.py:20
  187.9 4.4 all-to-all-done.4
  193.8 9.4 %collective-permute-done.17 = bf16[256,1024]{1,0:T(8,128)(2,1)} collective-permute-done((bf16[256,1024]{1,0:T(8,128)(2,1)}, bf16[256,1024]{1,0:T(8,128)(2,1)}, u32[]{:S(2)}, u32[]{:S(2)}) %collective-permute-start.17) | collective-permute-done | bytes 524320 | tf_op jit(solution)/shard_map/ppermute | solution.py:20
  208.3 13.1 %collective-permute-done.22 = bf16[256,1024]{1,0:T(8,128)(2,1)S(1)} collective-permute-done((bf16[256,1024]{1,0:T(8,128)(2,1)S(1)}, bf16[256,1024]{1,0:T(8,128)(2,1)S(1)}, u32[]{:S(2)}, u32[]{:S(2)}) %collective-permute-start.22) | collective-permute-done | bytes 524320 | tf_op jit(solution)/shard_map/ppermute | solution.py:20
  243.0 10.6 %collective-permute-done.25 = bf16[256,1024]{1,0:T(8,128)(2,1)S(1)} collective-permute-done((bf16[256,1024]{1,0:T(8,128)(2,1)S(1)}, bf16[256,1024]{1,0:T(8,128)(2,1)S(1)}, u32[]{:S(2)}, u32[]{:S(2)}) %collective-permute-start.25) | collective-permute-done | bytes 524320 | tf_op jit(solution)/shard_map/ppermute | solution.py:20
  261.6 9.5 %collective-permute-done.26 = bf16[256,1024]{1,0:T(8,128)(2,1)} collective-permute-done((bf16[256,1024]{1,0:T(8,128)(2,1)S(1)}, bf16[256,1024]{1,0:T(8,128)(2,1)}, u32[]{:S(2)}, u32[]{:S(2)}) %collective-permute-start.26) | collective-permute-done | bytes 524320 | tf_op jit(solution)/shard_map/ppermute | solution.py:20
  275.3 9.6 %collective-permute-done.29 = bf16[512,1024]{1,0:T(8,128)(2,1)} collective-permute-done((bf16[512,1024]{1,0:T(8,128)(2,1)S(1)}, bf16[512,1024]{1,0:T(8,128)(2,1)}, u32[]{:S(2)}, u32[]{:S(2)}) %collective-permute-start.29) | collective-permute-done | bytes 1048608 | tf_op jit(solution)/shard_map/ppermute | solution.py:20
  286.8 9.4 %shard_map.246 = bf16[1024,768]{1,0:T(8,128)(2,1)S(1)} custom-call(bf16[1024,768]{1,0:T(8,128)(2,1)S(1)} %add_convert_fusion.2.qkv_ref, bf16[1024,256]{1,0:T(8,128)(2,1)S(1)} %pad_maximum_fusion.18.d_context_ref), custom_call_target="tpu_custom_call" | custom-call | flops 1342177280 | bytes 3670016 | tf_op jit(solution)/shard_map/pallas_call | solution.py:157
  296.2 9.1 %collective-permute-done.30 = bf16[512,1024]{1,0:T(8,128)(2,1)} collective-permute-done((bf16[512,1024]{1,0:T(8,128)(2,1)}, bf16[512,1024]{1,0:T(8,128)(2,1)}, u32[]{:S(2)}, u32[]{:S(2)}) %collective-permute-start.30) | collective-permute-done | bytes 1048608 | tf_op jit(solution)/shard_map/ppermute | solution.py:20
  320.3 4.8 %all-to-all-start.5 = ((bf16[16,256,256]{2,1,0:T(8,128)(2,1)}), bf16[16,256,256]{2,1,0:T(8,128)(2,1)}, u32[]{:S(2)}, u32[]{:S(2)}) async-start(bf16[16,256,256]{2,1,0:T(8,128)(2,1)} %bitcast.192), calls=%async_computation.5 | async-start | bytes 4194304 | tf_op jit(solution)/shard_map/all_to_all | solution.py:34
  346.6 43.9 %collective-permute-done.36 = f32[12,1024]{1,0:T(8,128)S(1)} collective-permute-done((f32[12,1024]{1,0:T(8,128)S(1)}, f32[12,1024]{1,0:T(8,128)S(1)}, u32[]{:S(2)}, u32[]{:S(2)}) %collective-permute-start.36) | collective-permute-done | bytes 49184 | tf_op jit(solution)/shard_map/ppermute | solution.py:20
  390.5 4.7 %collective-permute-start.37 = (f32[12,1024]{1,0:T(8,128)S(1)}, f32[12,1024]{1,0:T(8,128)S(1)}, u32[]{:S(2)}, u32[]{:S(2)}) collective-permute-start(f32[12,1024]{1,0:T(8,128)S(1)} %add.409), channel_id=1, source_target_pairs={{0,2},{1,3},{2,0},{3,1},{4,6},{5,7},{6,4},{7,5},{8,10},{9,11},{10,... | collective-permute-start | bytes 147464 | tf_op jit(solution)/shard_map/ppermute | solution.py:20
  396.0 10.1 %collective-permute-done.37 = f32[12,1024]{1,0:T(8,128)S(1)} collective-permute-done((f32[12,1024]{1,0:T(8,128)S(1)}, f32[12,1024]{1,0:T(8,128)S(1)}, u32[]{:S(2)}, u32[]{:S(2)}) %collective-permute-start.37) | collective-permute-done | bytes 49184 | tf_op jit(solution)/shard_map/ppermute | solution.py:20
  435.6 6.0 %all-to-all-done.6 = bf16[8,256,256]{2,1,0:T(8,128)(2,1)S(1)} async-done(((bf16[8,256,256]{2,1,0:T(8,128)(2,1)}), bf16[8,256,256]{2,1,0:T(8,128)(2,1)S(1)}, u32[]{:S(2)}, u32[]{:S(2)}) %all-to-all-start.6) | async-done | bytes 1048608 | tf_op jit(solution)/shard_map/all_to_all | solution.py:34
  (425 shorter events, 196.2 us)
Async XLA Ops:
  27.2 17.5 %collective-permute-start.3 = (bf16[272,1024]{1,0:T(8,128)(2,1)S(1)}, bf16[272,1024]{1,0:T(8,128)(2,1)}, u32[]{:S(2)}, u32[]{:S(2)}) collective-permute-start(bf16[272,1024]{1,0:T(8,128)(2,1)S(1)} %fusion.38), channel_id=1, source_target_pairs={{1,0},{2,1},{3,2},{5,4},{6,5},{7,6},{9,8},{10,9},{11,10},{13,12},{... | collective-permute-start | bytes 1671176 | tf_op jit(solution)/shard_map/ppermute | solution.py:66
  28.5 17.7 %collective-permute-start.4 = (bf16[272,1024]{1,0:T(8,128)(2,1)S(1)}, bf16[272,1024]{1,0:T(8,128)(2,1)}, u32[]{:S(2)}, u32[]{:S(2)}) collective-permute-start(bf16[272,1024]{1,0:T(8,128)(2,1)S(1)} %fusion.38), channel_id=1, source_target_pairs={{0,1},{1,2},{2,3},{4,5},{5,6},{6,7},{8,9},{9,10},{10,11},{12,13},{... | collective-permute-start | bytes 1671176 | tf_op jit(solution)/shard_map/ppermute | solution.py:67
  37.6 42.0 %all-to-all-start.1 = ((bf16[4,128,1024]{2,1,0:T(8,128)(2,1)}), bf16[4,128,1024]{2,1,0:T(8,128)(2,1)}, u32[]{:S(2)}, u32[]{:S(2)}) async-start(bf16[4,128,1024]{2,1,0:T(8,128)(2,1)} %broadcast_in_dim.137), calls=%async_computation.1 | async-start | bytes 2097152 | tf_op jit(solution)/shard_map/all_to_all | solution.py:34
  47.6 26.5 %collective-permute-start.7 = (bf16[272,1024]{1,0:T(8,128)(2,1)}, bf16[272,1024]{1,0:T(8,128)(2,1)}, u32[]{:S(2)}, u32[]{:S(2)}) collective-permute-start(bf16[272,1024]{1,0:T(8,128)(2,1)} %collective-permute-done.3), channel_id=1, source_target_pairs={{1,0},{2,1},{5,4},{6,5},{9,8},{10,9},{13,12},{14,13},{17,16},{18,1... | collective-permute-start | bytes 1671176 | tf_op jit(solution)/shard_map/ppermute | solution.py:66
  48.9 26.5 %collective-permute-start.1 = (bf16[1024,256]{1,0:T(8,128)(2,1)}, bf16[1024,256]{1,0:T(8,128)(2,1)}, u32[]{:S(2)}, u32[]{:S(2)}) collective-permute-start(bf16[1024,256]{1,0:T(8,128)(2,1)} %param.14), channel_id=1, source_target_pairs={{0,4},{4,0},{8,12},{12,8},{1,5},{5,1},{9,13},{13,9},{2,6},{6,2},{1... | collective-permute-start | bytes 1572872 | tf_op jit(solution)/shard_map/ppermute | solution.py:20
  56.5 19.0 %collective-permute-start.2 = (bf16[1024,256]{1,0:T(8,128)(2,1)S(1)}, bf16[1024,256]{1,0:T(8,128)(2,1)}, u32[]{:S(2)}, u32[]{:S(2)}) collective-permute-start(bf16[1024,256]{1,0:T(8,128)(2,1)S(1)} %collective-permute-done), channel_id=1, source_target_pairs={{0,4},{4,0},{8,12},{12,8},{1,5},{5,1},{9,13},{13,9},{2,6},{6,2},{1... | collective-permute-start | bytes 1572872 | tf_op jit(solution)/shard_map/ppermute | solution.py:20
  57.0 24.1 %collective-permute-start.6 = (bf16[272,1024]{1,0:T(8,128)(2,1)}, bf16[272,1024]{1,0:T(8,128)(2,1)}, u32[]{:S(2)}, u32[]{:S(2)}) collective-permute-start(bf16[272,1024]{1,0:T(8,128)(2,1)} %collective-permute-done.5), channel_id=1, source_target_pairs={{2,3},{6,7},{10,11},{14,15},{18,19},{22,23},{26,27},{30,31}} | collective-permute-start | bytes 1671176 | tf_op jit(solution)/shard_map/ppermute | solution.py:67
  74.1 24.9 %collective-permute-start.8 = (bf16[272,1024]{1,0:T(8,128)(2,1)}, bf16[272,1024]{1,0:T(8,128)(2,1)}, u32[]{:S(2)}, u32[]{:S(2)}) collective-permute-start(bf16[272,1024]{1,0:T(8,128)(2,1)} %collective-permute-done.7), channel_id=1, source_target_pairs={{1,0},{5,4},{9,8},{13,12},{17,16},{21,20},{25,24},{29,28}} | collective-permute-start | bytes 1671176 | tf_op jit(solution)/shard_map/ppermute | solution.py:66
  79.6 42.1 %collective-permute-start.9 = (bf16[512,1024]{1,0:T(8,128)(2,1)}, bf16[512,1024]{1,0:T(8,128)(2,1)}, u32[]{:S(2)}, u32[]{:S(2)}) collective-permute-start(bf16[512,1024]{1,0:T(8,128)(2,1)} %bitcast.5), channel_id=1, source_target_pairs={{0,16},{16,0},{1,17},{17,1},{2,18},{18,2},{3,19},{19,3},{4,20},{20... | collective-permute-start | bytes 3145736 | tf_op jit(solution)/shard_map/ppermute | solution.py:20
  102.5 29.4 %all-to-all-start.3 = ((bf16[4,128,1024]{2,1,0:T(8,128)(2,1)}), bf16[4,128,1024]{2,1,0:T(8,128)(2,1)}, u32[]{:S(2)}, u32[]{:S(2)}) async-start(bf16[4,128,1024]{2,1,0:T(8,128)(2,1)} %broadcast_in_dim.146), calls=%async_computation.3 | async-start | bytes 2097152 | tf_op jit(solution)/shard_map/all_to_all | solution.py:34
  137.6 14.0 %collective-permute-start.11 = (bf16[256,1024]{1,0:T(8,128)(2,1)S(1)}, bf16[256,1024]{1,0:T(8,128)(2,1)S(1)}, u32[]{:S(2)}, u32[]{:S(2)}) collective-permute-start(bf16[256,1024]{1,0:T(8,128)(2,1)S(1)} %fusion.28), channel_id=1, source_target_pairs={{0,8},{4,12},{8,0},{12,4},{1,9},{5,13},{9,1},{13,5},{2,10},{6,14},... | collective-permute-start | bytes 1572872 | tf_op jit(solution)/shard_map/ppermute | solution.py:20
  141.5 25.8 %collective-permute-start.13 = (bf16[512,1024]{1,0:T(8,128)(2,1)}, bf16[512,1024]{1,0:T(8,128)(2,1)S(1)}, u32[]{:S(2)}, u32[]{:S(2)}) collective-permute-start(bf16[512,1024]{1,0:T(8,128)(2,1)} %bitcast.18), channel_id=1, source_target_pairs={{0,16},{16,0},{1,17},{17,1},{2,18},{18,2},{3,19},{19,3},{4,20},{20... | collective-permute-start | bytes 3145736 | tf_op jit(solution)/shard_map/ppermute | solution.py:20
  183.1 235.5 %reduce-scatter.2.cloned.1.call-start = ((), (), s32[]{:S(2)}) async-start(), calls=%async_computation.8 | async-start | bytes 2621440 | tf_op jit(solution)/shard_map/reduce_scatter | solution.py:350
  186.0 17.2 %collective-permute-start.17 = (bf16[256,1024]{1,0:T(8,128)(2,1)}, bf16[256,1024]{1,0:T(8,128)(2,1)}, u32[]{:S(2)}, u32[]{:S(2)}) collective-permute-start(bf16[256,1024]{1,0:T(8,128)(2,1)} %fusion.24), channel_id=1, source_target_pairs={{0,8},{4,12},{8,0},{12,4},{1,9},{5,13},{9,1},{13,5},{2,10},{6,14},... | collective-permute-start | bytes 1572872 | tf_op jit(solution)/shard_map/ppermute | solution.py:20
  239.6 14.0 %collective-permute-start.25 = (bf16[256,1024]{1,0:T(8,128)(2,1)S(1)}, bf16[256,1024]{1,0:T(8,128)(2,1)S(1)}, u32[]{:S(2)}, u32[]{:S(2)}) collective-permute-start(bf16[256,1024]{1,0:T(8,128)(2,1)S(1)} %fusion.21), channel_id=1, source_target_pairs={{0,8},{4,12},{8,0},{12,4},{1,9},{5,13},{9,1},{13,5},{2,10},{6,14},... | collective-permute-start | bytes 1572872 | tf_op jit(solution)/shard_map/ppermute | solution.py:20
  258.6 26.3 %collective-permute-start.29 = (bf16[512,1024]{1,0:T(8,128)(2,1)S(1)}, bf16[512,1024]{1,0:T(8,128)(2,1)}, u32[]{:S(2)}, u32[]{:S(2)}) collective-permute-start(bf16[512,1024]{1,0:T(8,128)(2,1)S(1)} %constant_dynamic-slice_fusion.11), channel_id=1, source_target_pairs={{0,16},{16,0},{1,17},{17,1},{2,18},{18,2},{3,19},{19,3},{4,20},{20... | collective-permute-start | bytes 3145736 | tf_op jit(solution)/shard_map/ppermute | solution.py:20
  272.2 33.1 %collective-permute-start.30 = (bf16[512,1024]{1,0:T(8,128)(2,1)}, bf16[512,1024]{1,0:T(8,128)(2,1)}, u32[]{:S(2)}, u32[]{:S(2)}) collective-permute-start(bf16[512,1024]{1,0:T(8,128)(2,1)} %constant_dynamic-slice_fusion.6), channel_id=1, source_target_pairs={{0,16},{16,0},{1,17},{17,1},{2,18},{18,2},{3,19},{19,3},{4,20},{20... | collective-permute-start | bytes 3145736 | tf_op jit(solution)/shard_map/ppermute | solution.py:20
  320.3 94.0 %all-to-all-start.5 = ((bf16[16,256,256]{2,1,0:T(8,128)(2,1)}), bf16[16,256,256]{2,1,0:T(8,128)(2,1)}, u32[]{:S(2)}, u32[]{:S(2)}) async-start(bf16[16,256,256]{2,1,0:T(8,128)(2,1)} %bitcast.192), calls=%async_computation.5 | async-start | bytes 4194304 | tf_op jit(solution)/shard_map/all_to_all | solution.py:34
  336.1 74.5 %collective-permute-start.31 = (bf16[1024,512]{1,0:T(8,128)(2,1)}, bf16[1024,512]{1,0:T(8,128)(2,1)}, u32[]{:S(2)}, u32[]{:S(2)}) collective-permute-start(bf16[1024,512]{1,0:T(8,128)(2,1)} %fusion.13), channel_id=1, source_target_pairs={{0,4},{4,0},{8,12},{12,8},{1,5},{5,1},{9,13},{13,9},{2,6},{6,2},{1... | collective-permute-start | bytes 3145736 | tf_op jit(solution)/shard_map/ppermute | solution.py:20
  346.5 44.0 %collective-permute-start.36 = (f32[12,1024]{1,0:T(8,128)S(1)}, f32[12,1024]{1,0:T(8,128)S(1)}, u32[]{:S(2)}, u32[]{:S(2)}) collective-permute-start(f32[12,1024]{1,0:T(8,128)S(1)} %add.408), channel_id=1, source_target_pairs={{0,1},{1,0},{2,3},{3,2},{4,5},{5,4},{6,7},{7,6},{8,9},{9,8},{10,11... | collective-permute-start | bytes 147464 | tf_op jit(solution)/shard_map/ppermute | solution.py:20
  390.5 15.6 %collective-permute-start.37 = (f32[12,1024]{1,0:T(8,128)S(1)}, f32[12,1024]{1,0:T(8,128)S(1)}, u32[]{:S(2)}, u32[]{:S(2)}) collective-permute-start(f32[12,1024]{1,0:T(8,128)S(1)} %add.409), channel_id=1, source_target_pairs={{0,2},{1,3},{2,0},{3,1},{4,6},{5,7},{6,4},{7,5},{8,10},{9,11},{10,... | collective-permute-start | bytes 147464 | tf_op jit(solution)/shard_map/ppermute | solution.py:20
  412.8 13.6 %collective-permute-start.32 = (bf16[1024,256]{1,0:T(8,128)(2,1)}, bf16[1024,256]{1,0:T(8,128)(2,1)}, u32[]{:S(2)}, u32[]{:S(2)}) collective-permute-start(bf16[1024,256]{1,0:T(8,128)(2,1)} %fusion.19), channel_id=1, source_target_pairs={{0,8},{4,12},{8,0},{12,4},{1,9},{5,13},{9,1},{13,5},{2,10},{6,14},... | collective-permute-start | bytes 1572872 | tf_op jit(solution)/shard_map/ppermute | solution.py:20
  417.1 15.2 %collective-permute-start.33 = (bf16[4,256,256]{2,1,0:T(8,128)(2,1)}, bf16[4,256,256]{2,1,0:T(8,128)(2,1)}, u32[]{:S(2)}, u32[]{:S(2)}) collective-permute-start(bf16[4,256,256]{2,1,0:T(8,128)(2,1)} %bitcast_reduce_fusion), channel_id=1, source_target_pairs={{0,16},{16,0},{1,17},{17,1},{2,18},{18,2},{3,19},{19,3},{4,20},{20... | collective-permute-start | bytes 1572872 | tf_op jit(solution)/shard_map/ppermute | solution.py:20
  420.7 20.9 %all-to-all-start.6 = ((bf16[8,256,256]{2,1,0:T(8,128)(2,1)}), bf16[8,256,256]{2,1,0:T(8,128)(2,1)S(1)}, u32[]{:S(2)}, u32[]{:S(2)}) async-start(bf16[8,256,256]{2,1,0:T(8,128)(2,1)} %bitcast.197), calls=%async_computation.7 | async-start | bytes 2097152 | tf_op jit(solution)/shard_map/all_to_all | solution.py:34
  (103 other events, 803.2 us)
Sparse Core Ops, SparseCore 0:
  316.7 74.0 reduce-scatter.1

commit v3 on v2

--- a/solution.py
+++ b/solution.py
@@ -332,16 +332,16 @@
 
     def by_owner(values):
         each = values.shape[2]
-        got = trade(values.reshape(-1, each, width_local), ("row", "col"))
-        got = jnp.sum(got.reshape(rows, cols, each, width_local).astype(f32), 1)
-        return dp_sum(got, 1)
+        raw = trade(values.reshape(-1, each, width_local), ("row", "col"))
+        got = jnp.sum(raw.reshape(rows, cols, each, width_local).astype(f32), 1)
+        return dp_sum(got, 1), raw
 
     grad_wo = dot(context, d_att_all, 0, 0).astype(bf16).reshape(cols, head_piece, rows, width_local)
     grad_wo = jnp.transpose(grad_wo, (2, 0, 1, 3))
 
     d_context = from_rel(dot(d_att_all, wo_all, 1, 1).astype(bf16), 0)
     d_joined = by_sequence(attend_back_kernel, [joined, d_context], 3 * heads_width, 10)
-    d_joined, wi_other = lax.optimization_barrier((d_joined, wi_other))
+    wi_other = after(wi_other, d_joined)
     hid_grads = [
         (half_of(grad, n).astype(f32) + other.astype(f32)).astype(bf16).reshape(cols, half, width)
         for grad, other in ((grad_wb, wb_other), (grad_wi, wi_other))
@@ -356,7 +356,7 @@
         grad_wq.append(dot(d_joined, owned, 0, 0).astype(bf16).reshape(cols, heads_rows, -1))
     grad_wq = jnp.concatenate([jnp.stack(grad_wq), grad_wo], 2)
     d_joined_late = after(d_joined, grad_wq)
-    grad_wq = by_owner(grad_wq)
+    grad_wq, arrived = by_owner(grad_wq)
     grad_w_out = grad_wq[:, heads_rows:].reshape(heads_tile, width_local)
     grad_wq = grad_wq[:, :heads_rows].reshape(rows, 3, head_piece, width_local)
     grad_w_qkv = jnp.transpose(grad_wq, (1, 3, 0, 2)).reshape(3, width_local, heads_tile)
@@ -397,8 +397,9 @@
     )
     col_sums = jnp.where((jnp.arange(rows) == r)[None, :, None], col_sums[:, None], 0.0)
     small = jnp.concatenate([vector_grads, col_sums.reshape(-1, width)], 0)
-    for axis in ("row", "col", "dp"):
+    for axis in ("row", "dp", "col"):
         bit = 1
+        small = after(small, arrived) if axis == "col" else small
         while bit < lax.axis_size(axis):
             small = small + swap(small, axis, bit)
             bit *= 2

time: 457 us -> 442 us (0.967)
  waiting for transfers between devices: 215 us -> 202 us
  local copies, waits for them, and re-layouts: 37.7 us -> 43.4 us
  starting transfers between devices: 69.5 us -> 64.4 us
    ppermute x33, waiting for transfers between devices: 155 us -> 106 us  [swap(): return lax.ppermute(values, axis, [(i, i ^ bit) for i in range(size)])]
    all_to_all x7, waiting for transfers between devices: 26.2 us -> 62.3 us  [trade(): return lax.all_to_all(values, axis, 0, 0, tiled=True)]
    ppermute x33, starting transfers between devices: 27.5 us -> 22.5 us  [swap(): return lax.ppermute(values, axis, [(i, i ^ bit) for i in range(size)])]
    unnamed x176 -> x174, local copies, waits for them, and re-layouts: 14 us -> 14.7 us
  transfers between devices with their start and end apart: 47 -> 47, of which waited for: 28 -> 27; matrix products, arithmetic and copies ran while one was open for 19% -> 22% of each run, Pallas kernels for 4% -> 4%
where the time goes in v3:
time: 442 us; the launch traced here: 436 us
  waiting for transfers between devices  202 us (46%)
  starting transfers between devices  64.4 us (15%)
  other arithmetic  51.9 us (12%)
  local copies, waits for them, and re-layouts  43.4 us (10%)
  matrix products  42.2 us (10%)
  between operations  16.1 us (4%)
  Pallas kernels  15.9 us (4%)
    ppermute x33, waiting for transfers between devices, swap(): return lax.ppermute(values, axis, [(i, i ^ bit) for i in range(size)])  106 us
    all_to_all x7, waiting for transfers between devices, trade(): return lax.all_to_all(values, axis, 0, 0, tiled=True)  62.3 us
    dot_general x23, matrix products, dot(): lax.dot_general(left, right, (((left_dim,), (right_dim,)), ((), ())), pre...  42.2 us
    ppermute x3, waiting for transfers between devices, line_step(): lax.ppermute(up, 'col', [(i, i - 1) for i in range(1, size - step + 1)])  31.8 us
    all_to_all x7, starting transfers between devices, trade(): return lax.all_to_all(values, axis, 0, 0, tiled=True)  29.2 us
    ppermute x33, starting transfers between devices, swap(): return lax.ppermute(values, axis, [(i, i ^ bit) for i in range(size)])  22.5 us
    pallas_call x2, Pallas kernels, by_sequence(): pl.pallas_call(kernel, grid=(tokens // SEQ_LEN,), in_specs=[pl.BlockSpec(...  15.9 us
    unnamed x174, local copies, waits for them, and re-layouts  14.7 us
  transfers between devices with their start and end apart: 47, of which 27 were waited for; matrix products, arithmetic and copies ran while one was open for 22% of the time, Pallas kernels for 4%

profile of v3, /device:TPU:0, one launch (start us, length us, event | category | flops | bytes accessed | tf_op | source)
XLA Modules:
  0.0 435.7 jit_solution(13121910695306084214)
XLA Ops:
  10.3 4.2 all-to-all-start.2
  16.8 6.6 %all-to-all-done.2 = bf16[4,256,256]{2,1,0:T(8,128)(2,1)S(1)} async-done(((bf16[4,256,256]{2,1,0:T(8,128)(2,1)}), bf16[4,256,256]{2,1,0:T(8,128)(2,1)S(1)}, u32[]{:S(2)}, u32[]{:S(2)}) %all-to-all-start.2) | async-done | bytes 524320 | tf_op jit(solution)/shard_map/all_to_all | solution.py:34
  28.5 5.6 %collective-permute-start.4 = (bf16[272,1024]{1,0:T(8,128)(2,1)S(1)}, bf16[272,1024]{1,0:T(8,128)(2,1)}, u32[]{:S(2)}, u32[]{:S(2)}) collective-permute-start(bf16[272,1024]{1,0:T(8,128)(2,1)S(1)} %fusion.38), channel_id=1, source_target_pairs={{0,1},{1,2},{2,3},{4,5},{5,6},{6,7},{8,9},{9,10},{10,11},{12,13},{... | collective-permute-start | bytes 1671176 | tf_op jit(solution)/shard_map/ppermute | solution.py:67
  37.6 5.5 %all-to-all-start.1 = ((bf16[4,128,1024]{2,1,0:T(8,128)(2,1)}), bf16[4,128,1024]{2,1,0:T(8,128)(2,1)}, u32[]{:S(2)}, u32[]{:S(2)}) async-start(bf16[4,128,1024]{2,1,0:T(8,128)(2,1)} %broadcast_in_dim.137), calls=%async_computation.1 | async-start | bytes 2097152 | tf_op jit(solution)/shard_map/all_to_all | solution.py:34
  49.0 7.5 %collective-permute-done = bf16[1024,256]{1,0:T(8,128)(2,1)S(1)} collective-permute-done((bf16[1024,256]{1,0:T(8,128)(2,1)}, bf16[1024,256]{1,0:T(8,128)(2,1)S(1)}, u32[]{:S(2)}, u32[]{:S(2)}) %collective-permute-start) | collective-permute-done | bytes 524320 | tf_op jit(solution)/shard_map/ppermute | solution.py:20
  60.3 13.9 %collective-permute-done.7 = bf16[272,1024]{1,0:T(8,128)(2,1)} collective-permute-done((bf16[272,1024]{1,0:T(8,128)(2,1)}, bf16[272,1024]{1,0:T(8,128)(2,1)}, u32[]{:S(2)}, u32[]{:S(2)}) %collective-permute-start.7) | collective-permute-done | bytes 557088 | tf_op jit(solution)/shard_map/ppermute | solution.py:66
  82.3 16.7 %collective-permute-done.8 = bf16[272,1024]{1,0:T(8,128)(2,1)} collective-permute-done((bf16[272,1024]{1,0:T(8,128)(2,1)}, bf16[272,1024]{1,0:T(8,128)(2,1)}, u32[]{:S(2)}, u32[]{:S(2)}) %collective-permute-start.8) | collective-permute-done | bytes 557088 | tf_op jit(solution)/shard_map/ppermute | solution.py:66
  102.5 4.5 %all-to-all-start.3 = ((bf16[4,128,1024]{2,1,0:T(8,128)(2,1)}), bf16[4,128,1024]{2,1,0:T(8,128)(2,1)}, u32[]{:S(2)}, u32[]{:S(2)}) async-start(bf16[4,128,1024]{2,1,0:T(8,128)(2,1)} %broadcast_in_dim.146), calls=%async_computation.3 | async-start | bytes 2097152 | tf_op jit(solution)/shard_map/all_to_all | solution.py:34
  110.5 6.5 %shard_map.245 = bf16[1024,256]{1,0:T(8,128)(2,1)S(1)} custom-call(bf16[1024,768]{1,0:T(8,128)(2,1)S(1)} %add_convert_fusion.2.qkv_ref), custom_call_target="tpu_custom_call" | custom-call | flops 536870912 | bytes 2097152 | tf_op jit(solution)/shard_map/pallas_call | solution.py:157
  124.8 7.1 %all-to-all-done.3 = bf16[4,128,1024]{2,1,0:T(8,128)(2,1)} async-done(((bf16[4,128,1024]{2,1,0:T(8,128)(2,1)}), bf16[4,128,1024]{2,1,0:T(8,128)(2,1)}, u32[]{:S(2)}, u32[]{:S(2)}) %all-to-all-start.3) | async-done | bytes 1048608 | tf_op jit(solution)/shard_map/all_to_all | solution.py:34
  143.1 8.5 %collective-permute-done.11 = bf16[256,1024]{1,0:T(8,128)(2,1)S(1)} collective-permute-done((bf16[256,1024]{1,0:T(8,128)(2,1)S(1)}, bf16[256,1024]{1,0:T(8,128)(2,1)S(1)}, u32[]{:S(2)}, u32[]{:S(2)}) %collective-permute-start.11) | collective-permute-done | bytes 524320 | tf_op jit(solution)/shard_map/ppermute | solution.py:20
  155.2 12.2 %collective-permute-done.14 = bf16[256,1024]{1,0:T(8,128)(2,1)S(1)} collective-permute-done((bf16[256,1024]{1,0:T(8,128)(2,1)S(1)}, bf16[256,1024]{1,0:T(8,128)(2,1)S(1)}, u32[]{:S(2)}, u32[]{:S(2)}) %collective-permute-start.14) | collective-permute-done | bytes 524320 | tf_op jit(solution)/shard_map/ppermute | solution.py:20
  188.0 4.4 %all-to-all-done.4 = bf16[4,256,256]{2,1,0:T(8,128)(2,1)S(1)} async-done(((bf16[4,256,256]{2,1,0:T(8,128)(2,1)}), bf16[4,256,256]{2,1,0:T(8,128)(2,1)S(1)}, u32[]{:S(2)}, u32[]{:S(2)}) %all-to-all-start.4) | async-done | bytes 524320 | tf_op jit(solution)/shard_map/all_to_all | solution.py:34
  193.8 9.4 %collective-permute-done.17 = bf16[256,1024]{1,0:T(8,128)(2,1)} collective-permute-done((bf16[256,1024]{1,0:T(8,128)(2,1)}, bf16[256,1024]{1,0:T(8,128)(2,1)}, u32[]{:S(2)}, u32[]{:S(2)}) %collective-permute-start.17) | collective-permute-done | bytes 524320 | tf_op jit(solution)/shard_map/ppermute | solution.py:20
  208.3 13.1 %collective-permute-done.22 = bf16[256,1024]{1,0:T(8,128)(2,1)S(1)} collective-permute-done((bf16[256,1024]{1,0:T(8,128)(2,1)S(1)}, bf16[256,1024]{1,0:T(8,128)(2,1)S(1)}, u32[]{:S(2)}, u32[]{:S(2)}) %collective-permute-start.22) | collective-permute-done | bytes 524320 | tf_op jit(solution)/shard_map/ppermute | solution.py:20
  227.6 3.8 convert_reduce_fusion.1
  242.6 10.6 %collective-permute-done.25 = bf16[256,1024]{1,0:T(8,128)(2,1)S(1)} collective-permute-done((bf16[256,1024]{1,0:T(8,128)(2,1)S(1)}, bf16[256,1024]{1,0:T(8,128)(2,1)S(1)}, u32[]{:S(2)}, u32[]{:S(2)}) %collective-permute-start.25) | collective-permute-done | bytes 524320 | tf_op jit(solution)/shard_map/ppermute | solution.py:20
  262.5 8.2 %collective-permute-done.26 = bf16[256,1024]{1,0:T(8,128)(2,1)} collective-permute-done((bf16[256,1024]{1,0:T(8,128)(2,1)S(1)}, bf16[256,1024]{1,0:T(8,128)(2,1)}, u32[]{:S(2)}, u32[]{:S(2)}) %collective-permute-start.26) | collective-permute-done | bytes 524320 | tf_op jit(solution)/shard_map/ppermute | solution.py:20
  275.2 9.3 %collective-permute-done.29 = bf16[512,1024]{1,0:T(8,128)(2,1)} collective-permute-done((bf16[512,1024]{1,0:T(8,128)(2,1)S(1)}, bf16[512,1024]{1,0:T(8,128)(2,1)}, u32[]{:S(2)}, u32[]{:S(2)}) %collective-permute-start.29) | collective-permute-done | bytes 1048608 | tf_op jit(solution)/shard_map/ppermute | solution.py:20
  286.4 9.4 %shard_map.246 = bf16[1024,768]{1,0:T(8,128)(2,1)S(1)} custom-call(bf16[1024,768]{1,0:T(8,128)(2,1)S(1)} %add_convert_fusion.2.qkv_ref, bf16[1024,256]{1,0:T(8,128)(2,1)S(1)} %pad_maximum_fusion.18.d_context_ref), custom_call_target="tpu_custom_call" | custom-call | flops 1342177280 | bytes 3670016 | tf_op jit(solution)/shard_map/pallas_call | solution.py:157
  308.1 4.4 %all-to-all-start.5 = ((bf16[16,256,256]{2,1,0:T(8,128)(2,1)}), bf16[16,256,256]{2,1,0:T(8,128)(2,1)}, u32[]{:S(2)}, u32[]{:S(2)}) async-start(bf16[16,256,256]{2,1,0:T(8,128)(2,1)} %bitcast.192), calls=%async_computation.5 | async-start | bytes 4194304 | tf_op jit(solution)/shard_map/all_to_all | solution.py:34
  345.0 12.8 %collective-permute-done.34 = f32[12,1024]{1,0:T(8,128)S(1)} collective-permute-done((f32[12,1024]{1,0:T(8,128)S(1)}, f32[12,1024]{1,0:T(8,128)S(1)}, u32[]{:S(2)}, u32[]{:S(2)}) %collective-permute-start.34) | collective-permute-done | bytes 49184 | tf_op jit(solution)/shard_map/ppermute | solution.py:20
  362.2 33.5 %all-to-all-done.5 = bf16[16,256,256]{2,1,0:T(8,128)(2,1)} async-done(((bf16[16,256,256]{2,1,0:T(8,128)(2,1)}), bf16[16,256,256]{2,1,0:T(8,128)(2,1)}, u32[]{:S(2)}, u32[]{:S(2)}) %all-to-all-start.5) | async-done | bytes 2097184 | tf_op jit(solution)/shard_map/all_to_all | solution.py:34
  417.3 8.6 %all-to-all-done.6 = bf16[8,256,256]{2,1,0:T(8,128)(2,1)S(1)} async-done(((bf16[8,256,256]{2,1,0:T(8,128)(2,1)}), bf16[8,256,256]{2,1,0:T(8,128)(2,1)S(1)}, u32[]{:S(2)}, u32[]{:S(2)}) %all-to-all-start.6) | async-done | bytes 1048608 | tf_op jit(solution)/shard_map/all_to_all | solution.py:34
  (423 shorter events, 193.1 us)
Async XLA Ops:
  27.2 17.5 %collective-permute-start.3 = (bf16[272,1024]{1,0:T(8,128)(2,1)S(1)}, bf16[272,1024]{1,0:T(8,128)(2,1)}, u32[]{:S(2)}, u32[]{:S(2)}) collective-permute-start(bf16[272,1024]{1,0:T(8,128)(2,1)S(1)} %fusion.38), channel_id=1, source_target_pairs={{1,0},{2,1},{3,2},{5,4},{6,5},{7,6},{9,8},{10,9},{11,10},{13,12},{... | collective-permute-start | bytes 1671176 | tf_op jit(solution)/shard_map/ppermute | solution.py:66
  28.5 17.7 %collective-permute-start.4 = (bf16[272,1024]{1,0:T(8,128)(2,1)S(1)}, bf16[272,1024]{1,0:T(8,128)(2,1)}, u32[]{:S(2)}, u32[]{:S(2)}) collective-permute-start(bf16[272,1024]{1,0:T(8,128)(2,1)S(1)} %fusion.38), channel_id=1, source_target_pairs={{0,1},{1,2},{2,3},{4,5},{5,6},{6,7},{8,9},{9,10},{10,11},{12,13},{... | collective-permute-start | bytes 1671176 | tf_op jit(solution)/shard_map/ppermute | solution.py:67
  37.6 42.0 %all-to-all-start.1 = ((bf16[4,128,1024]{2,1,0:T(8,128)(2,1)}), bf16[4,128,1024]{2,1,0:T(8,128)(2,1)}, u32[]{:S(2)}, u32[]{:S(2)}) async-start(bf16[4,128,1024]{2,1,0:T(8,128)(2,1)} %broadcast_in_dim.137), calls=%async_computation.1 | async-start | bytes 2097152 | tf_op jit(solution)/shard_map/all_to_all | solution.py:34
  43.1 13.4 %collective-permute-start = (bf16[1024,256]{1,0:T(8,128)(2,1)}, bf16[1024,256]{1,0:T(8,128)(2,1)S(1)}, u32[]{:S(2)}, u32[]{:S(2)}) collective-permute-start(bf16[1024,256]{1,0:T(8,128)(2,1)} %param.14), channel_id=1, source_target_pairs={{0,8},{4,12},{8,0},{12,4},{1,9},{5,13},{9,1},{13,5},{2,10},{6,14},... | collective-permute-start | bytes 1572872 | tf_op jit(solution)/shard_map/ppermute | solution.py:20
  47.7 26.5 %collective-permute-start.7 = (bf16[272,1024]{1,0:T(8,128)(2,1)}, bf16[272,1024]{1,0:T(8,128)(2,1)}, u32[]{:S(2)}, u32[]{:S(2)}) collective-permute-start(bf16[272,1024]{1,0:T(8,128)(2,1)} %collective-permute-done.3), channel_id=1, source_target_pairs={{1,0},{2,1},{5,4},{6,5},{9,8},{10,9},{13,12},{14,13},{17,16},{18,1... | collective-permute-start | bytes 1671176 | tf_op jit(solution)/shard_map/ppermute | solution.py:66
  48.9 26.5 %collective-permute-start.1 = (bf16[1024,256]{1,0:T(8,128)(2,1)}, bf16[1024,256]{1,0:T(8,128)(2,1)}, u32[]{:S(2)}, u32[]{:S(2)}) collective-permute-start(bf16[1024,256]{1,0:T(8,128)(2,1)} %param.14), channel_id=1, source_target_pairs={{0,4},{4,0},{8,12},{12,8},{1,5},{5,1},{9,13},{13,9},{2,6},{6,2},{1... | collective-permute-start | bytes 1572872 | tf_op jit(solution)/shard_map/ppermute | solution.py:20
  56.5 19.0 %collective-permute-start.2 = (bf16[1024,256]{1,0:T(8,128)(2,1)S(1)}, bf16[1024,256]{1,0:T(8,128)(2,1)}, u32[]{:S(2)}, u32[]{:S(2)}) collective-permute-start(bf16[1024,256]{1,0:T(8,128)(2,1)S(1)} %collective-permute-done), channel_id=1, source_target_pairs={{0,4},{4,0},{8,12},{12,8},{1,5},{5,1},{9,13},{13,9},{2,6},{6,2},{1... | collective-permute-start | bytes 1572872 | tf_op jit(solution)/shard_map/ppermute | solution.py:20
  57.0 24.1 %collective-permute-start.6 = (bf16[272,1024]{1,0:T(8,128)(2,1)}, bf16[272,1024]{1,0:T(8,128)(2,1)}, u32[]{:S(2)}, u32[]{:S(2)}) collective-permute-start(bf16[272,1024]{1,0:T(8,128)(2,1)} %collective-permute-done.5), channel_id=1, source_target_pairs={{2,3},{6,7},{10,11},{14,15},{18,19},{22,23},{26,27},{30,31}} | collective-permute-start | bytes 1671176 | tf_op jit(solution)/shard_map/ppermute | solution.py:67
  74.1 24.9 %collective-permute-start.8 = (bf16[272,1024]{1,0:T(8,128)(2,1)}, bf16[272,1024]{1,0:T(8,128)(2,1)}, u32[]{:S(2)}, u32[]{:S(2)}) collective-permute-start(bf16[272,1024]{1,0:T(8,128)(2,1)} %collective-permute-done.7), channel_id=1, source_target_pairs={{1,0},{5,4},{9,8},{13,12},{17,16},{21,20},{25,24},{29,28}} | collective-permute-start | bytes 1671176 | tf_op jit(solution)/shard_map/ppermute | solution.py:66
  79.6 42.1 %collective-permute-start.9 = (bf16[512,1024]{1,0:T(8,128)(2,1)}, bf16[512,1024]{1,0:T(8,128)(2,1)}, u32[]{:S(2)}, u32[]{:S(2)}) collective-permute-start(bf16[512,1024]{1,0:T(8,128)(2,1)} %bitcast.5), channel_id=1, source_target_pairs={{0,16},{16,0},{1,17},{17,1},{2,18},{18,2},{3,19},{19,3},{4,20},{20... | collective-permute-start | bytes 3145736 | tf_op jit(solution)/shard_map/ppermute | solution.py:20
  102.5 29.4 %all-to-all-start.3 = ((bf16[4,128,1024]{2,1,0:T(8,128)(2,1)}), bf16[4,128,1024]{2,1,0:T(8,128)(2,1)}, u32[]{:S(2)}, u32[]{:S(2)}) async-start(bf16[4,128,1024]{2,1,0:T(8,128)(2,1)} %broadcast_in_dim.146), calls=%async_computation.3 | async-start | bytes 2097152 | tf_op jit(solution)/shard_map/all_to_all | solution.py:34
  137.6 14.0 %collective-permute-start.11 = (bf16[256,1024]{1,0:T(8,128)(2,1)S(1)}, bf16[256,1024]{1,0:T(8,128)(2,1)S(1)}, u32[]{:S(2)}, u32[]{:S(2)}) collective-permute-start(bf16[256,1024]{1,0:T(8,128)(2,1)S(1)} %fusion.28), channel_id=1, source_target_pairs={{0,8},{4,12},{8,0},{12,4},{1,9},{5,13},{9,1},{13,5},{2,10},{6,14},... | collective-permute-start | bytes 1572872 | tf_op jit(solution)/shard_map/ppermute | solution.py:20
  141.6 25.8 %collective-permute-start.13 = (bf16[512,1024]{1,0:T(8,128)(2,1)}, bf16[512,1024]{1,0:T(8,128)(2,1)S(1)}, u32[]{:S(2)}, u32[]{:S(2)}) collective-permute-start(bf16[512,1024]{1,0:T(8,128)(2,1)} %bitcast.18), channel_id=1, source_target_pairs={{0,16},{16,0},{1,17},{17,1},{2,18},{18,2},{3,19},{19,3},{4,20},{20... | collective-permute-start | bytes 3145736 | tf_op jit(solution)/shard_map/ppermute | solution.py:20
  186.0 17.3 %collective-permute-start.17 = (bf16[256,1024]{1,0:T(8,128)(2,1)}, bf16[256,1024]{1,0:T(8,128)(2,1)}, u32[]{:S(2)}, u32[]{:S(2)}) collective-permute-start(bf16[256,1024]{1,0:T(8,128)(2,1)} %fusion.24), channel_id=1, source_target_pairs={{0,8},{4,12},{8,0},{12,4},{1,9},{5,13},{9,1},{13,5},{2,10},{6,14},... | collective-permute-start | bytes 1572872 | tf_op jit(solution)/shard_map/ppermute | solution.py:20
  208.0 13.5 %collective-permute-start.22 = (bf16[256,1024]{1,0:T(8,128)(2,1)S(1)}, bf16[256,1024]{1,0:T(8,128)(2,1)S(1)}, u32[]{:S(2)}, u32[]{:S(2)}) collective-permute-start(bf16[256,1024]{1,0:T(8,128)(2,1)S(1)} %get-tuple-element.99), channel_id=1, source_target_pairs={{0,8},{4,12},{8,0},{12,4},{1,9},{5,13},{9,1},{13,5},{2,10},{6,14},... | collective-permute-start | bytes 1572872 | tf_op jit(solution)/shard_map/ppermute | solution.py:20
  239.2 14.0 %collective-permute-start.25 = (bf16[256,1024]{1,0:T(8,128)(2,1)S(1)}, bf16[256,1024]{1,0:T(8,128)(2,1)S(1)}, u32[]{:S(2)}, u32[]{:S(2)}) collective-permute-start(bf16[256,1024]{1,0:T(8,128)(2,1)S(1)} %fusion.21), channel_id=1, source_target_pairs={{0,8},{4,12},{8,0},{12,4},{1,9},{5,13},{9,1},{13,5},{2,10},{6,14},... | collective-permute-start | bytes 1572872 | tf_op jit(solution)/shard_map/ppermute | solution.py:20
  258.2 26.3 %collective-permute-start.29 = (bf16[512,1024]{1,0:T(8,128)(2,1)S(1)}, bf16[512,1024]{1,0:T(8,128)(2,1)}, u32[]{:S(2)}, u32[]{:S(2)}) collective-permute-start(bf16[512,1024]{1,0:T(8,128)(2,1)S(1)} %constant_dynamic-slice_fusion.11), channel_id=1, source_target_pairs={{0,16},{16,0},{1,17},{17,1},{2,18},{18,2},{3,19},{19,3},{4,20},{20... | collective-permute-start | bytes 3145736 | tf_op jit(solution)/shard_map/ppermute | solution.py:20
  272.0 32.9 %collective-permute-start.38 = (bf16[512,1024]{1,0:T(8,128)(2,1)S(1)}, bf16[512,1024]{1,0:T(8,128)(2,1)}, u32[]{:S(2)}, u32[]{:S(2)}) collective-permute-start(bf16[512,1024]{1,0:T(8,128)(2,1)S(1)} %constant_dynamic-slice_fusion.1), channel_id=1, source_target_pairs={{0,16},{16,0},{1,17},{17,1},{2,18},{18,2},{3,19},{19,3},{4,20},{20... | collective-permute-start | bytes 3145736 | tf_op jit(solution)/shard_map/ppermute | solution.py:20
  308.1 87.6 %all-to-all-start.5 = ((bf16[16,256,256]{2,1,0:T(8,128)(2,1)}), bf16[16,256,256]{2,1,0:T(8,128)(2,1)}, u32[]{:S(2)}, u32[]{:S(2)}) async-start(bf16[16,256,256]{2,1,0:T(8,128)(2,1)} %bitcast.192), calls=%async_computation.5 | async-start | bytes 4194304 | tf_op jit(solution)/shard_map/all_to_all | solution.py:34
  312.5 92.8 %reduce-scatter.2.cloned.1.call-start = ((), (), s32[]{:S(2)}) async-start(), calls=%async_computation.8 | async-start | bytes 2621440 | tf_op jit(solution)/shard_map/reduce_scatter | solution.py:350
  322.6 13.5 %collective-permute-start.30 = (bf16[1024,512]{1,0:T(8,128)(2,1)}, bf16[1024,512]{1,0:T(8,128)(2,1)}, u32[]{:S(2)}, u32[]{:S(2)}) collective-permute-start(bf16[1024,512]{1,0:T(8,128)(2,1)} %fusion.13), channel_id=1, source_target_pairs={{0,4},{4,0},{8,12},{12,8},{1,5},{5,1},{9,13},{13,9},{2,6},{6,2},{1... | collective-permute-start | bytes 3145736 | tf_op jit(solution)/shard_map/ppermute | solution.py:20
  338.6 57.1 %collective-permute-start.31 = (bf16[1024,256]{1,0:T(8,128)(2,1)S(1)}, bf16[1024,256]{1,0:T(8,128)(2,1)S(1)}, u32[]{:S(2)}, u32[]{:S(2)}) collective-permute-start(bf16[1024,256]{1,0:T(8,128)(2,1)S(1)} %fusion.19), channel_id=1, source_target_pairs={{0,8},{4,12},{8,0},{12,4},{1,9},{5,13},{9,1},{13,5},{2,10},{6,14},... | collective-permute-start | bytes 1572872 | tf_op jit(solution)/shard_map/ppermute | solution.py:20
  343.8 14.0 %collective-permute-start.34 = (f32[12,1024]{1,0:T(8,128)S(1)}, f32[12,1024]{1,0:T(8,128)S(1)}, u32[]{:S(2)}, u32[]{:S(2)}) collective-permute-start(f32[12,1024]{1,0:T(8,128)S(1)} %add.407), channel_id=1, source_target_pairs={{0,8},{4,12},{8,0},{12,4},{1,9},{5,13},{9,1},{13,5},{2,10},{6,14},... | collective-permute-start | bytes 147464 | tf_op jit(solution)/shard_map/ppermute | solution.py:20
  407.5 18.4 %all-to-all-start.6 = ((bf16[8,256,256]{2,1,0:T(8,128)(2,1)}), bf16[8,256,256]{2,1,0:T(8,128)(2,1)S(1)}, u32[]{:S(2)}, u32[]{:S(2)}) async-start(bf16[8,256,256]{2,1,0:T(8,128)(2,1)} %bitcast.69), calls=%async_computation.7 | async-start | bytes 2097152 | tf_op jit(solution)/shard_map/all_to_all | solution.py:34
  (102 other events, 688.1 us)
Sparse Core Ops, SparseCore 0:
  318.2 66.4 reduce-scatter.1

commit v4 on v3

--- a/solution.py
+++ b/solution.py
@@ -331,10 +331,17 @@
     d_att_all, wb_other = lax.optimization_barrier((d_att_all, wb_other))
 
     def by_owner(values):
-        each = values.shape[2]
-        raw = trade(values.reshape(-1, each, width_local), ("row", "col"))
+        each = values.shape[2] // 2
+        own, other = [
+            lax.dynamic_slice_in_dim(values, k * each, each, 2) for k in (n, 1 - n)
+        ]
+        paired = (own.astype(f32) + swap(other, "dp", 1).astype(f32)).astype(bf16)
+        raw = trade(paired.reshape(-1, each, width_local), ("row", "col"))
         got = jnp.sum(raw.reshape(rows, cols, each, width_local).astype(f32), 1)
-        return dp_sum(got, 1), raw
+        low = dp_sum(got, 2).astype(bf16)
+        back = swap(low, "dp", 1)
+        both = [jnp.where(n == 0, low, back), jnp.where(n == 0, back, low)]
+        return jnp.concatenate(both, 1).astype(f32), raw
 
     grad_wo = dot(context, d_att_all, 0, 0).astype(bf16).reshape(cols, head_piece, rows, width_local)
     grad_wo = jnp.transpose(grad_wo, (2, 0, 1, 3))

time: 442 us -> 432 us (0.977)
  waiting for transfers between devices: 202 us -> 182 us
  starting transfers between devices: 64.4 us -> 71.6 us
    all_to_all x7, waiting for transfers between devices: 62.3 us -> 30.3 us  [trade(): return lax.all_to_all(values, axis, 0, 0, tiled=True)]
    ppermute x33 -> x34, waiting for transfers between devices: 106 us -> 119 us  [swap(): return lax.ppermute(values, axis, [(i, i ^ bit) for i in range(size)])]
    ppermute x33 -> x34, starting transfers between devices: 22.5 us -> 29.6 us  [swap(): return lax.ppermute(values, axis, [(i, i ^ bit) for i in range(size)])]
    unnamed x174 -> x182, local copies, waits for them, and re-layouts: 14.7 us -> 16.5 us
  transfers between devices with their start and end apart: 47 -> 48, of which waited for: 27 -> 24; matrix products, arithmetic and copies ran while one was open for 22% -> 22% of each run, Pallas kernels for 4% -> 4%
where the time goes in v4:
time: 432 us; the launch traced here: 426 us
  waiting for transfers between devices  182 us (42%)
  starting transfers between devices  71.6 us (17%)
  other arithmetic  52.6 us (12%)
  local copies, waits for them, and re-layouts  44.4 us (10%)
  matrix products  42.6 us (10%)
  between operations  16.1 us (4%)
  Pallas kernels  15.9 us (4%)
    ppermute x34, waiting for transfers between devices, swap(): return lax.ppermute(values, axis, [(i, i ^ bit) for i in range(size)])  119 us
    dot_general x23, matrix products, dot(): lax.dot_general(left, right, (((left_dim,), (right_dim,)), ((), ())), pre...  42.6 us
    ppermute x3, waiting for transfers between devices, line_step(): lax.ppermute(up, 'col', [(i, i - 1) for i in range(1, size - step + 1)])  31.8 us
    all_to_all x7, waiting for transfers between devices, trade(): return lax.all_to_all(values, axis, 0, 0, tiled=True)  30.3 us
    ppermute x34, starting transfers between devices, swap(): return lax.ppermute(values, axis, [(i, i ^ bit) for i in range(size)])  29.6 us
    all_to_all x7, starting transfers between devices, trade(): return lax.all_to_all(values, axis, 0, 0, tiled=True)  29.4 us
    unnamed x182, local copies, waits for them, and re-layouts  16.5 us
    pallas_call x2, Pallas kernels, by_sequence(): pl.pallas_call(kernel, grid=(tokens // SEQ_LEN,), in_specs=[pl.BlockSpec(...  15.9 us
  transfers between devices with their start and end apart: 48, of which 24 were waited for; matrix products, arithmetic and copies ran while one was open for 22% of the time, Pallas kernels for 4%

profile of v4, /device:TPU:0, one launch (start us, length us, event | category | flops | bytes accessed | tf_op | source)
XLA Modules:
  0.0 425.7 jit_solution(13451380831373341027)
XLA Ops:
  10.3 4.2 all-to-all-start.2
  16.8 6.6 %all-to-all-done.2 = bf16[4,256,256]{2,1,0:T(8,128)(2,1)S(1)} async-done(((bf16[4,256,256]{2,1,0:T(8,128)(2,1)}), bf16[4,256,256]{2,1,0:T(8,128)(2,1)S(1)}, u32[]{:S(2)}, u32[]{:S(2)}) %all-to-all-start.2) | async-done | bytes 524320 | tf_op jit(solution)/shard_map/all_to_all | solution.py:34
  28.5 5.6 %collective-permute-start.4 = (bf16[272,1024]{1,0:T(8,128)(2,1)S(1)}, bf16[272,1024]{1,0:T(8,128)(2,1)}, u32[]{:S(2)}, u32[]{:S(2)}) collective-permute-start(bf16[272,1024]{1,0:T(8,128)(2,1)S(1)} %fusion.38), channel_id=1, source_target_pairs={{0,1},{1,2},{2,3},{4,5},{5,6},{6,7},{8,9},{9,10},{10,11},{12,13},{... | collective-permute-start | bytes 1671176 | tf_op jit(solution)/shard_map/ppermute | solution.py:67
  37.6 5.5 %all-to-all-start.1 = ((bf16[4,128,1024]{2,1,0:T(8,128)(2,1)}), bf16[4,128,1024]{2,1,0:T(8,128)(2,1)}, u32[]{:S(2)}, u32[]{:S(2)}) async-start(bf16[4,128,1024]{2,1,0:T(8,128)(2,1)} %broadcast_in_dim.137), calls=%async_computation.1 | async-start | bytes 2097152 | tf_op jit(solution)/shard_map/all_to_all | solution.py:34
  49.0 7.5 %collective-permute-done = bf16[1024,256]{1,0:T(8,128)(2,1)S(1)} collective-permute-done((bf16[1024,256]{1,0:T(8,128)(2,1)}, bf16[1024,256]{1,0:T(8,128)(2,1)S(1)}, u32[]{:S(2)}, u32[]{:S(2)}) %collective-permute-start) | collective-permute-done | bytes 524320 | tf_op jit(solution)/shard_map/ppermute | solution.py:20
  60.3 13.9 %collective-permute-done.7 = bf16[272,1024]{1,0:T(8,128)(2,1)} collective-permute-done((bf16[272,1024]{1,0:T(8,128)(2,1)}, bf16[272,1024]{1,0:T(8,128)(2,1)}, u32[]{:S(2)}, u32[]{:S(2)}) %collective-permute-start.7) | collective-permute-done | bytes 557088 | tf_op jit(solution)/shard_map/ppermute | solution.py:66
  82.3 16.8 %collective-permute-done.8 = bf16[272,1024]{1,0:T(8,128)(2,1)} collective-permute-done((bf16[272,1024]{1,0:T(8,128)(2,1)}, bf16[272,1024]{1,0:T(8,128)(2,1)}, u32[]{:S(2)}, u32[]{:S(2)}) %collective-permute-start.8) | collective-permute-done | bytes 557088 | tf_op jit(solution)/shard_map/ppermute | solution.py:66
  102.5 4.5 %all-to-all-start.3 = ((bf16[4,128,1024]{2,1,0:T(8,128)(2,1)}), bf16[4,128,1024]{2,1,0:T(8,128)(2,1)}, u32[]{:S(2)}, u32[]{:S(2)}) async-start(bf16[4,128,1024]{2,1,0:T(8,128)(2,1)} %broadcast_in_dim.146), calls=%async_computation.3 | async-start | bytes 2097152 | tf_op jit(solution)/shard_map/all_to_all | solution.py:34
  110.5 6.5 %shard_map.245 = bf16[1024,256]{1,0:T(8,128)(2,1)S(1)} custom-call(bf16[1024,768]{1,0:T(8,128)(2,1)S(1)} %add_convert_fusion.2.qkv_ref), custom_call_target="tpu_custom_call" | custom-call | flops 536870912 | bytes 2097152 | tf_op jit(solution)/shard_map/pallas_call | solution.py:157
  124.9 7.1 %all-to-all-done.3 = bf16[4,128,1024]{2,1,0:T(8,128)(2,1)} async-done(((bf16[4,128,1024]{2,1,0:T(8,128)(2,1)}), bf16[4,128,1024]{2,1,0:T(8,128)(2,1)}, u32[]{:S(2)}, u32[]{:S(2)}) %all-to-all-start.3) | async-done | bytes 1048608 | tf_op jit(solution)/shard_map/all_to_all | solution.py:34
  143.1 8.5 %collective-permute-done.11 = bf16[256,1024]{1,0:T(8,128)(2,1)S(1)} collective-permute-done((bf16[256,1024]{1,0:T(8,128)(2,1)S(1)}, bf16[256,1024]{1,0:T(8,128)(2,1)S(1)}, u32[]{:S(2)}, u32[]{:S(2)}) %collective-permute-start.11) | collective-permute-done | bytes 524320 | tf_op jit(solution)/shard_map/ppermute | solution.py:20
  155.2 12.2 %collective-permute-done.14 = bf16[256,1024]{1,0:T(8,128)(2,1)S(1)} collective-permute-done((bf16[256,1024]{1,0:T(8,128)(2,1)S(1)}, bf16[256,1024]{1,0:T(8,128)(2,1)S(1)}, u32[]{:S(2)}, u32[]{:S(2)}) %collective-permute-start.14) | collective-permute-done | bytes 524320 | tf_op jit(solution)/shard_map/ppermute | solution.py:20
  188.0 4.4 %all-to-all-done.4 = bf16[4,256,256]{2,1,0:T(8,128)(2,1)S(1)} async-done(((bf16[4,256,256]{2,1,0:T(8,128)(2,1)}), bf16[4,256,256]{2,1,0:T(8,128)(2,1)S(1)}, u32[]{:S(2)}, u32[]{:S(2)}) %all-to-all-start.4) | async-done | bytes 524320 | tf_op jit(solution)/shard_map/all_to_all | solution.py:34
  193.9 9.4 %collective-permute-done.17 = bf16[256,1024]{1,0:T(8,128)(2,1)} collective-permute-done((bf16[256,1024]{1,0:T(8,128)(2,1)}, bf16[256,1024]{1,0:T(8,128)(2,1)}, u32[]{:S(2)}, u32[]{:S(2)}) %collective-permute-start.17) | collective-permute-done | bytes 524320 | tf_op jit(solution)/shard_map/ppermute | solution.py:20
  208.3 13.1 %collective-permute-done.22 = bf16[256,1024]{1,0:T(8,128)(2,1)S(1)} collective-permute-done((bf16[256,1024]{1,0:T(8,128)(2,1)S(1)}, bf16[256,1024]{1,0:T(8,128)(2,1)S(1)}, u32[]{:S(2)}, u32[]{:S(2)}) %collective-permute-start.22) | collective-permute-done | bytes 524320 | tf_op jit(solution)/shard_map/ppermute | solution.py:20
  227.7 4.3 %convert_reduce_fusion.1 = (f32[1024]{0:T(1024)}, bf16[512,1024]{1,0:T(8,128)(2,1)S(1)}) fusion(f32[512,1024]{1,0:T(8,128)S(1)} %copy-done.81, f32[1024]{0:T(1024)S(1)} %bitcast.250, bf16[512,1024]{1,0:T(8,128)(2,1)S(1)} %constant_dynamic-update-slice_fusion.3, bf16[512,1024]{1,0:T(8,128)(2,1)S(1)} %copy-done.41, bf16[512,1024]{1,0:T(8,128)(2,1)S(1)} %copy-done.39), kind=kOutput, calls=%fused_computation.31 | convolution fusion | flops 1084750848 | bytes 6299648 | tf_op jit(solution)/shard_map/dot_general | solution.py:24
  243.1 10.6 %collective-permute-done.25 = bf16[256,1024]{1,0:T(8,128)(2,1)S(1)} collective-permute-done((bf16[256,1024]{1,0:T(8,128)(2,1)S(1)}, bf16[256,1024]{1,0:T(8,128)(2,1)S(1)}, u32[]{:S(2)}, u32[]{:S(2)}) %collective-permute-start.25) | collective-permute-done | bytes 524320 | tf_op jit(solution)/shard_map/ppermute | solution.py:20
  263.0 8.3 %collective-permute-done.26 = bf16[256,1024]{1,0:T(8,128)(2,1)} collective-permute-done((bf16[256,1024]{1,0:T(8,128)(2,1)S(1)}, bf16[256,1024]{1,0:T(8,128)(2,1)}, u32[]{:S(2)}, u32[]{:S(2)}) %collective-permute-start.26) | collective-permute-done | bytes 524320 | tf_op jit(solution)/shard_map/ppermute | solution.py:20
  275.7 9.3 %collective-permute-done.29 = bf16[512,1024]{1,0:T(8,128)(2,1)} collective-permute-done((bf16[512,1024]{1,0:T(8,128)(2,1)S(1)}, bf16[512,1024]{1,0:T(8,128)(2,1)}, u32[]{:S(2)}, u32[]{:S(2)}) %collective-permute-start.29) | collective-permute-done | bytes 1048608 | tf_op jit(solution)/shard_map/ppermute | solution.py:20
  286.9 9.4 %shard_map.246 = bf16[1024,768]{1,0:T(8,128)(2,1)S(1)} custom-call(bf16[1024,768]{1,0:T(8,128)(2,1)S(1)} %add_convert_fusion.2.qkv_ref, bf16[1024,256]{1,0:T(8,128)(2,1)S(1)} %pad_maximum_fusion.18.d_context_ref), custom_call_target="tpu_custom_call" | custom-call | flops 1342177280 | bytes 3670016 | tf_op jit(solution)/shard_map/pallas_call | solution.py:157
  316.4 20.5 %collective-permute-done.32 = bf16[4,4,128,256]{3,2,1,0:T(8,128)(2,1)} collective-permute-done((bf16[4,4,128,256]{3,2,1,0:T(8,128)(2,1)}, bf16[4,4,128,256]{3,2,1,0:T(8,128)(2,1)}, u32[]{:S(2)}, u32[]{:S(2)}) %collective-permute-start.32) | collective-permute-done | bytes 1048608 | tf_op jit(solution)/shard_map/ppermute | solution.py:20
  339.5 4.7 %all-to-all-start.5 = ((bf16[16,128,256]{2,1,0:T(8,128)(2,1)}), bf16[16,128,256]{2,1,0:T(8,128)(2,1)}, u32[]{:S(2)}, u32[]{:S(2)}) async-start(bf16[16,128,256]{2,1,0:T(8,128)(2,1)} %bitcast.196), calls=%async_computation.5 | async-start | bytes 2097152 | tf_op jit(solution)/shard_map/all_to_all | solution.py:34
  368.9 11.3 %collective-permute-done.35 = f32[12,1024]{1,0:T(8,128)S(1)} collective-permute-done((f32[12,1024]{1,0:T(8,128)S(1)}, f32[12,1024]{1,0:T(8,128)S(1)}, u32[]{:S(2)}, u32[]{:S(2)}) %collective-permute-start.35) | collective-permute-done | bytes 49184 | tf_op jit(solution)/shard_map/ppermute | solution.py:20
  405.7 10.2 %all-to-all-done.6 = bf16[8,256,256]{2,1,0:T(8,128)(2,1)S(1)} async-done(((bf16[8,256,256]{2,1,0:T(8,128)(2,1)}), bf16[8,256,256]{2,1,0:T(8,128)(2,1)S(1)}, u32[]{:S(2)}, u32[]{:S(2)}) %all-to-all-start.6) | async-done | bytes 1048608 | tf_op jit(solution)/shard_map/all_to_all | solution.py:34
  (436 shorter events, 195.2 us)
Async XLA Ops:
  27.2 17.5 %collective-permute-start.3 = (bf16[272,1024]{1,0:T(8,128)(2,1)S(1)}, bf16[272,1024]{1,0:T(8,128)(2,1)}, u32[]{:S(2)}, u32[]{:S(2)}) collective-permute-start(bf16[272,1024]{1,0:T(8,128)(2,1)S(1)} %fusion.38), channel_id=1, source_target_pairs={{1,0},{2,1},{3,2},{5,4},{6,5},{7,6},{9,8},{10,9},{11,10},{13,12},{... | collective-permute-start | bytes 1671176 | tf_op jit(solution)/shard_map/ppermute | solution.py:66
  28.5 17.7 %collective-permute-start.4 = (bf16[272,1024]{1,0:T(8,128)(2,1)S(1)}, bf16[272,1024]{1,0:T(8,128)(2,1)}, u32[]{:S(2)}, u32[]{:S(2)}) collective-permute-start(bf16[272,1024]{1,0:T(8,128)(2,1)S(1)} %fusion.38), channel_id=1, source_target_pairs={{0,1},{1,2},{2,3},{4,5},{5,6},{6,7},{8,9},{9,10},{10,11},{12,13},{... | collective-permute-start | bytes 1671176 | tf_op jit(solution)/shard_map/ppermute | solution.py:67
  37.6 42.0 %all-to-all-start.1 = ((bf16[4,128,1024]{2,1,0:T(8,128)(2,1)}), bf16[4,128,1024]{2,1,0:T(8,128)(2,1)}, u32[]{:S(2)}, u32[]{:S(2)}) async-start(bf16[4,128,1024]{2,1,0:T(8,128)(2,1)} %broadcast_in_dim.137), calls=%async_computation.1 | async-start | bytes 2097152 | tf_op jit(solution)/shard_map/all_to_all | solution.py:34
  43.1 13.4 %collective-permute-start = (bf16[1024,256]{1,0:T(8,128)(2,1)}, bf16[1024,256]{1,0:T(8,128)(2,1)S(1)}, u32[]{:S(2)}, u32[]{:S(2)}) collective-permute-start(bf16[1024,256]{1,0:T(8,128)(2,1)} %param.14), channel_id=1, source_target_pairs={{0,8},{4,12},{8,0},{12,4},{1,9},{5,13},{9,1},{13,5},{2,10},{6,14},... | collective-permute-start | bytes 1572872 | tf_op jit(solution)/shard_map/ppermute | solution.py:20
  47.6 26.5 %collective-permute-start.7 = (bf16[272,1024]{1,0:T(8,128)(2,1)}, bf16[272,1024]{1,0:T(8,128)(2,1)}, u32[]{:S(2)}, u32[]{:S(2)}) collective-permute-start(bf16[272,1024]{1,0:T(8,128)(2,1)} %collective-permute-done.3), channel_id=1, source_target_pairs={{1,0},{2,1},{5,4},{6,5},{9,8},{10,9},{13,12},{14,13},{17,16},{18,1... | collective-permute-start | bytes 1671176 | tf_op jit(solution)/shard_map/ppermute | solution.py:66
  48.9 26.5 %collective-permute-start.1 = (bf16[1024,256]{1,0:T(8,128)(2,1)}, bf16[1024,256]{1,0:T(8,128)(2,1)}, u32[]{:S(2)}, u32[]{:S(2)}) collective-permute-start(bf16[1024,256]{1,0:T(8,128)(2,1)} %param.14), channel_id=1, source_target_pairs={{0,4},{4,0},{8,12},{12,8},{1,5},{5,1},{9,13},{13,9},{2,6},{6,2},{1... | collective-permute-start | bytes 1572872 | tf_op jit(solution)/shard_map/ppermute | solution.py:20
  56.5 19.0 %collective-permute-start.2 = (bf16[1024,256]{1,0:T(8,128)(2,1)S(1)}, bf16[1024,256]{1,0:T(8,128)(2,1)}, u32[]{:S(2)}, u32[]{:S(2)}) collective-permute-start(bf16[1024,256]{1,0:T(8,128)(2,1)S(1)} %collective-permute-done), channel_id=1, source_target_pairs={{0,4},{4,0},{8,12},{12,8},{1,5},{5,1},{9,13},{13,9},{2,6},{6,2},{1... | collective-permute-start | bytes 1572872 | tf_op jit(solution)/shard_map/ppermute | solution.py:20
  57.0 24.1 %collective-permute-start.6 = (bf16[272,1024]{1,0:T(8,128)(2,1)}, bf16[272,1024]{1,0:T(8,128)(2,1)}, u32[]{:S(2)}, u32[]{:S(2)}) collective-permute-start(bf16[272,1024]{1,0:T(8,128)(2,1)} %collective-permute-done.5), channel_id=1, source_target_pairs={{2,3},{6,7},{10,11},{14,15},{18,19},{22,23},{26,27},{30,31}} | collective-permute-start | bytes 1671176 | tf_op jit(solution)/shard_map/ppermute | solution.py:67
  74.1 24.9 %collective-permute-start.8 = (bf16[272,1024]{1,0:T(8,128)(2,1)}, bf16[272,1024]{1,0:T(8,128)(2,1)}, u32[]{:S(2)}, u32[]{:S(2)}) collective-permute-start(bf16[272,1024]{1,0:T(8,128)(2,1)} %collective-permute-done.7), channel_id=1, source_target_pairs={{1,0},{5,4},{9,8},{13,12},{17,16},{21,20},{25,24},{29,28}} | collective-permute-start | bytes 1671176 | tf_op jit(solution)/shard_map/ppermute | solution.py:66
  79.6 42.1 %collective-permute-start.9 = (bf16[512,1024]{1,0:T(8,128)(2,1)}, bf16[512,1024]{1,0:T(8,128)(2,1)}, u32[]{:S(2)}, u32[]{:S(2)}) collective-permute-start(bf16[512,1024]{1,0:T(8,128)(2,1)} %bitcast.5), channel_id=1, source_target_pairs={{0,16},{16,0},{1,17},{17,1},{2,18},{18,2},{3,19},{19,3},{4,20},{20... | collective-permute-start | bytes 3145736 | tf_op jit(solution)/shard_map/ppermute | solution.py:20
  102.5 29.5 %all-to-all-start.3 = ((bf16[4,128,1024]{2,1,0:T(8,128)(2,1)}), bf16[4,128,1024]{2,1,0:T(8,128)(2,1)}, u32[]{:S(2)}, u32[]{:S(2)}) async-start(bf16[4,128,1024]{2,1,0:T(8,128)(2,1)} %broadcast_in_dim.146), calls=%async_computation.3 | async-start | bytes 2097152 | tf_op jit(solution)/shard_map/all_to_all | solution.py:34
  137.6 14.0 %collective-permute-start.11 = (bf16[256,1024]{1,0:T(8,128)(2,1)S(1)}, bf16[256,1024]{1,0:T(8,128)(2,1)S(1)}, u32[]{:S(2)}, u32[]{:S(2)}) collective-permute-start(bf16[256,1024]{1,0:T(8,128)(2,1)S(1)} %fusion.28), channel_id=1, source_target_pairs={{0,8},{4,12},{8,0},{12,4},{1,9},{5,13},{9,1},{13,5},{2,10},{6,14},... | collective-permute-start | bytes 1572872 | tf_op jit(solution)/shard_map/ppermute | solution.py:20
  141.6 25.8 %collective-permute-start.13 = (bf16[512,1024]{1,0:T(8,128)(2,1)}, bf16[512,1024]{1,0:T(8,128)(2,1)S(1)}, u32[]{:S(2)}, u32[]{:S(2)}) collective-permute-start(bf16[512,1024]{1,0:T(8,128)(2,1)} %bitcast.18), channel_id=1, source_target_pairs={{0,16},{16,0},{1,17},{17,1},{2,18},{18,2},{3,19},{19,3},{4,20},{20... | collective-permute-start | bytes 3145736 | tf_op jit(solution)/shard_map/ppermute | solution.py:20
  183.1 212.7 %reduce-scatter.2.cloned.1.call-start = ((), (), s32[]{:S(2)}) async-start(), calls=%async_computation.8 | async-start | bytes 2621440 | tf_op jit(solution)/shard_map/reduce_scatter | solution.py:357
  186.1 17.2 %collective-permute-start.17 = (bf16[256,1024]{1,0:T(8,128)(2,1)}, bf16[256,1024]{1,0:T(8,128)(2,1)}, u32[]{:S(2)}, u32[]{:S(2)}) collective-permute-start(bf16[256,1024]{1,0:T(8,128)(2,1)} %fusion.24), channel_id=1, source_target_pairs={{0,8},{4,12},{8,0},{12,4},{1,9},{5,13},{9,1},{13,5},{2,10},{6,14},... | collective-permute-start | bytes 1572872 | tf_op jit(solution)/shard_map/ppermute | solution.py:20
  208.0 13.5 %collective-permute-start.22 = (bf16[256,1024]{1,0:T(8,128)(2,1)S(1)}, bf16[256,1024]{1,0:T(8,128)(2,1)S(1)}, u32[]{:S(2)}, u32[]{:S(2)}) collective-permute-start(bf16[256,1024]{1,0:T(8,128)(2,1)S(1)} %get-tuple-element.99), channel_id=1, source_target_pairs={{0,8},{4,12},{8,0},{12,4},{1,9},{5,13},{9,1},{13,5},{2,10},{6,14},... | collective-permute-start | bytes 1572872 | tf_op jit(solution)/shard_map/ppermute | solution.py:20
  239.7 14.0 %collective-permute-start.25 = (bf16[256,1024]{1,0:T(8,128)(2,1)S(1)}, bf16[256,1024]{1,0:T(8,128)(2,1)S(1)}, u32[]{:S(2)}, u32[]{:S(2)}) collective-permute-start(bf16[256,1024]{1,0:T(8,128)(2,1)S(1)} %fusion.21), channel_id=1, source_target_pairs={{0,8},{4,12},{8,0},{12,4},{1,9},{5,13},{9,1},{13,5},{2,10},{6,14},... | collective-permute-start | bytes 1572872 | tf_op jit(solution)/shard_map/ppermute | solution.py:20
  258.7 26.3 %collective-permute-start.29 = (bf16[512,1024]{1,0:T(8,128)(2,1)S(1)}, bf16[512,1024]{1,0:T(8,128)(2,1)}, u32[]{:S(2)}, u32[]{:S(2)}) collective-permute-start(bf16[512,1024]{1,0:T(8,128)(2,1)S(1)} %constant_dynamic-slice_fusion.12), channel_id=1, source_target_pairs={{0,16},{16,0},{1,17},{17,1},{2,18},{18,2},{3,19},{19,3},{4,20},{20... | collective-permute-start | bytes 3145736 | tf_op jit(solution)/shard_map/ppermute | solution.py:20
  272.5 32.8 %collective-permute-start.39 = (bf16[512,1024]{1,0:T(8,128)(2,1)S(1)}, bf16[512,1024]{1,0:T(8,128)(2,1)S(1)}, u32[]{:S(2)}, u32[]{:S(2)}) collective-permute-start(bf16[512,1024]{1,0:T(8,128)(2,1)S(1)} %constant_dynamic-slice_fusion.1), channel_id=1, source_target_pairs={{0,16},{16,0},{1,17},{17,1},{2,18},{18,2},{3,19},{19,3},{4,20},{20... | collective-permute-start | bytes 3145736 | tf_op jit(solution)/shard_map/ppermute | solution.py:20
  313.5 23.4 %collective-permute-start.32 = (bf16[4,4,128,256]{3,2,1,0:T(8,128)(2,1)}, bf16[4,4,128,256]{3,2,1,0:T(8,128)(2,1)}, u32[]{:S(2)}, u32[]{:S(2)}) collective-permute-start(bf16[4,4,128,256]{3,2,1,0:T(8,128)(2,1)} %constant_dynamic-slice_fusion.3), channel_id=1, source_target_pairs={{0,16},{16,0},{1,17},{17,1},{2,18},{18,2},{3,19},{19,3},{4,20},{20... | collective-permute-start | bytes 3145736 | tf_op jit(solution)/shard_map/ppermute | solution.py:20
  339.5 45.1 %all-to-all-start.5 = ((bf16[16,128,256]{2,1,0:T(8,128)(2,1)}), bf16[16,128,256]{2,1,0:T(8,128)(2,1)}, u32[]{:S(2)}, u32[]{:S(2)}) async-start(bf16[16,128,256]{2,1,0:T(8,128)(2,1)} %bitcast.196), calls=%async_computation.5 | async-start | bytes 2097152 | tf_op jit(solution)/shard_map/all_to_all | solution.py:34
  347.3 13.7 %collective-permute-start.30 = (bf16[1024,512]{1,0:T(8,128)(2,1)}, bf16[1024,512]{1,0:T(8,128)(2,1)}, u32[]{:S(2)}, u32[]{:S(2)}) collective-permute-start(bf16[1024,512]{1,0:T(8,128)(2,1)} %fusion.13), channel_id=1, source_target_pairs={{0,4},{4,0},{8,12},{12,8},{1,5},{5,1},{9,13},{13,9},{2,6},{6,2},{1... | collective-permute-start | bytes 3145736 | tf_op jit(solution)/shard_map/ppermute | solution.py:20
  363.3 24.7 %collective-permute-start.31 = (bf16[1024,256]{1,0:T(8,128)(2,1)S(1)}, bf16[1024,256]{1,0:T(8,128)(2,1)S(1)}, u32[]{:S(2)}, u32[]{:S(2)}) collective-permute-start(bf16[1024,256]{1,0:T(8,128)(2,1)S(1)} %fusion.19), channel_id=1, source_target_pairs={{0,8},{4,12},{8,0},{12,4},{1,9},{5,13},{9,1},{13,5},{2,10},{6,14},... | collective-permute-start | bytes 1572872 | tf_op jit(solution)/shard_map/ppermute | solution.py:20
  398.0 17.9 %all-to-all-start.6 = ((bf16[8,256,256]{2,1,0:T(8,128)(2,1)}), bf16[8,256,256]{2,1,0:T(8,128)(2,1)S(1)}, u32[]{:S(2)}, u32[]{:S(2)}) async-start(bf16[8,256,256]{2,1,0:T(8,128)(2,1)} %bitcast.69), calls=%async_computation.7 | async-start | bytes 2097152 | tf_op jit(solution)/shard_map/all_to_all | solution.py:34
  (107 other events, 698.1 us)
Sparse Core Ops, SparseCore 0:
  308.9 44.2 reduce-scatter.1

commit v5 on v4

--- a/solution.py
+++ b/solution.py
@@ -86,6 +86,14 @@
 
 def spread(block, axis):
     return trade(jnp.broadcast_to(block[None], (lax.axis_size(axis),) + block.shape), axis)
+
+
+def butterfly(values, axis):
+    bit = 1
+    while bit < lax.axis_size(axis):
+        values = values + swap(values, axis, bit)
+        bit *= 2
+    return values
 
 
 def normalize(resid):
@@ -341,14 +349,33 @@
         low = dp_sum(got, 2).astype(bf16)
         back = swap(low, "dp", 1)
         both = [jnp.where(n == 0, low, back), jnp.where(n == 0, back, low)]
-        return jnp.concatenate(both, 1).astype(f32), raw
+        return jnp.concatenate(both, 1).astype(f32)
 
     grad_wo = dot(context, d_att_all, 0, 0).astype(bf16).reshape(cols, head_piece, rows, width_local)
     grad_wo = jnp.transpose(grad_wo, (2, 0, 1, 3))
 
     d_context = from_rel(dot(d_att_all, wo_all, 1, 1).astype(bf16), 0)
     d_joined = by_sequence(attend_back_kernel, [joined, d_context], 3 * heads_width, 10)
-    wi_other = after(wi_other, d_joined)
+    vector_grads = jnp.stack(
+        [
+            jnp.sum(d_att, 0, dtype=f32),
+            jnp.sum(d_hidden * normed_one, 0),
+            jnp.sum(d_hidden, 0),
+            jnp.sum(d_mlp_low, 0, dtype=f32),
+            jnp.sum(cot * normed_two, 0),
+            jnp.sum(cot, 0),
+        ]
+    )
+    hid_sums = sum(jnp.sum(d, 0, dtype=f32) for d in d_pre).reshape(2, cols, half)
+    hid_sums = jnp.transpose(hid_sums, (1, 0, 2)).reshape(cols, hid_piece)
+    head_sums = jnp.sum(d_joined, 0, dtype=f32).reshape(cols, 3 * head_piece)
+    col_sums = jnp.concatenate(
+        [hid_sums, head_sums[:, :head_piece], head_sums[:, 2 * head_piece :]], 1
+    )
+    col_sums = jnp.where((jnp.arange(rows) == r)[None, :, None], col_sums[:, None], 0.0)
+    small = jnp.concatenate([vector_grads, col_sums.reshape(-1, width)], 0)
+    small = butterfly(small, "col")
+    wi_other = after(wi_other, small)
     hid_grads = [
         (half_of(grad, n).astype(f32) + other.astype(f32)).astype(bf16).reshape(cols, half, width)
         for grad, other in ((grad_wb, wb_other), (grad_wi, wi_other))
@@ -362,8 +389,9 @@
         owned = lax.dynamic_slice_in_dim(tokens_all, place, width_local, 1)
         grad_wq.append(dot(d_joined, owned, 0, 0).astype(bf16).reshape(cols, heads_rows, -1))
     grad_wq = jnp.concatenate([jnp.stack(grad_wq), grad_wo], 2)
+    grad_wq, small = lax.optimization_barrier((grad_wq, small))
     d_joined_late = after(d_joined, grad_wq)
-    grad_wq, arrived = by_owner(grad_wq)
+    grad_wq = by_owner(grad_wq)
     grad_w_out = grad_wq[:, heads_rows:].reshape(heads_tile, width_local)
     grad_wq = grad_wq[:, :heads_rows].reshape(rows, 3, head_piece, width_local)
     grad_w_qkv = jnp.transpose(grad_wq, (1, 3, 0, 2)).reshape(3, width_local, heads_tile)
@@ -386,30 +414,7 @@
         1,
     )
 
-    vector_grads = jnp.stack(
-        [
-            jnp.sum(d_att, 0, dtype=f32),
-            jnp.sum(d_hidden * normed_one, 0),
-            jnp.sum(d_hidden, 0),
-            jnp.sum(d_mlp_low, 0, dtype=f32),
-            jnp.sum(cot * normed_two, 0),
-            jnp.sum(cot, 0),
-        ]
-    )
-    hid_sums = sum(jnp.sum(d, 0, dtype=f32) for d in d_pre).reshape(2, cols, half)
-    hid_sums = jnp.transpose(hid_sums, (1, 0, 2)).reshape(cols, hid_piece)
-    head_sums = jnp.sum(d_joined, 0, dtype=f32).reshape(cols, 3 * head_piece)
-    col_sums = jnp.concatenate(
-        [hid_sums, head_sums[:, :head_piece], head_sums[:, 2 * head_piece :]], 1
-    )
-    col_sums = jnp.where((jnp.arange(rows) == r)[None, :, None], col_sums[:, None], 0.0)
-    small = jnp.concatenate([vector_grads, col_sums.reshape(-1, width)], 0)
-    for axis in ("row", "dp", "col"):
-        bit = 1
-        small = after(small, arrived) if axis == "col" else small
-        while bit < lax.axis_size(axis):
-            small = small + swap(small, axis, bit)
-            bit *= 2
+    small = butterfly(butterfly(small, "row"), "dp")
     vector_grads = lax.dynamic_slice_in_dim(small[:6], r * width_local, width_local, 1)
     col_sums = small[6:].reshape(cols, rows, hid_piece + 2 * head_piece)
     col_sums = lax.dynamic_slice_in_dim(col_sums, lax.axis_index("col"), 1, 0)[0]

time: 432 us -> 433 us (level)
  other arithmetic: 52.6 us -> 57.9 us
    all_to_all x7, waiting for transfers between devices: 30.3 us -> 20.2 us  [trade(): return lax.all_to_all(values, axis, 0, 0, tiled=True)]
    ppermute x34, waiting for transfers between devices: 119 us -> 124 us  [swap(): return lax.ppermute(values, axis, [(i, i ^ bit) for i in range(size)])]
    unnamed x182 -> x174, local copies, waits for them, and re-layouts: 16.5 us -> 14.4 us
  transfers between devices with their start and end apart: 48 -> 48, of which waited for: 24 -> 26; matrix products, arithmetic and copies ran while one was open for 22% -> 25% of each run, Pallas kernels for 4% -> 4%
where the time goes in v5:
time: 433 us; the launch traced here: 427 us
  waiting for transfers between devices  178 us (41%)
  starting transfers between devices  68.4 us (16%)
  other arithmetic  57.9 us (13%)
  local copies, waits for them, and re-layouts  46.2 us (11%)
  matrix products  44.4 us (10%)
  between operations  16 us (4%)
  Pallas kernels  15.9 us (4%)
    ppermute x34, waiting for transfers between devices, swap(): return lax.ppermute(values, axis, [(i, i ^ bit) for i in range(size)])  124 us
    dot_general x23, matrix products, dot(): lax.dot_general(left, right, (((left_dim,), (right_dim,)), ((), ())), pre...  44.4 us
    ppermute x3, waiting for transfers between devices, line_step(): lax.ppermute(up, 'col', [(i, i - 1) for i in range(1, size - step + 1)])  31.8 us
    all_to_all x7, starting transfers between devices, trade(): return lax.all_to_all(values, axis, 0, 0, tiled=True)  29.7 us
    ppermute x34, starting transfers between devices, swap(): return lax.ppermute(values, axis, [(i, i ^ bit) for i in range(size)])  26.1 us
    all_to_all x7, waiting for transfers between devices, trade(): return lax.all_to_all(values, axis, 0, 0, tiled=True)  20.2 us
    pallas_call x2, Pallas kernels, by_sequence(): pl.pallas_call(kernel, grid=(tokens // SEQ_LEN,), in_specs=[pl.BlockSpec(...  15.9 us
    unnamed x174, local copies, waits for them, and re-layouts  14.4 us
  transfers between devices with their start and end apart: 48, of which 26 were waited for; matrix products, arithmetic and copies ran while one was open for 25% of the time, Pallas kernels for 4%

profile of v5, /device:TPU:0, one launch (start us, length us, event | category | flops | bytes accessed | tf_op | source)
XLA Modules:
  0.0 426.6 jit_solution(16050820808923967624)
XLA Ops:
  10.3 4.2 all-to-all-start.2
  16.8 6.6 %all-to-all-done.2 = bf16[4,256,256]{2,1,0:T(8,128)(2,1)S(1)} async-done(((bf16[4,256,256]{2,1,0:T(8,128)(2,1)}), bf16[4,256,256]{2,1,0:T(8,128)(2,1)S(1)}, u32[]{:S(2)}, u32[]{:S(2)}) %all-to-all-start.2) | async-done | bytes 524320 | tf_op jit(solution)/shard_map/all_to_all | solution.py:34
  28.5 5.6 %collective-permute-start.4 = (bf16[272,1024]{1,0:T(8,128)(2,1)S(1)}, bf16[272,1024]{1,0:T(8,128)(2,1)}, u32[]{:S(2)}, u32[]{:S(2)}) collective-permute-start(bf16[272,1024]{1,0:T(8,128)(2,1)S(1)} %fusion.38), channel_id=1, source_target_pairs={{0,1},{1,2},{2,3},{4,5},{5,6},{6,7},{8,9},{9,10},{10,11},{12,13},{... | collective-permute-start | bytes 1671176 | tf_op jit(solution)/shard_map/ppermute | solution.py:67
  37.6 5.5 %all-to-all-start.1 = ((bf16[4,128,1024]{2,1,0:T(8,128)(2,1)}), bf16[4,128,1024]{2,1,0:T(8,128)(2,1)}, u32[]{:S(2)}, u32[]{:S(2)}) async-start(bf16[4,128,1024]{2,1,0:T(8,128)(2,1)} %broadcast_in_dim.137), calls=%async_computation.1 | async-start | bytes 2097152 | tf_op jit(solution)/shard_map/all_to_all | solution.py:34
  49.0 7.4 %collective-permute-done = bf16[1024,256]{1,0:T(8,128)(2,1)S(1)} collective-permute-done((bf16[1024,256]{1,0:T(8,128)(2,1)}, bf16[1024,256]{1,0:T(8,128)(2,1)S(1)}, u32[]{:S(2)}, u32[]{:S(2)}) %collective-permute-start) | collective-permute-done | bytes 524320 | tf_op jit(solution)/shard_map/ppermute | solution.py:20
  60.3 13.9 %collective-permute-done.7 = bf16[272,1024]{1,0:T(8,128)(2,1)} collective-permute-done((bf16[272,1024]{1,0:T(8,128)(2,1)}, bf16[272,1024]{1,0:T(8,128)(2,1)}, u32[]{:S(2)}, u32[]{:S(2)}) %collective-permute-start.7) | collective-permute-done | bytes 557088 | tf_op jit(solution)/shard_map/ppermute | solution.py:66
  82.3 16.7 %collective-permute-done.8 = bf16[272,1024]{1,0:T(8,128)(2,1)} collective-permute-done((bf16[272,1024]{1,0:T(8,128)(2,1)}, bf16[272,1024]{1,0:T(8,128)(2,1)}, u32[]{:S(2)}, u32[]{:S(2)}) %collective-permute-start.8) | collective-permute-done | bytes 557088 | tf_op jit(solution)/shard_map/ppermute | solution.py:66
  102.5 4.5 %all-to-all-start.3 = ((bf16[4,128,1024]{2,1,0:T(8,128)(2,1)}), bf16[4,128,1024]{2,1,0:T(8,128)(2,1)}, u32[]{:S(2)}, u32[]{:S(2)}) async-start(bf16[4,128,1024]{2,1,0:T(8,128)(2,1)} %broadcast_in_dim.146), calls=%async_computation.3 | async-start | bytes 2097152 | tf_op jit(solution)/shard_map/all_to_all | solution.py:34
  110.5 6.5 %shard_map.245 = bf16[1024,256]{1,0:T(8,128)(2,1)S(1)} custom-call(bf16[1024,768]{1,0:T(8,128)(2,1)S(1)} %add_convert_fusion.2.qkv_ref), custom_call_target="tpu_custom_call" | custom-call | flops 536870912 | bytes 2097152 | tf_op jit(solution)/shard_map/pallas_call | solution.py:165
  124.8 7.1 %all-to-all-done.3 = bf16[4,128,1024]{2,1,0:T(8,128)(2,1)} async-done(((bf16[4,128,1024]{2,1,0:T(8,128)(2,1)}), bf16[4,128,1024]{2,1,0:T(8,128)(2,1)}, u32[]{:S(2)}, u32[]{:S(2)}) %all-to-all-start.3) | async-done | bytes 1048608 | tf_op jit(solution)/shard_map/all_to_all | solution.py:34
  143.1 8.5 %collective-permute-done.11 = bf16[256,1024]{1,0:T(8,128)(2,1)S(1)} collective-permute-done((bf16[256,1024]{1,0:T(8,128)(2,1)S(1)}, bf16[256,1024]{1,0:T(8,128)(2,1)S(1)}, u32[]{:S(2)}, u32[]{:S(2)}) %collective-permute-start.11) | collective-permute-done | bytes 524320 | tf_op jit(solution)/shard_map/ppermute | solution.py:20
  155.2 12.2 %collective-permute-done.14 = bf16[256,1024]{1,0:T(8,128)(2,1)S(1)} collective-permute-done((bf16[256,1024]{1,0:T(8,128)(2,1)S(1)}, bf16[256,1024]{1,0:T(8,128)(2,1)S(1)}, u32[]{:S(2)}, u32[]{:S(2)}) %collective-permute-start.14) | collective-permute-done | bytes 524320 | tf_op jit(solution)/shard_map/ppermute | solution.py:20
  188.0 4.4 %all-to-all-done.4 = bf16[4,256,256]{2,1,0:T(8,128)(2,1)S(1)} async-done(((bf16[4,256,256]{2,1,0:T(8,128)(2,1)}), bf16[4,256,256]{2,1,0:T(8,128)(2,1)S(1)}, u32[]{:S(2)}, u32[]{:S(2)}) %all-to-all-start.4) | async-done | bytes 524320 | tf_op jit(solution)/shard_map/all_to_all | solution.py:34
  193.8 9.4 %collective-permute-done.17 = bf16[256,1024]{1,0:T(8,128)(2,1)} collective-permute-done((bf16[256,1024]{1,0:T(8,128)(2,1)}, bf16[256,1024]{1,0:T(8,128)(2,1)}, u32[]{:S(2)}, u32[]{:S(2)}) %collective-permute-start.17) | collective-permute-done | bytes 524320 | tf_op jit(solution)/shard_map/ppermute | solution.py:20
  208.3 13.1 %collective-permute-done.22 = bf16[256,1024]{1,0:T(8,128)(2,1)S(1)} collective-permute-done((bf16[256,1024]{1,0:T(8,128)(2,1)S(1)}, bf16[256,1024]{1,0:T(8,128)(2,1)S(1)}, u32[]{:S(2)}, u32[]{:S(2)}) %collective-permute-start.22) | collective-permute-done | bytes 524320 | tf_op jit(solution)/shard_map/ppermute | solution.py:20
  227.6 4.3 %convert_reduce_fusion.1 = (f32[1024]{0:T(1024)}, bf16[512,1024]{1,0:T(8,128)(2,1)S(1)}) fusion(f32[512,1024]{1,0:T(8,128)S(1)} %copy-done.77, f32[1024]{0:T(1024)S(1)} %bitcast.250, bf16[512,1024]{1,0:T(8,128)(2,1)S(1)} %constant_dynamic-update-slice_fusion.3, bf16[512,1024]{1,0:T(8,128)(2,1)S(1)} %copy-done.39, bf16[512,1024]{1,0:T(8,128)(2,1)S(1)} %copy-done.37), kind=kOutput, calls=%fused_computation.32 | convolution fusion | flops 1084750848 | bytes 6299648 | tf_op jit(solution)/shard_map/dot_general | solution.py:24
  243.1 10.6 %collective-permute-done.25 = bf16[256,1024]{1,0:T(8,128)(2,1)S(1)} collective-permute-done((bf16[256,1024]{1,0:T(8,128)(2,1)S(1)}, bf16[256,1024]{1,0:T(8,128)(2,1)S(1)}, u32[]{:S(2)}, u32[]{:S(2)}) %collective-permute-start.25) | collective-permute-done | bytes 524320 | tf_op jit(solution)/shard_map/ppermute | solution.py:20
  263.0 8.2 %collective-permute-done.26 = bf16[256,1024]{1,0:T(8,128)(2,1)} collective-permute-done((bf16[256,1024]{1,0:T(8,128)(2,1)S(1)}, bf16[256,1024]{1,0:T(8,128)(2,1)}, u32[]{:S(2)}, u32[]{:S(2)}) %collective-permute-start.26) | collective-permute-done | bytes 524320 | tf_op jit(solution)/shard_map/ppermute | solution.py:20
  278.3 6.7 %collective-permute-done.29 = bf16[512,1024]{1,0:T(8,128)(2,1)} collective-permute-done((bf16[512,1024]{1,0:T(8,128)(2,1)S(1)}, bf16[512,1024]{1,0:T(8,128)(2,1)}, u32[]{:S(2)}, u32[]{:S(2)}) %collective-permute-start.29) | collective-permute-done | bytes 1048608 | tf_op jit(solution)/shard_map/ppermute | solution.py:20
  286.9 9.4 %shard_map.246 = bf16[1024,768]{1,0:T(8,128)(2,1)S(1)} custom-call(bf16[1024,768]{1,0:T(8,128)(2,1)S(1)} %add_convert_fusion.2.qkv_ref, bf16[1024,256]{1,0:T(8,128)(2,1)S(1)} %pad_maximum_fusion.18.d_context_ref), custom_call_target="tpu_custom_call" | custom-call | flops 1342177280 | bytes 3670016 | tf_op jit(solution)/shard_map/pallas_call | solution.py:165
  321.5 19.1 %collective-permute-done.34 = bf16[4,4,128,256]{3,2,1,0:T(8,128)(2,1)} collective-permute-done((bf16[4,4,128,256]{3,2,1,0:T(8,128)(2,1)S(1)}, bf16[4,4,128,256]{3,2,1,0:T(8,128)(2,1)}, u32[]{:S(2)}, u32[]{:S(2)}) %collective-permute-start.34) | collective-permute-done | bytes 1048608 | tf_op jit(solution)/shard_map/ppermute | solution.py:20
  343.4 4.8 %all-to-all-start.5 = ((bf16[16,128,256]{2,1,0:T(8,128)(2,1)}), bf16[16,128,256]{2,1,0:T(8,128)(2,1)}, u32[]{:S(2)}, u32[]{:S(2)}) async-start(bf16[16,128,256]{2,1,0:T(8,128)(2,1)} %bitcast.54), calls=%async_computation.5 | async-start | bytes 2097152 | tf_op jit(solution)/shard_map/all_to_all | solution.py:34
  362.2 6.7 %collective-permute-done.19 = bf16[1,256,256]{2,1,0:T(8,128)(2,1)} collective-permute-done((bf16[1,256,256]{2,1,0:T(8,128)(2,1)}, bf16[1,256,256]{2,1,0:T(8,128)(2,1)}, u32[]{:S(2)}, u32[]{:S(2)}) %collective-permute-start.19) | collective-permute-done | bytes 131104 | tf_op jit(solution)/shard_map/ppermute | solution.py:20
  401.6 13.1 %collective-permute-done.35 = bf16[4,128,256]{2,1,0:T(8,128)(2,1)S(1)} collective-permute-done((bf16[4,128,256]{2,1,0:T(8,128)(2,1)S(1)}, bf16[4,128,256]{2,1,0:T(8,128)(2,1)S(1)}, u32[]{:S(2)}, u32[]{:S(2)}) %collective-permute-start.35) | collective-permute-done | bytes 262176 | tf_op jit(solution)/shard_map/ppermute | solution.py:20
  (428 shorter events, 201.9 us)
Async XLA Ops:
  27.2 17.5 %collective-permute-start.3 = (bf16[272,1024]{1,0:T(8,128)(2,1)S(1)}, bf16[272,1024]{1,0:T(8,128)(2,1)}, u32[]{:S(2)}, u32[]{:S(2)}) collective-permute-start(bf16[272,1024]{1,0:T(8,128)(2,1)S(1)} %fusion.38), channel_id=1, source_target_pairs={{1,0},{2,1},{3,2},{5,4},{6,5},{7,6},{9,8},{10,9},{11,10},{13,12},{... | collective-permute-start | bytes 1671176 | tf_op jit(solution)/shard_map/ppermute | solution.py:66
  28.5 17.7 %collective-permute-start.4 = (bf16[272,1024]{1,0:T(8,128)(2,1)S(1)}, bf16[272,1024]{1,0:T(8,128)(2,1)}, u32[]{:S(2)}, u32[]{:S(2)}) collective-permute-start(bf16[272,1024]{1,0:T(8,128)(2,1)S(1)} %fusion.38), channel_id=1, source_target_pairs={{0,1},{1,2},{2,3},{4,5},{5,6},{6,7},{8,9},{9,10},{10,11},{12,13},{... | collective-permute-start | bytes 1671176 | tf_op jit(solution)/shard_map/ppermute | solution.py:67
  37.6 42.0 %all-to-all-start.1 = ((bf16[4,128,1024]{2,1,0:T(8,128)(2,1)}), bf16[4,128,1024]{2,1,0:T(8,128)(2,1)}, u32[]{:S(2)}, u32[]{:S(2)}) async-start(bf16[4,128,1024]{2,1,0:T(8,128)(2,1)} %broadcast_in_dim.137), calls=%async_computation.1 | async-start | bytes 2097152 | tf_op jit(solution)/shard_map/all_to_all | solution.py:34
  47.7 26.5 %collective-permute-start.7 = (bf16[272,1024]{1,0:T(8,128)(2,1)}, bf16[272,1024]{1,0:T(8,128)(2,1)}, u32[]{:S(2)}, u32[]{:S(2)}) collective-permute-start(bf16[272,1024]{1,0:T(8,128)(2,1)} %collective-permute-done.3), channel_id=1, source_target_pairs={{1,0},{2,1},{5,4},{6,5},{9,8},{10,9},{13,12},{14,13},{17,16},{18,1... | collective-permute-start | bytes 1671176 | tf_op jit(solution)/shard_map/ppermute | solution.py:66
  48.9 26.5 %collective-permute-start.1 = (bf16[1024,256]{1,0:T(8,128)(2,1)}, bf16[1024,256]{1,0:T(8,128)(2,1)}, u32[]{:S(2)}, u32[]{:S(2)}) collective-permute-start(bf16[1024,256]{1,0:T(8,128)(2,1)} %param.14), channel_id=1, source_target_pairs={{0,4},{4,0},{8,12},{12,8},{1,5},{5,1},{9,13},{13,9},{2,6},{6,2},{1... | collective-permute-start | bytes 1572872 | tf_op jit(solution)/shard_map/ppermute | solution.py:20
  56.5 19.0 %collective-permute-start.2 = (bf16[1024,256]{1,0:T(8,128)(2,1)S(1)}, bf16[1024,256]{1,0:T(8,128)(2,1)}, u32[]{:S(2)}, u32[]{:S(2)}) collective-permute-start(bf16[1024,256]{1,0:T(8,128)(2,1)S(1)} %collective-permute-done), channel_id=1, source_target_pairs={{0,4},{4,0},{8,12},{12,8},{1,5},{5,1},{9,13},{13,9},{2,6},{6,2},{1... | collective-permute-start | bytes 1572872 | tf_op jit(solution)/shard_map/ppermute | solution.py:20
  57.0 24.1 %collective-permute-start.6 = (bf16[272,1024]{1,0:T(8,128)(2,1)}, bf16[272,1024]{1,0:T(8,128)(2,1)}, u32[]{:S(2)}, u32[]{:S(2)}) collective-permute-start(bf16[272,1024]{1,0:T(8,128)(2,1)} %collective-permute-done.5), channel_id=1, source_target_pairs={{2,3},{6,7},{10,11},{14,15},{18,19},{22,23},{26,27},{30,31}} | collective-permute-start | bytes 1671176 | tf_op jit(solution)/shard_map/ppermute | solution.py:67
  74.1 24.9 %collective-permute-start.8 = (bf16[272,1024]{1,0:T(8,128)(2,1)}, bf16[272,1024]{1,0:T(8,128)(2,1)}, u32[]{:S(2)}, u32[]{:S(2)}) collective-permute-start(bf16[272,1024]{1,0:T(8,128)(2,1)} %collective-permute-done.7), channel_id=1, source_target_pairs={{1,0},{5,4},{9,8},{13,12},{17,16},{21,20},{25,24},{29,28}} | collective-permute-start | bytes 1671176 | tf_op jit(solution)/shard_map/ppermute | solution.py:66
  79.6 42.1 %collective-permute-start.9 = (bf16[512,1024]{1,0:T(8,128)(2,1)}, bf16[512,1024]{1,0:T(8,128)(2,1)}, u32[]{:S(2)}, u32[]{:S(2)}) collective-permute-start(bf16[512,1024]{1,0:T(8,128)(2,1)} %bitcast.5), channel_id=1, source_target_pairs={{0,16},{16,0},{1,17},{17,1},{2,18},{18,2},{3,19},{19,3},{4,20},{20... | collective-permute-start | bytes 3145736 | tf_op jit(solution)/shard_map/ppermute | solution.py:20
  102.5 29.4 %all-to-all-start.3 = ((bf16[4,128,1024]{2,1,0:T(8,128)(2,1)}), bf16[4,128,1024]{2,1,0:T(8,128)(2,1)}, u32[]{:S(2)}, u32[]{:S(2)}) async-start(bf16[4,128,1024]{2,1,0:T(8,128)(2,1)} %broadcast_in_dim.146), calls=%async_computation.3 | async-start | bytes 2097152 | tf_op jit(solution)/shard_map/all_to_all | solution.py:34
  137.6 14.0 %collective-permute-start.11 = (bf16[256,1024]{1,0:T(8,128)(2,1)S(1)}, bf16[256,1024]{1,0:T(8,128)(2,1)S(1)}, u32[]{:S(2)}, u32[]{:S(2)}) collective-permute-start(bf16[256,1024]{1,0:T(8,128)(2,1)S(1)} %fusion.28), channel_id=1, source_target_pairs={{0,8},{4,12},{8,0},{12,4},{1,9},{5,13},{9,1},{13,5},{2,10},{6,14},... | collective-permute-start | bytes 1572872 | tf_op jit(solution)/shard_map/ppermute | solution.py:20
  141.6 25.8 %collective-permute-start.13 = (bf16[512,1024]{1,0:T(8,128)(2,1)}, bf16[512,1024]{1,0:T(8,128)(2,1)S(1)}, u32[]{:S(2)}, u32[]{:S(2)}) collective-permute-start(bf16[512,1024]{1,0:T(8,128)(2,1)} %bitcast.18), channel_id=1, source_target_pairs={{0,16},{16,0},{1,17},{17,1},{2,18},{18,2},{3,19},{19,3},{4,20},{20... | collective-permute-start | bytes 3145736 | tf_op jit(solution)/shard_map/ppermute | solution.py:20
  183.1 205.8 %reduce-scatter.2.cloned.1.call-start = ((), (), s32[]{:S(2)}) async-start(), calls=%async_computation.8 | async-start | bytes 2621440 | tf_op jit(solution)/shard_map/reduce_scatter | solution.py:384
  186.0 17.2 %collective-permute-start.17 = (bf16[256,1024]{1,0:T(8,128)(2,1)}, bf16[256,1024]{1,0:T(8,128)(2,1)}, u32[]{:S(2)}, u32[]{:S(2)}) collective-permute-start(bf16[256,1024]{1,0:T(8,128)(2,1)} %fusion.24), channel_id=1, source_target_pairs={{0,8},{4,12},{8,0},{12,4},{1,9},{5,13},{9,1},{13,5},{2,10},{6,14},... | collective-permute-start | bytes 1572872 | tf_op jit(solution)/shard_map/ppermute | solution.py:20
  239.6 14.0 %collective-permute-start.25 = (bf16[256,1024]{1,0:T(8,128)(2,1)S(1)}, bf16[256,1024]{1,0:T(8,128)(2,1)S(1)}, u32[]{:S(2)}, u32[]{:S(2)}) collective-permute-start(bf16[256,1024]{1,0:T(8,128)(2,1)S(1)} %fusion.21), channel_id=1, source_target_pairs={{0,8},{4,12},{8,0},{12,4},{1,9},{5,13},{9,1},{13,5},{2,10},{6,14},... | collective-permute-start | bytes 1572872 | tf_op jit(solution)/shard_map/ppermute | solution.py:20
  258.7 26.3 %collective-permute-start.29 = (bf16[512,1024]{1,0:T(8,128)(2,1)S(1)}, bf16[512,1024]{1,0:T(8,128)(2,1)}, u32[]{:S(2)}, u32[]{:S(2)}) collective-permute-start(bf16[512,1024]{1,0:T(8,128)(2,1)S(1)} %constant_dynamic-slice_fusion.12), channel_id=1, source_target_pairs={{0,16},{16,0},{1,17},{17,1},{2,18},{18,2},{3,19},{19,3},{4,20},{20... | collective-permute-start | bytes 3145736 | tf_op jit(solution)/shard_map/ppermute | solution.py:20
  263.0 13.7 %collective-permute-start.27 = (bf16[256,1024]{1,0:T(8,128)(2,1)S(1)}, bf16[256,1024]{1,0:T(8,128)(2,1)}, u32[]{:S(2)}, u32[]{:S(2)}) collective-permute-start(bf16[256,1024]{1,0:T(8,128)(2,1)S(1)} %get-tuple-element.104), channel_id=1, source_target_pairs={{0,4},{4,0},{8,12},{12,8},{1,5},{5,1},{9,13},{13,9},{2,6},{6,2},{1... | collective-permute-start | bytes 1572872 | tf_op jit(solution)/shard_map/ppermute | solution.py:20
  274.6 36.6 %collective-permute-start.39 = (bf16[512,1024]{1,0:T(8,128)(2,1)}, bf16[512,1024]{1,0:T(8,128)(2,1)}, u32[]{:S(2)}, u32[]{:S(2)}) collective-permute-start(bf16[512,1024]{1,0:T(8,128)(2,1)} %constant_dynamic-slice_fusion.1), channel_id=1, source_target_pairs={{0,16},{16,0},{1,17},{17,1},{2,18},{18,2},{3,19},{19,3},{4,20},{20... | collective-permute-start | bytes 3145736 | tf_op jit(solution)/shard_map/ppermute | solution.py:20
  319.8 20.7 %collective-permute-start.34 = (bf16[4,4,128,256]{3,2,1,0:T(8,128)(2,1)S(1)}, bf16[4,4,128,256]{3,2,1,0:T(8,128)(2,1)}, u32[]{:S(2)}, u32[]{:S(2)}) collective-permute-start(bf16[4,4,128,256]{3,2,1,0:T(8,128)(2,1)S(1)} %constant_dynamic-slice_fusion.3), channel_id=1, source_target_pairs={{0,16},{16,0},{1,17},{17,1},{2,18},{18,2},{3,19},{19,3},{4,20},{20... | collective-permute-start | bytes 3145736 | tf_op jit(solution)/shard_map/ppermute | solution.py:20
  343.4 46.5 %all-to-all-start.5 = ((bf16[16,128,256]{2,1,0:T(8,128)(2,1)}), bf16[16,128,256]{2,1,0:T(8,128)(2,1)}, u32[]{:S(2)}, u32[]{:S(2)}) async-start(bf16[16,128,256]{2,1,0:T(8,128)(2,1)} %bitcast.54), calls=%async_computation.5 | async-start | bytes 2097152 | tf_op jit(solution)/shard_map/all_to_all | solution.py:34
  352.5 30.8 %collective-permute-start.32 = (bf16[1024,512]{1,0:T(8,128)(2,1)}, bf16[1024,512]{1,0:T(8,128)(2,1)}, u32[]{:S(2)}, u32[]{:S(2)}) collective-permute-start(bf16[1024,512]{1,0:T(8,128)(2,1)} %fusion.13), channel_id=1, source_target_pairs={{0,4},{4,0},{8,12},{12,8},{1,5},{5,1},{9,13},{13,9},{2,6},{6,2},{1... | collective-permute-start | bytes 3145736 | tf_op jit(solution)/shard_map/ppermute | solution.py:20
  385.5 13.7 %collective-permute-start.33 = (bf16[1024,256]{1,0:T(8,128)(2,1)}, bf16[1024,256]{1,0:T(8,128)(2,1)}, u32[]{:S(2)}, u32[]{:S(2)}) collective-permute-start(bf16[1024,256]{1,0:T(8,128)(2,1)} %fusion.19), channel_id=1, source_target_pairs={{0,8},{4,12},{8,0},{12,4},{1,9},{5,13},{9,1},{13,5},{2,10},{6,14},... | collective-permute-start | bytes 1572872 | tf_op jit(solution)/shard_map/ppermute | solution.py:20
  391.0 25.8 %all-to-all-start.6 = ((bf16[8,256,256]{2,1,0:T(8,128)(2,1)}), bf16[8,256,256]{2,1,0:T(8,128)(2,1)S(1)}, u32[]{:S(2)}, u32[]{:S(2)}) async-start(bf16[8,256,256]{2,1,0:T(8,128)(2,1)} %bitcast.196), calls=%async_computation.7 | async-start | bytes 2097152 | tf_op jit(solution)/shard_map/all_to_all | solution.py:34
  396.1 18.6 %collective-permute-start.35 = (bf16[4,128,256]{2,1,0:T(8,128)(2,1)S(1)}, bf16[4,128,256]{2,1,0:T(8,128)(2,1)S(1)}, u32[]{:S(2)}, u32[]{:S(2)}) collective-permute-start(bf16[4,128,256]{2,1,0:T(8,128)(2,1)S(1)} %bitcast_reduce_fusion), channel_id=1, source_target_pairs={{0,16},{16,0},{1,17},{17,1},{2,18},{18,2},{3,19},{19,3},{4,20},{20... | collective-permute-start | bytes 786440 | tf_op jit(solution)/shard_map/ppermute | solution.py:20
  (103 other events, 709.9 us)
Sparse Core Ops, SparseCore 0:
  314.9 47.8 reduce-scatter.1
